TPU v7x, 32 devices: a whole 2x2x4 slice. The times are simulated.
32 devices in a mesh: groups: 2 (over y), frames: 4 (over z), rows: 2 (over x), heads: 2 (over core).
Axes of the slice: x: 2, y: 2, z: 4, core: 2. Of those that a mesh axis runs over, the one named last changes fastest.
Arguments:
- clip_latent: bfloat16 [8, 12, 48, 640], P(('groups', 'frames'), 'rows', None, 'heads'), parts along dimension 0, may hold values from -40 to 40, as said below
- norm_gain: float32 [640], replicated, may hold values from 0.1 to 1.9
- w_time: bfloat16 [3, 640, 640], replicated, may hold values from -0.125 to 0.125
- w_query: bfloat16 [640, 640], P(None, 'heads'), may hold values from -0.7109375 to 0.7109375
- w_key: bfloat16 [640, 640], P(None, 'heads'), may hold values from -0.25 to 0.25
- w_value: bfloat16 [640, 640], P(None, 'heads'), may hold values from -0.25 to 0.25
- w_out: bfloat16 [640, 640], P('heads'), may hold values from -0.25 to 0.25
- reference_tokens: bfloat16 [288, 640], P(('groups', 'frames', 'rows'), 'heads'), parts along dimension 0, may hold values from -160 to 160, as said below
Outputs:
- block_out: bfloat16 [8, 12, 48, 640], P(('groups', 'frames'), 'rows', None, 'heads'), parts along dimension 0
There are 2 independent parts, one for each index of `groups`. A program takes and returns all parts, laid end to end along the dimension named above; an argument that names none is the same for every part. Nothing has to cross between parts.
Inputs may be any that keep to these rules, and one draw needn't show every extreme that they name: `clip_latent`: Real-valued latent features; each channel and each position has its own scale. `reference_tokens`: Real-valued reference features.
All inputs are finite; a program needn't handle non-finite values.
Results may differ from a plain program's by a relative error of at most 0.022.
Values may be sent and summed in bfloat16 or wider, within the bound.
No kernel may reach another device: no remote copies, remote signals or barrier semaphores. Data moves between devices by JAX's collectives and lax.ppermute only.
A program may use at most 64 MiB of HBM per device.

v0:
```python
import jax
import jax.numpy as jnp
from jax import lax
from jax.sharding import PartitionSpec as P

C = 640
HEADS = 8


def with_halo(block, sides, width):
    for axis, dim in sides:
        count = lax.axis_size(axis)
        forward = [(i, i + 1) for i in range(count - 1)]
        backward = [(target, source) for source, target in forward]
        low = lax.ppermute(
            lax.slice_in_dim(block, block.shape[dim] - width, None, axis=dim), axis, forward
        )
        high = lax.ppermute(lax.slice_in_dim(block, 0, width, axis=dim), axis, backward)
        block = jnp.concatenate([low, block, high], axis=dim)
    return block


def temporal_terms(padded, weights, frames_here):
    summed = jnp.dot(padded[0:frames_here], weights[0], preferred_element_type=jnp.float32)
    summed = summed + jnp.dot(
        padded[1 : 1 + frames_here], weights[1], preferred_element_type=jnp.float32
    )
    summed = summed + jnp.dot(
        padded[2 : 2 + frames_here], weights[2], preferred_element_type=jnp.float32
    )
    return summed


def attend_head(operands):
    query_head, key_head, value_head = operands
    scores = jnp.dot(query_head, key_head.T, preferred_element_type=jnp.float32)
    top = jnp.max(scores, axis=1, keepdims=True)
    expo = jnp.exp(scores - top)
    total = jnp.sum(expo, axis=1, keepdims=True)
    probs = expo.astype(jnp.bfloat16)
    return (jnp.dot(probs, value_head, preferred_element_type=jnp.float32) / total).astype(
        jnp.bfloat16
    )


def body(clip_latent, norm_gain, w_time, w_query, w_key, w_value, w_out, reference_tokens):
    frames_here, rows_here, cols_here, half_width = clip_latent.shape
    head_size = C // HEADS
    local_heads = half_width // head_size
    position = lax.axis_index("heads")
    padded_half = with_halo(clip_latent, (("frames", 0),), 1)
    padded = lax.all_gather(padded_half, "heads", axis=3, tiled=True)
    summed = temporal_terms(padded, w_time, frames_here)
    temporal_full = (padded[1 : 1 + frames_here].astype(jnp.float32) + summed).astype(jnp.bfloat16)
    temporal_half = lax.dynamic_slice_in_dim(temporal_full, position * half_width, half_width, 3)
    feats = temporal_full.astype(jnp.float32)
    centre = jnp.mean(feats, axis=-1, keepdims=True)
    spread = jnp.mean((feats - centre) ** 2, axis=-1, keepdims=True)
    normed = ((feats - centre) * lax.rsqrt(spread + 1e-05) * norm_gain).astype(jnp.bfloat16)
    scale = 1.0 / jnp.sqrt(jnp.float32(head_size))
    query = (jnp.dot(normed, w_query, preferred_element_type=jnp.float32) * scale).astype(
        jnp.bfloat16
    )
    ref_full = lax.all_gather(reference_tokens, "heads", axis=1, tiled=True)
    w_both = jnp.concatenate([w_key, w_value], axis=1)
    key_value = lax.all_gather(
        jnp.dot(ref_full, w_both, preferred_element_type=jnp.float32).astype(jnp.bfloat16),
        ("frames", "rows"),
        axis=0,
        tiled=True,
    )
    key_heads = key_value[:, :half_width].reshape(-1, local_heads, head_size).transpose(1, 0, 2)
    value_heads = key_value[:, half_width:].reshape(-1, local_heads, head_size).transpose(1, 0, 2)
    query_heads = query.reshape(-1, local_heads, head_size).transpose(1, 0, 2)
    attended = lax.map(attend_head, (query_heads, key_heads, value_heads))
    attended = attended.transpose(1, 0, 2).reshape(frames_here, rows_here, cols_here, half_width)
    partial_out = jnp.dot(attended, w_out, preferred_element_type=jnp.float32)
    summed_out = lax.psum_scatter(partial_out, "heads", scatter_dimension=3, tiled=True)
    return (temporal_half.astype(jnp.float32) + summed_out).astype(jnp.bfloat16)


def solution(mesh):
    return jax.shard_map(
        body,
        mesh=mesh,
        in_specs=(
            P(("groups", "frames"), "rows", None, "heads"),
            P(),
            P(),
            P(None, "heads"),
            P(None, "heads"),
            P(None, "heads"),
            P("heads", None),
            P(("groups", "frames", "rows"), "heads"),
        ),
        out_specs=P(("groups", "frames"), "rows", None, "heads"),
        check_vma=False,
    )
```

profile of v0, /device:TPU:0, one launch (start us, length us, event | category | flops | bytes accessed | tf_op | source)
XLA Modules:
  0.0 101.6 jit_solution(3994693648743988713)
XLA Ops:
  6.5 5.1 %collective-permute-start = (bf16[1,6,48,320]{3,2,1,0:T(8,128)(2,1)}, bf16[1,6,48,320]{3,2,1,0:T(8,128)(2,1)S(1)}, u32[]{:S(2)}, u32[]{:S(2)}) collective-permute-start(bf16[1,6,48,320]{3,2,1,0:T(8,128)(2,1)} %param.10), channel_id=1, source_target_pairs={{0,4},{4,8},{8,12},{1,5},{5,9},{9,13},{2,6},{6,10},{10,14},{3,7},{... | collective-permute-start | bytes 552968 | tf_op jit(solution)/shard_map/ppermute | solution.py:15
  11.6 1.3 %collective-permute-start.1 = (bf16[1,6,48,320]{3,2,1,0:T(8,128)(2,1)}, bf16[1,6,48,320]{3,2,1,0:T(8,128)(2,1)S(1)}, u32[]{:S(2)}, u32[]{:S(2)}) collective-permute-start(bf16[1,6,48,320]{3,2,1,0:T(8,128)(2,1)} %param.10), channel_id=1, source_target_pairs={{4,0},{8,4},{12,8},{5,1},{9,5},{13,9},{6,2},{10,6},{14,10},{7,3},{... | collective-permute-start | bytes 552968 | tf_op jit(solution)/shard_map/ppermute | solution.py:18
  12.9 3.7 %collective-permute-done = bf16[1,6,48,320]{3,2,1,0:T(8,128)(2,1)S(1)} collective-permute-done((bf16[1,6,48,320]{3,2,1,0:T(8,128)(2,1)}, bf16[1,6,48,320]{3,2,1,0:T(8,128)(2,1)S(1)}, u32[]{:S(2)}, u32[]{:S(2)}) %collective-permute-start) | collective-permute-done | bytes 184352 | tf_op jit(solution)/shard_map/ppermute | solution.py:15
  16.6 4.0 %collective-permute-done.1 = bf16[1,6,48,320]{3,2,1,0:T(8,128)(2,1)S(1)} collective-permute-done((bf16[1,6,48,320]{3,2,1,0:T(8,128)(2,1)}, bf16[1,6,48,320]{3,2,1,0:T(8,128)(2,1)S(1)}, u32[]{:S(2)}, u32[]{:S(2)}) %collective-permute-start.1) | collective-permute-done | bytes 184352 | tf_op jit(solution)/shard_map/ppermute | solution.py:18
  20.6 1.1 %pad_maximum_fusion = bf16[3,6,48,320]{3,2,1,0:T(8,128)(2,1)S(1)} fusion(bf16[1,6,48,320]{3,2,1,0:T(8,128)(2,1)S(1)} %collective-permute-done.1, bf16[1,6,48,320]{3,2,1,0:T(8,128)(2,1)} %param.10, bf16[1,6,48,320]{3,2,1,0:T(8,128)(2,1)S(1)} %collective-permute-done), kind=kLoop, calls=%fused_computation.44 | loop fusion | flops 552960 | bytes 1105920 | tf_op jit(solution)/shard_map/concatenate | solution.py:19
  21.7 2.6 %copy.27 = bf16[3,6,48,320]{2,1,0,3:T(8,128)(2,1)} copy(bf16[3,6,48,320]{3,2,1,0:T(8,128)(2,1)S(1)} %pad_maximum_fusion) | data formatting | bytes 1105920 | tf_op jit(solution)/shard_map/concatenate | solution.py:19
  24.5 1.8 %all-gather = bf16[2,320,18]{1,2,0:T(8,128)(2,1)S(1)} all-gather(bf16[1,320,18]{1,2,0:T(8,128)(2,1)S(1)} %bitcast.90), channel_id=1, replica_groups=mesh['groups'=2,'frames'=4,'rows'=2,'heads'=2] {'heads'}, dimensions={0}, use_global_device_ids=true | all-gather | bytes 34560 | tf_op jit(solution)/shard_map/all_gather | solution.py:64
  26.8 30.8 %all-gather.1 = bf16[8,18,640]{2,1,0:T(8,128)(2,1)S(1)} all-gather(bf16[1,18,640]{2,1,0:T(8,128)(2,1)S(1)} %fusion.20), channel_id=1, replica_groups=mesh['groups'=2,'frames'=4,'rows'=2,'heads'=2] {'frames','rows'}, dimensions={0}, use_global_device_ids=true | all-gather | bytes 207360 | tf_op jit(solution)/shard_map/all_gather | solution.py:66
  58.8 3.8 %fusion.48 = (bf16[1,6,48,640]{2,1,0,3:T(8,128)(2,1)S(1)}, bf16[1,6,48,640]{2,1,0,3:T(8,128)(2,1)S(1)}, bf16[1,6,48,640]{2,1,0,3:T(8,128)(2,1)}) fusion(bf16[3,6,48,640]{2,1,0,3:T(8,128)(2,1)} %all-gather.4.cloned.1.call-done), kind=kLoop, calls=%fused_computation.59 | loop fusion | bytes 2211840 | tf_op jit(solution)/shard_map/slice | solution.py:29
  62.7 1.9 %copy.38 = bf16[1,6,48,640]{3,2,1,0:T(8,128)(2,1)S(1)} copy(bf16[1,6,48,640]{2,1,0,3:T(8,128)(2,1)} %get-tuple-element.62) | data formatting | bytes 737280
  64.6 1.7 %copy.39 = bf16[1,6,48,640]{3,2,1,0:T(8,128)(2,1)} copy(bf16[1,6,48,640]{2,1,0,3:T(8,128)(2,1)S(1)} %get-tuple-element.61) | data formatting | bytes 737280
  66.3 1.1 %copy.40 = bf16[1,6,48,640]{3,2,1,0:T(8,128)(2,1)S(1)} copy(bf16[1,6,48,640]{2,1,0,3:T(8,128)(2,1)S(1)} %get-tuple-element.60) | data formatting | bytes 737280
  67.4 1.8 %fusion.28 = f32[6,48,640]{2,1,0:T(8,128)S(1)} fusion(bf16[3,640,640]{2,1,0:T(8,128)(2,1)} %param.12, bf16[1,6,48,640]{3,2,1,0:T(8,128)(2,1)} %copy.39), kind=kOutput, calls=%fused_computation.36 | convolution fusion | flops 235929600 | bytes 1925120 | tf_op jit(solution)/shard_map/dot_general | solution.py:24
  69.2 1.6 %convolution_add_fusion.1 = f32[6,48,640]{2,1,0:T(8,128)S(1)} fusion(f32[6,48,640]{2,1,0:T(8,128)S(1)} %fusion.28, bf16[3,640,640]{2,1,0:T(8,128)(2,1)} %param.12, bf16[1,6,48,640]{3,2,1,0:T(8,128)(2,1)S(1)} %copy.38), kind=kOutput, calls=%fused_computation.20 | convolution fusion | flops 236113920 | bytes 2662400 | tf_op jit(solution)/shard_map/dot_general | solution.py:25
  70.8 1.8 %convert_reduce_fusion = (f32[6,48]{1,0:T(8,128)S(1)}, bf16[1,6,48,640]{3,2,1,0:T(8,128)(2,1)S(1)}) fusion(f32[6,48,640]{2,1,0:T(8,128)S(1)} %convolution_add_fusion.1, bf16[3,640,640]{2,1,0:T(8,128)(2,1)} %param.12, bf16[1,6,48,640]{3,2,1,0:T(8,128)(2,1)S(1)} %copy.40, bf16[1,6,48,640]{3,2,1,0:T(8,128)(2,1)S(1)} %copy.38), kind=kOutput, calls=%fused_computation.28 | convolution fusion | flops 237035232 | bytes 2663552 | tf_op jit(solution)/shard_map/dot_general | solution.py:28
  73.6 5.1 %while.10 = (s32[]{:T(128)}, bf16[4,288,80]{1,2,0:T(8,128)(2,1)S(1)}, bf16[4,288,80]{2,1,0:T(8,128)(2,1)S(1)}, bf16[4,144,80]{2,1,0:T(8,128)(2,1)S(1)}, bf16[4,144,80]{2,1,0:T(8,128)(2,1)}, /*index=5*/s32[]{:T(128)}) while((s32[]{:T(128)}, bf16[4,288,80]{1,2,0:T(8,128)(2,1)S(1)}, bf16[4,288,80]{2,1,0:T(8,128)(2,1)S(1)}, ...), condition=%wide.region_5.6_spmd, body=%wide.region_2.5_spmd.sunk | while | flops 13523906 | bytes 771525 | solution.py:75
  75.2 1.0 fusion.61
  76.5 1.0 fusion.61
  77.8 1.0 fusion.61
  79.2 1.2 %convolution_bitcast_fusion = f32[1,6,48,640]{3,2,1,0:T(8,128)} fusion(bf16[6,48,320]{2,1,0:T(8,128)(2,1)S(1)} %reshape.70, bf16[320,640]{1,0:T(8,128)(2,1)S(1)} %copy-done), kind=kOutput, calls=%fused_computation.17 | convolution fusion | flops 117964800 | bytes 1331200 | tf_op jit(solution)/shard_map/dot_general | solution.py:77
  80.5 2.2 %copy.36 = f32[1,6,48,640]{2,1,0,3:T(8,128)S(1)} copy(f32[1,6,48,640]{3,2,1,0:T(8,128)} %convolution_bitcast_fusion) | data formatting | bytes 1474560
  82.7 1.5 %reshape.80 = f32[640,288]{1,0:T(8,128)} reshape(f32[640,1,6,48]{3,2,1,0:T(8,128)S(1)} %bitcast.84) | data formatting | bytes 1474560
  84.2 7.8 %reduce-scatter.4.cloned.1.call-done = f32[320,288]{1,0:T(8,128)} async-done(((f32[640,288]{1,0:T(8,128)}), f32[320,288]{1,0:T(8,128)}) %reduce-scatter.4.cloned.1.call-update) | async-done | bytes 368656
  92.0 1.4 %reshape.81 = f32[320,1,6,48]{3,2,1,0:T(8,128)S(1)} reshape(f32[320,288]{1,0:T(8,128)} %reduce-scatter.4.cloned.1.call-done) | data formatting | bytes 737280
  (48 shorter events, 6.4 us)
Async XLA Ops:
  6.5 72.7 %copy-start = (bf16[320,640]{1,0:T(8,128)(2,1)S(1)}, bf16[320,640]{1,0:T(8,128)(2,1)}, u32[]{:S(2)}) copy-start(bf16[320,640]{1,0:T(8,128)(2,1)} %param.16) | copy-start | bytes 1228804
  6.5 52.3 %all-gather.4.cloned.1.call-start = ((), (), s32[]{:S(2)}) async-start(), calls=%async_computation.1 | async-start | bytes 5898240 | tf_op jit(solution)/shard_map/all_gather | solution.py:52
  6.5 10.0 %collective-permute-start = (bf16[1,6,48,320]{3,2,1,0:T(8,128)(2,1)}, bf16[1,6,48,320]{3,2,1,0:T(8,128)(2,1)S(1)}, u32[]{:S(2)}, u32[]{:S(2)}) collective-permute-start(bf16[1,6,48,320]{3,2,1,0:T(8,128)(2,1)} %param.10), channel_id=1, source_target_pairs={{0,4},{4,8},{8,12},{1,5},{5,9},{9,13},{2,6},{6,10},{10,14},{3,7},{... | collective-permute-start | bytes 552968 | tf_op jit(solution)/shard_map/ppermute | solution.py:15
  11.6 9.0 %collective-permute-start.1 = (bf16[1,6,48,320]{3,2,1,0:T(8,128)(2,1)}, bf16[1,6,48,320]{3,2,1,0:T(8,128)(2,1)S(1)}, u32[]{:S(2)}, u32[]{:S(2)}) collective-permute-start(bf16[1,6,48,320]{3,2,1,0:T(8,128)(2,1)} %param.10), channel_id=1, source_target_pairs={{4,0},{8,4},{12,8},{5,1},{9,5},{13,9},{6,2},{10,6},{14,10},{7,3},{... | collective-permute-start | bytes 552968 | tf_op jit(solution)/shard_map/ppermute | solution.py:18
  21.7 2.8 %copy-start.2 = (bf16[18,320]{1,0:T(8,128)(2,1)S(1)}, bf16[18,320]{1,0:T(8,128)(2,1)}, u32[]{:S(2)}) copy-start(bf16[18,320]{1,0:T(8,128)(2,1)} %param.17) | copy-start | bytes 34564
  21.7 4.7 %copy-start.3 = (bf16[640,320]{0,1:T(8,128)(2,1)S(1)}, bf16[640,320]{0,1:T(8,128)(2,1)}, u32[]{:S(2)}) copy-start(bf16[640,320]{0,1:T(8,128)(2,1)} %param.15) | copy-start | bytes 1228804
  21.7 4.7 %copy-start.4 = (bf16[640,320]{0,1:T(8,128)(2,1)S(1)}, bf16[640,320]{0,1:T(8,128)(2,1)}, u32[]{:S(2)}) copy-start(bf16[640,320]{0,1:T(8,128)(2,1)} %param.14) | copy-start | bytes 1228804
  24.4 67.7 %reduce-scatter.4.cloned.1.call-start = ((), (), s32[]{:S(2)}) async-start(), calls=%async_computation.2 | async-start | bytes 1474560
  70.8 2.1 %copy-start.5 = (bf16[640,320]{0,1:T(8,128)(2,1)S(1)}, bf16[640,320]{0,1:T(8,128)(2,1)}, u32[]{:S(2)}) copy-start(bf16[640,320]{0,1:T(8,128)(2,1)} %param.13) | copy-start | bytes 1228804
  70.8 2.1 %copy-start.6 = (f32[640]{0:T(1024)S(1)}, f32[640]{0:T(1024)}, u32[]{:S(2)}) copy-start(f32[640]{0:T(1024)} %param.11) | copy-start | bytes 7684
  72.6 1.0 copy-start.1
Sparse Core Ops, SparseCore 0:
  24.5 13.5 all-gather.3
  84.3 7.6 reduce-scatter.3
where the time goes:
time: 102 us
  blocking collectives  32.7 us (32%)
  local copies, waits for them, and re-layouts  18.7 us (18%)
  waiting for transfers between devices  15.5 us (15%)
  between operations  13.7 us (13%)
  matrix products  12 us (12%)
  starting transfers between devices  6.4 us (6%)
  other arithmetic  2.41 us (2%)
    all_gather x1, blocking collectives, body(): lax.all_gather(jnp.dot(ref_full, w_both, preferred_element_type=jnp.float...  30.8 us
    unnamed x23, local copies, waits for them, and re-layouts  10.5 us
    unnamed x3, waiting for transfers between devices  7.85 us
    ppermute x1, starting transfers between devices, with_halo(): lax.ppermute(lax.slice_in_dim(block, block.shape[dim] - width, None, axis...  5.06 us
    ppermute x1, waiting for transfers between devices, with_halo(): lax.ppermute(lax.slice_in_dim(block, 0, width, axis=dim), axis, backward)  4.02 us
    dot_general x4, matrix products, attend_head(): jnp.dot(probs, value_head, preferred_element_type=jnp.float32) / total  3.96 us
    slice x1, local copies, waits for them, and re-layouts, temporal_terms(): padded[2:2 + frames_here]  3.84 us
    ppermute x1, waiting for transfers between devices, with_halo(): lax.ppermute(lax.slice_in_dim(block, block.shape[dim] - width, None, axis...  3.67 us
  transfers between devices with their start and end apart: 4, of which 3 were waited for; matrix products, arithmetic and copies ran while one was open for 2% of the time, Pallas kernels for 0%

commit v1 on v0

v1 whole, which is shorter than its diff:
```python
import functools

import jax
import jax.numpy as jnp
from jax import lax
from jax.experimental import pallas as pl
from jax.experimental.pallas import tpu as pltpu
from jax.sharding import PartitionSpec as P

C = 640
HEADS = 8
EPS = 1e-05

F32 = jnp.float32
BF16 = jnp.bfloat16


def nt_dot(a, b):
    return lax.dot_general(a, b, (((1,), (1,)), ((), ())), preferred_element_type=F32)


def tn_dot(a, b):
    return lax.dot_general(a, b, (((0,), (0,)), ((), ())), preferred_element_type=F32)


def sibling(x):
    return lax.ppermute(x, "heads", [(0, 1), (1, 0)])


def frame_pairs(x):
    count = lax.axis_size("frames")
    perm = []
    for core in range(2):
        for low in range(core, count - 1, 2):
            perm.append((low * 2 + core, (low + 1) * 2 + core))
            perm.append(((low + 1) * 2 + core, low * 2 + core))
    return lax.ppermute(x, ("frames", "heads"), perm)


def gather_blocks(x, axis):
    count = lax.axis_size(axis)
    if count & (count - 1):
        return lax.all_gather(x, axis, axis=0, tiled=True)
    step = 1
    while step < count:
        other = lax.ppermute(x, axis, [(i, i ^ step) for i in range(count)])
        x = jnp.concatenate([x, other], axis=0)
        step *= 2
    return x


def join_halves(core, own, other):
    first = jnp.where(core == 0, own, other)
    second = jnp.where(core == 0, other, own)
    return jnp.concatenate([first, second], axis=-1)


def middle_kernel(full_ref, w_ref, acc_ref):
    full = full_ref[...]
    acc_ref[...] = full.astype(F32) + jnp.dot(full, w_ref[1], preferred_element_type=F32)


def query_kernel(acc_ref, own_ref, other_ref, w_ref, wq_own_ref, wq_other_ref, gain_ref, temporal_ref, query_ref):
    core = lax.axis_index("heads")
    frame = lax.axis_index("frames")
    tap = jnp.where(lax.rem(frame, 2) == core, 2, 0)
    summed = acc_ref[...]
    summed = summed + jnp.dot(own_ref[...], w_ref[tap], preferred_element_type=F32)
    summed = summed + jnp.dot(other_ref[...], w_ref[2 - tap], preferred_element_type=F32)
    temporal = summed.astype(BF16)
    temporal_ref[...] = temporal
    feats = temporal.astype(F32)
    centre = jnp.mean(feats, axis=-1, keepdims=True)
    centred = feats - centre
    spread = jnp.mean(centred * centred, axis=-1, keepdims=True)
    normed = (centred * lax.rsqrt(spread + EPS) * gain_ref[...]).astype(BF16)
    scale = (C // HEADS) ** -0.5
    half = wq_own_ref.shape[0]
    query_ref[:half] = (nt_dot(wq_own_ref[...], normed) * scale).astype(BF16)
    query_ref[half:] = (nt_dot(wq_other_ref[...], normed) * scale).astype(BF16)


def attend_kernel(
    tok_ref, query_ref, temporal_ref, wk_own_ref, wk_other_ref, wv_own_ref, wv_other_ref, wo_own_ref, wo_other_ref,
    out_ref, tokens, attended,
):
    core = lax.axis_index("heads")
    blocks, width, _ = tok_ref.shape
    for i in range(blocks):
        tokens[i * width : (i + 1) * width] = tok_ref[i]
    toks = tokens[...].astype(BF16)
    size = C // HEADS
    half = wk_own_ref.shape[0]
    for part, (wk_ref, wv_ref) in enumerate(((wk_own_ref, wv_own_ref), (wk_other_ref, wv_other_ref))):
        values = nt_dot(wv_ref[...], toks).astype(BF16)
        for head in range(half // size):
            rows = slice(head * size, (head + 1) * size)
            keys = nt_dot(toks, wk_ref[rows]).astype(BF16)
            at = part * half + head * size
            scores = jnp.dot(keys, query_ref[at : at + size], preferred_element_type=F32)
            expo = jnp.exp(scores - jnp.max(scores, axis=0, keepdims=True))
            total = jnp.sum(expo, axis=0, keepdims=True)
            mixed = jnp.dot(values[rows], expo.astype(BF16), preferred_element_type=F32)
            attended[at : at + size] = (mixed / total).astype(BF16)
    mixed = tn_dot(attended[:half], wo_own_ref[...]) + tn_dot(attended[half:], wo_other_ref[...])
    mixed = temporal_ref[...].astype(F32) + mixed
    out_ref[...] = jnp.where(core == 0, mixed[:, :half], mixed[:, half:]).astype(BF16)


VMEM = pl.BlockSpec(memory_space=pltpu.VMEM)


def call(kernel, operands, outs, scratch=(), flops=0):
    return pl.pallas_call(
        kernel,
        out_shape=[jax.ShapeDtypeStruct(shape, dtype) for shape, dtype in outs],
        in_specs=[VMEM] * len(operands),
        out_specs=[VMEM] * len(outs),
        scratch_shapes=list(scratch),
        compiler_params=pltpu.CompilerParams(vmem_limit_bytes=48 * 2**20),
        cost_estimate=pl.CostEstimate(
            flops=flops, bytes_accessed=sum(x.size * x.dtype.itemsize for x in operands), transcendentals=0
        ),
    )(*operands)


def body(clip_latent, norm_gain, w_time, w_query, w_key, w_value, w_out, reference_tokens):
    frames_here, rows_here, cols_here, half = clip_latent.shape
    assert frames_here == 1 and lax.axis_size("heads") == 2
    core = lax.axis_index("heads")
    places = rows_here * cols_here
    clip = clip_latent.reshape(places, half)
    full = join_halves(core, clip, sibling(clip))
    near = frame_pairs(full)
    wq, wk, wv = w_query.T, w_key.T, w_value.T
    wq_other, wk_other, wv_other, wo_other = sibling(wq), sibling(wk), sibling(wv), sibling(w_out)
    toks = gather_blocks(gather_blocks(reference_tokens[None], "rows"), "frames")
    toks = join_halves(core, toks, sibling(toks))
    near_other = sibling(near)
    (acc,) = call(middle_kernel, (full, w_time), [((places, C), F32)], flops=2 * places * C * C)
    temporal, query = call(
        query_kernel,
        (acc, near, near_other, w_time, wq, wq_other, norm_gain[None]),
        [((places, C), BF16), ((C, places), BF16)],
        flops=6 * places * C * C,
    )
    count = toks.shape[0] * toks.shape[1]
    (out,) = call(
        attend_kernel,
        (toks, query, temporal, wk, wk_other, wv, wv_other, w_out, wo_other),
        [((places, half), BF16)],
        [pltpu.VMEM((count, C), BF16), pltpu.VMEM((C, places), BF16)],
        flops=4 * places * count * C + 2 * places * C * C + 4 * count * C * C,
    )
    return out.reshape(clip_latent.shape)


def solution(mesh):
    return jax.shard_map(
        body,
        mesh=mesh,
        in_specs=(
            P(("groups", "frames"), "rows", None, "heads"),
            P(),
            P(),
            P(None, "heads"),
            P(None, "heads"),
            P(None, "heads"),
            P("heads", None),
            P(("groups", "frames", "rows"), "heads"),
        ),
        out_specs=P(("groups", "frames"), "rows", None, "heads"),
        check_vma=False,
    )
```

time: 102 us -> 31.7 us (0.31)
  the two profiles are of different devices: /device:TPU:0 before, /device:TPU:11 now
where the time goes in v1:
time: 31.7 us; the launch traced here: 31.3 us
  waiting for transfers between devices  10 us (32%)
  starting transfers between devices  9.42 us (30%)
  Pallas kernels  6.7 us (21%)
  other arithmetic  4.25 us (13%)
  local copies, waits for them, and re-layouts  0.72 us (2%)
    ppermute x3, waiting for transfers between devices, gather_blocks(): other = lax.ppermute(x, axis, [(i, i ^ step) for i in range(count)])  9.31 us
    pallas_call x3, Pallas kernels, call(): pl.pallas_call(kernel, out_shape=[jax.ShapeDtypeStruct(shape, dtype) for...  6.7 us
    ppermute x7, starting transfers between devices, sibling(): return lax.ppermute(x, 'heads', [(0, 1), (1, 0)])  4.52 us
    ppermute x1, starting transfers between devices, frame_pairs(): return lax.ppermute(x, ('frames', 'heads'), perm)  4.33 us
    concatenate x3, other arithmetic, gather_blocks(): x = jnp.concatenate([x, other], axis=0)  2.24 us
    select_n x2, other arithmetic, join_halves(): first = jnp.where(core == 0, own, other)  1.77 us
    ppermute x7, waiting for transfers between devices, sibling(): return lax.ppermute(x, 'heads', [(0, 1), (1, 0)])  0.72 us
    broadcast_in_dim x1, local copies, waits for them, and re-layouts, body(): norm_gain[None]  0.69 us
  transfers between devices with their start and end apart: 11, of which 3 were waited for; matrix products, arithmetic and copies ran while one was open for 16% of the time, Pallas kernels for 7%

profile of v1, /device:TPU:11, one launch (start us, length us, event | category | flops | bytes accessed | tf_op | source)
XLA Modules:
  0.0 31.3 jit_solution(11732312050528085800)
XLA Ops:
  0.0 0.7 %collective-permute-start.4 = (bf16[288,320]{1,0:T(8,128)(2,1)}, bf16[288,320]{1,0:T(8,128)(2,1)S(1)}, u32[]{:S(2)}, u32[]{:S(2)}) collective-permute-start(bf16[288,320]{1,0:T(8,128)(2,1)} %bitcast.19), channel_id=1, source_target_pairs={{0,1},{1,0},{2,3},{3,2},{4,5},{5,4},{6,7},{7,6},{8,9},{9,8},{10,11... | collective-permute-start | bytes 552968 | tf_op jit(solution)/shard_map/ppermute | solution.py:27
  0.7 0.3 collective-permute-start
  0.9 2.6 %collective-permute-done = bf16[1,18,320]{2,1,0:T(8,128)(2,1)S(1)} collective-permute-done((bf16[1,18,320]{2,1,0:T(8,128)(2,1)}, bf16[1,18,320]{2,1,0:T(8,128)(2,1)S(1)}, u32[]{:S(2)}, u32[]{:S(2)}) %collective-permute-start) | collective-permute-done | bytes 11552 | tf_op jit(solution)/shard_map/ppermute | solution.py:46
  3.5 0.7 %pad_maximum_fusion.4 = bf16[2,18,320]{2,1,0:T(8,128)(2,1)S(1)} fusion(bf16[1,18,320]{2,1,0:T(8,128)(2,1)S(1)} %collective-permute-done, bf16[1,18,320]{2,1,0:T(8,128)(2,1)} %bitcast.15), kind=kLoop, calls=%fused_computation.8 | loop fusion | flops 11520 | bytes 46080 | tf_op jit(solution)/shard_map/concatenate | solution.py:47
  4.2 0.2 collective-permute-start.1
  4.5 1.0 %broadcast_select_fusion.1 = (bf16[288,320]{1,0:T(8,128)(2,1)S(1)}, bf16[288,320]{1,0:T(8,128)(2,1)S(1)}) fusion(bf16[288,320]{1,0:T(8,128)(2,1)S(1)} %collective-permute-done.4, pred[]{:T(512)S(6)} %eq.2, bf16[1,6,48,320]{3,2,1,0:T(8,128)(2,1)} %param.8), kind=kLoop, calls=%fused_computation.3 | loop fusion | flops 184320 | bytes 737281 | tf_op jit(solution)/shard_map/jit(_where)/select_n | solution.py:53
  5.5 0.1 pad_maximum_fusion.full_ref
  5.6 4.3 %collective-permute-start.5 = (bf16[288,640]{1,0:T(8,128)(2,1)S(1)}, bf16[288,640]{1,0:T(8,128)(2,1)S(1)}, u32[]{:S(2)}, u32[]{:S(2)}) collective-permute-start(bf16[288,640]{1,0:T(8,128)(2,1)S(1)} %pad_maximum_fusion.full_ref), channel_id=1, source_target_pairs={{0,4},{4,0},{8,12},{12,8},{5,9},{9,5},{2,6},{6,2},{10,14},{14,10},... | collective-permute-start | bytes 1105928 | tf_op jit(solution)/shard_map/ppermute | solution.py:37
  9.9 0.7 %pad_maximum_fusion.3 = bf16[4,18,320]{2,1,0:T(8,128)(2,1)S(1)} fusion(bf16[2,18,320]{2,1,0:T(8,128)(2,1)S(1)} %collective-permute-done.1, bf16[1,18,320]{2,1,0:T(8,128)(2,1)S(1)} %collective-permute-done, bf16[1,18,320]{2,1,0:T(8,128)(2,1)} %bitcast.16), kind=kLoop, calls=%fused_computation.7 | loop fusion | flops 46080 | bytes 92160 | tf_op jit(solution)/shard_map/concatenate | solution.py:47
  10.8 6.7 %collective-permute-done.2 = bf16[4,18,320]{2,1,0:T(8,128)(2,1)S(1)} collective-permute-done((bf16[4,18,320]{2,1,0:T(8,128)(2,1)S(1)}, bf16[4,18,320]{2,1,0:T(8,128)(2,1)S(1)}, u32[]{:S(2)}, u32[]{:S(2)}) %collective-permute-start.2) | collective-permute-done | bytes 46112 | tf_op jit(solution)/shard_map/ppermute | solution.py:46
  17.5 0.8 %pad_maximum_fusion.2 = bf16[8,18,320]{2,1,0:T(8,128)(2,1)S(1)} fusion(bf16[4,18,320]{2,1,0:T(8,128)(2,1)S(1)} %collective-permute-done.2, bf16[2,18,320]{2,1,0:T(8,128)(2,1)S(1)} %collective-permute-done.1, bf16[1,18,320]{2,1,0:T(8,128)(2,1)S(1)} %collective-permute-done, bf16[1,18,320]{2,1,0:T(8,128)(2,1)} %bitcast.17), kind=kLoop, calls=%fused_computation.4 | loop fusion | flops 138240 | bytes 184320 | tf_op jit(solution)/shard_map/concatenate | solution.py:47
  18.3 2.7 %collective-permute-start.3 = (bf16[8,18,320]{2,1,0:T(8,128)(2,1)S(1)}, bf16[8,18,320]{2,1,0:T(8,128)(2,1)S(1)}, u32[]{:S(2)}, u32[]{:S(2)}) collective-permute-start(bf16[8,18,320]{2,1,0:T(8,128)(2,1)S(1)} %pad_maximum_fusion.2), channel_id=1, source_target_pairs={{0,1},{1,0},{2,3},{3,2},{4,5},{5,4},{6,7},{7,6},{8,9},{9,8},{10,11... | collective-permute-start | bytes 276488 | tf_op jit(solution)/shard_map/ppermute | solution.py:27
  21.0 0.1 collective-permute-start.7
  21.1 0.4 %collective-permute-start.8 = (bf16[320,640]{1,0:T(8,128)(2,1)}, bf16[320,640]{1,0:T(8,128)(2,1)S(1)}, u32[]{:S(2)}, u32[]{:S(2)}) collective-permute-start(bf16[320,640]{1,0:T(8,128)(2,1)} %bitcast.10), channel_id=1, source_target_pairs={{0,1},{1,0},{2,3},{3,2},{4,5},{5,4},{6,7},{7,6},{8,9},{9,8},{10,11... | collective-permute-start | bytes 1228808 | tf_op jit(solution)/shard_map/ppermute | solution.py:27
  21.6 0.1 collective-permute-start.9
  21.6 0.7 %broadcast_in_dim.7.gain_ref = f32[1,640]{1,0:T(1,128)S(1)} reshape(f32[640]{0:T(1024)} %param.9) | data formatting | bytes 5120 | tf_op jit(solution)/shard_map/broadcast_in_dim | solution.py:143
  22.3 0.4 %collective-permute-start.10 = (bf16[320,640]{1,0:T(8,128)(2,1)}, bf16[320,640]{1,0:T(8,128)(2,1)S(1)}, u32[]{:S(2)}, u32[]{:S(2)}) collective-permute-start(bf16[320,640]{1,0:T(8,128)(2,1)} %wo_own_ref.1), channel_id=1, source_target_pairs={{0,1},{1,0},{2,3},{3,2},{4,5},{5,4},{6,7},{7,6},{8,9},{9,8},{10,11... | collective-permute-start | bytes 1228808 | tf_op jit(solution)/shard_map/ppermute | solution.py:27
  22.8 0.1 collective-permute-start.6
  22.8 0.8 %broadcast_select_fusion.3 = (bf16[8,18,320]{2,1,0:T(8,128)(2,1)S(1)}, bf16[8,18,320]{2,1,0:T(8,128)(2,1)S(1)}) fusion(bf16[8,18,320]{2,1,0:T(8,128)(2,1)S(1)} %collective-permute-done.3, pred[]{:T(512)S(6)} %eq.2, bf16[4,18,320]{2,1,0:T(8,128)(2,1)S(1)} %collective-permute-done.2, bf16[2,18,320]{2,1,0:T(8,128)(2,1)S(1)} %collective-permute-done.1, ...), kind=kLoop, calls=%fused_computation.6 | loop fusion | flops 230400 | bytes 368641 | tf_op jit(solution)/shard_map/jit(_where)/select_n | solution.py:53
  23.6 0.1 pad_maximum_fusion.1.tok_ref
  23.8 0.5 %shard_map.82.acc_ref = f32[288,640]{1,0:T(8,128)S(1)} custom-call(bf16[288,640]{1,0:T(8,128)(2,1)S(1)} %pad_maximum_fusion.full_ref, bf16[3,640,640]{2,1,0:T(8,128)(2,1)S(1)} %copy-done), custom_call_target="tpu_custom_call" | custom-call | flops 235929600 | bytes 2826240 | tf_op jit(solution)/shard_map/pallas_call | solution.py:114
  24.3 0.7 %collective-permute-done.6.other_ref = bf16[288,640]{1,0:T(8,128)(2,1)S(1)} collective-permute-done((bf16[288,640]{1,0:T(8,128)(2,1)S(1)}, bf16[288,640]{1,0:T(8,128)(2,1)S(1)}, u32[]{:S(2)}, u32[]{:S(2)}) %collective-permute-start.6) | collective-permute-done | bytes 368672 | tf_op jit(solution)/shard_map/ppermute | solution.py:27
  25.0 1.7 %shard_map.83 = (bf16[288,640]{1,0:T(8,128)(2,1)S(1)}, bf16[640,288]{1,0:T(8,128)(2,1)S(1)}) custom-call(f32[288,640]{1,0:T(8,128)S(1)} %shard_map.82.acc_ref, bf16[288,640]{1,0:T(8,128)(2,1)S(1)} %collective-permute-done.5.own_ref, bf16[288,640]{1,0:T(8,128)(2,1)S(1)} %collective-permute-done.6.other_ref, bf16[3,640,640]{2,1,0:T(8,128)(2,1)S(1)} %copy-done, ...), custom_call_target="tpu_custom_call" | custom-call | flops 707788800 | bytes 4753920 | tf_op jit(solution)/shard_map/pallas_call | solution.py:114
  26.8 4.5 %shard_map.84 = bf16[288,320]{1,0:T(8,128)(2,1)} custom-call(bf16[8,18,640]{2,1,0:T(8,128)(2,1)S(1)} %pad_maximum_fusion.1.tok_ref, bf16[640,288]{1,0:T(8,128)(2,1)S(1)} %get-tuple-element.7.query_ref, bf16[288,640]{1,0:T(8,128)(2,1)S(1)} %get-tuple-element.8.temporal_ref, bf16[320,640]{1,0:T(8,128)(2,1)S(1)} %bitcast.11, ...), custom_call_target="tpu_custom_call" | custom-call | flops 578027520 | bytes 3379200 | tf_op jit(solution)/shard_map/pallas_call | solution.py:114
  (19 shorter events, 0.1 us)
Async XLA Ops:
  0.0 23.7 %copy-start = (bf16[3,640,640]{2,1,0:T(8,128)(2,1)S(1)}, bf16[3,640,640]{2,1,0:T(8,128)(2,1)}, u32[]{:S(2)}) copy-start(bf16[3,640,640]{2,1,0:T(8,128)(2,1)} %w_ref.3) | copy-start | bytes 7372804
  0.0 4.5 %collective-permute-start.4 = (bf16[288,320]{1,0:T(8,128)(2,1)}, bf16[288,320]{1,0:T(8,128)(2,1)S(1)}, u32[]{:S(2)}, u32[]{:S(2)}) collective-permute-start(bf16[288,320]{1,0:T(8,128)(2,1)} %bitcast.19), channel_id=1, source_target_pairs={{0,1},{1,0},{2,3},{3,2},{4,5},{5,4},{6,7},{7,6},{8,9},{9,8},{10,11... | collective-permute-start | bytes 552968 | tf_op jit(solution)/shard_map/ppermute | solution.py:27
  0.7 2.8 %collective-permute-start = (bf16[1,18,320]{2,1,0:T(8,128)(2,1)}, bf16[1,18,320]{2,1,0:T(8,128)(2,1)S(1)}, u32[]{:S(2)}, u32[]{:S(2)}) collective-permute-start(bf16[1,18,320]{2,1,0:T(8,128)(2,1)} %bitcast.14), channel_id=1, source_target_pairs={{0,2},{2,0},{1,3},{3,1},{4,6},{6,4},{5,7},{7,5},{8,10},{10,8},{9,1... | collective-permute-start | bytes 34568 | tf_op jit(solution)/shard_map/ppermute | solution.py:46
  4.2 5.7 %collective-permute-start.1 = (bf16[2,18,320]{2,1,0:T(8,128)(2,1)S(1)}, bf16[2,18,320]{2,1,0:T(8,128)(2,1)S(1)}, u32[]{:S(2)}, u32[]{:S(2)}) collective-permute-start(bf16[2,18,320]{2,1,0:T(8,128)(2,1)S(1)} %pad_maximum_fusion.4), channel_id=1, source_target_pairs={{0,4},{4,0},{8,12},{12,8},{1,5},{5,1},{9,13},{13,9},{2,6},{6,2},{1... | collective-permute-start | bytes 69128 | tf_op jit(solution)/shard_map/ppermute | solution.py:46
  5.6 17.2 %collective-permute-start.5 = (bf16[288,640]{1,0:T(8,128)(2,1)S(1)}, bf16[288,640]{1,0:T(8,128)(2,1)S(1)}, u32[]{:S(2)}, u32[]{:S(2)}) collective-permute-start(bf16[288,640]{1,0:T(8,128)(2,1)S(1)} %pad_maximum_fusion.full_ref), channel_id=1, source_target_pairs={{0,4},{4,0},{8,12},{12,8},{5,9},{9,5},{2,6},{6,2},{10,14},{14,10},... | collective-permute-start | bytes 1105928 | tf_op jit(solution)/shard_map/ppermute | solution.py:37
  10.7 14.3 %copy-start.1 = (bf16[640,320]{0,1:T(8,128)(2,1)S(1)}, bf16[640,320]{0,1:T(8,128)(2,1)}, u32[]{:S(2)}) copy-start(bf16[640,320]{0,1:T(8,128)(2,1)} %param.11) | copy-start | bytes 1228804
  10.7 6.8 %collective-permute-start.2 = (bf16[4,18,320]{2,1,0:T(8,128)(2,1)S(1)}, bf16[4,18,320]{2,1,0:T(8,128)(2,1)S(1)}, u32[]{:S(2)}, u32[]{:S(2)}) collective-permute-start(bf16[4,18,320]{2,1,0:T(8,128)(2,1)S(1)} %pad_maximum_fusion.3), channel_id=1, source_target_pairs={{0,8},{4,12},{8,0},{12,4},{1,9},{5,13},{9,1},{13,5},{2,10},{6,14},... | collective-permute-start | bytes 138248 | tf_op jit(solution)/shard_map/ppermute | solution.py:46
  18.3 4.0 %collective-permute-start.3 = (bf16[8,18,320]{2,1,0:T(8,128)(2,1)S(1)}, bf16[8,18,320]{2,1,0:T(8,128)(2,1)S(1)}, u32[]{:S(2)}, u32[]{:S(2)}) collective-permute-start(bf16[8,18,320]{2,1,0:T(8,128)(2,1)S(1)} %pad_maximum_fusion.2), channel_id=1, source_target_pairs={{0,1},{1,0},{2,3},{3,2},{4,5},{5,4},{6,7},{7,6},{8,9},{9,8},{10,11... | collective-permute-start | bytes 276488 | tf_op jit(solution)/shard_map/ppermute | solution.py:27
  21.0 3.3 %collective-permute-start.7 = (bf16[320,640]{1,0:T(8,128)(2,1)}, bf16[320,640]{1,0:T(8,128)(2,1)S(1)}, u32[]{:S(2)}, u32[]{:S(2)}) collective-permute-start(bf16[320,640]{1,0:T(8,128)(2,1)} %bitcast.8), channel_id=1, source_target_pairs={{0,1},{1,0},{2,3},{3,2},{4,5},{5,4},{6,7},{7,6},{8,9},{9,8},{10,11... | collective-permute-start | bytes 1228808 | tf_op jit(solution)/shard_map/ppermute | solution.py:27
  21.1 5.6 %collective-permute-start.8 = (bf16[320,640]{1,0:T(8,128)(2,1)}, bf16[320,640]{1,0:T(8,128)(2,1)S(1)}, u32[]{:S(2)}, u32[]{:S(2)}) collective-permute-start(bf16[320,640]{1,0:T(8,128)(2,1)} %bitcast.10), channel_id=1, source_target_pairs={{0,1},{1,0},{2,3},{3,2},{4,5},{5,4},{6,7},{7,6},{8,9},{9,8},{10,11... | collective-permute-start | bytes 1228808 | tf_op jit(solution)/shard_map/ppermute | solution.py:27
  21.6 5.2 %collective-permute-start.9 = (bf16[320,640]{1,0:T(8,128)(2,1)}, bf16[320,640]{1,0:T(8,128)(2,1)S(1)}, u32[]{:S(2)}, u32[]{:S(2)}) collective-permute-start(bf16[320,640]{1,0:T(8,128)(2,1)} %bitcast.12), channel_id=1, source_target_pairs={{0,1},{1,0},{2,3},{3,2},{4,5},{5,4},{6,7},{7,6},{8,9},{9,8},{10,11... | collective-permute-start | bytes 1228808 | tf_op jit(solution)/shard_map/ppermute | solution.py:27
  22.3 4.4 %collective-permute-start.10 = (bf16[320,640]{1,0:T(8,128)(2,1)}, bf16[320,640]{1,0:T(8,128)(2,1)S(1)}, u32[]{:S(2)}, u32[]{:S(2)}) collective-permute-start(bf16[320,640]{1,0:T(8,128)(2,1)} %wo_own_ref.1), channel_id=1, source_target_pairs={{0,1},{1,0},{2,3},{3,2},{4,5},{5,4},{6,7},{7,6},{8,9},{9,8},{10,11... | collective-permute-start | bytes 1228808 | tf_op jit(solution)/shard_map/ppermute | solution.py:27
  22.8 2.3 %collective-permute-start.6 = (bf16[288,640]{1,0:T(8,128)(2,1)S(1)}, bf16[288,640]{1,0:T(8,128)(2,1)S(1)}, u32[]{:S(2)}, u32[]{:S(2)}) collective-permute-start(bf16[288,640]{1,0:T(8,128)(2,1)S(1)} %collective-permute-done.5.own_ref), channel_id=1, source_target_pairs={{0,1},{1,0},{2,3},{3,2},{4,5},{5,4},{6,7},{7,6},{8,9},{9,8},{10,11... | collective-permute-start | bytes 1105928 | tf_op jit(solution)/shard_map/ppermute | solution.py:27
  24.3 2.5 %copy-start.2 = (bf16[640,320]{0,1:T(8,128)(2,1)S(1)}, bf16[640,320]{0,1:T(8,128)(2,1)}, u32[]{:S(2)}) copy-start(bf16[640,320]{0,1:T(8,128)(2,1)} %param.12) | copy-start | bytes 1228804
  24.3 2.5 %copy-start.3 = (bf16[640,320]{0,1:T(8,128)(2,1)S(1)}, bf16[640,320]{0,1:T(8,128)(2,1)}, u32[]{:S(2)}) copy-start(bf16[640,320]{0,1:T(8,128)(2,1)} %param.13) | copy-start | bytes 1228804
  24.3 2.5 %copy-start.4 = (bf16[320,640]{1,0:T(8,128)(2,1)S(1)}, bf16[320,640]{1,0:T(8,128)(2,1)}, u32[]{:S(2)}) copy-start(bf16[320,640]{1,0:T(8,128)(2,1)} %wo_own_ref.1) | copy-start | bytes 1228804

commit v2 on v1

v2 whole, which is shorter than its diff:
```python
import functools

import jax
import jax.numpy as jnp
from jax import lax
from jax.experimental import pallas as pl
from jax.experimental.pallas import tpu as pltpu
from jax.sharding import PartitionSpec as P

C = 640
HEADS = 8
EPS = 1e-05

PACK, SHARE, FAR = 10**9, 10**9, 5 * 10**9
MIDDLE, FIRST, SECOND, QUERY, ATTEND = 5 * 10**8, 5 * 10**8, 3 * 10**8, 10**9, 2 * 10**9

F32 = jnp.float32
BF16 = jnp.bfloat16


def nt_dot(a, b):
    return lax.dot_general(a, b, (((1,), (1,)), ((), ())), preferred_element_type=F32)


def tn_dot(a, b):
    return lax.dot_general(a, b, (((0,), (0,)), ((), ())), preferred_element_type=F32)


def sibling(x):
    return lax.ppermute(x, "heads", [(0, 1), (1, 0)])


def swap(x, partner):
    frames, rows = lax.axis_size("frames"), lax.axis_size("rows")
    perm = []
    for frame in range(frames):
        for row in range(rows):
            for core in range(2):
                to = partner(frame, row, core)
                if to is not None:
                    perm.append((((frame * rows) + row) * 2 + core, ((to[0] * rows) + to[1]) * 2 + to[2]))
    return lax.ppermute(x, ("frames", "rows", "heads"), perm)


def swap_near(x):
    frames, rows = lax.axis_size("frames"), lax.axis_size("rows")

    def partner(frame, row, core):
        to = frame + 1 if frame % 2 == core else frame - 1
        if 0 <= to < frames:
            return to, row, core
        return (frame, row ^ 1, core) if rows % 2 == 0 else None

    return swap(x, partner)


def swap_far(x):
    return swap(x, lambda frame, row, core: (frame ^ (3 if core else 2), row, core))


def swap_bit(x, axis, bit):
    return lax.ppermute(x, axis, [(i, i ^ bit) for i in range(lax.axis_size(axis))])


VMEM = pl.BlockSpec(memory_space=pltpu.VMEM)


def call(kernel, operands, outs, scratch=(), flops=0):
    return pl.pallas_call(
        kernel,
        out_shape=[jax.ShapeDtypeStruct(shape, dtype) for shape, dtype in outs],
        in_specs=[VMEM] * len(operands),
        out_specs=[VMEM] * len(outs),
        scratch_shapes=list(scratch),
        compiler_params=pltpu.CompilerParams(vmem_limit_bytes=40 * 2**20),
        cost_estimate=pl.CostEstimate(flops=flops, bytes_accessed=0, transcendentals=0),
    )(*operands)


def pack_kernel(clip_other_ref, tok_ref, tok_other_ref, message_ref, pair_ref):
    places, width = clip_other_ref.shape[0], tok_ref.shape[0]
    message_ref[:places] = clip_other_ref[...]
    message_ref[places : places + width] = pair_ref[0] = tok_ref[...]
    message_ref[places + width :] = pair_ref[1] = tok_other_ref[...]


def stack_kernel(*refs):
    at = 0
    for ref in refs[:-1]:
        refs[-1][at : at + ref.shape[0]] = ref[...]
        at += ref.shape[0]


def stack(*parts, flops):
    shape = (sum(part.shape[0] for part in parts),) + parts[0].shape[1:]
    return call(stack_kernel, parts, [(shape, BF16)], flops=flops)[0]


def share_kernel(frames, pair_ref, near_ref, far_ref, out_ref):
    core = lax.axis_index("heads")
    frame = lax.axis_index("frames")
    edge = (frame == 0) | (frame == frames - 1)
    width = pair_ref.shape[1]
    places = near_ref.shape[0] - 2 * width
    for side in range(2):
        near = near_ref[places + side * width : places + (side + 1) * width]
        out_ref[side] = jnp.where(core == 0, near, pair_ref[side])
        out_ref[2 + side] = jnp.where((core == 0) | edge, far_ref[side], near)


def gather_tokens(pair, near):
    frames, rows = lax.axis_size("frames"), lax.axis_size("rows")
    if frames == 4 and rows == 2:
        far = stack(swap_far(pair), flops=FAR)
        (mine,) = call(
            functools.partial(share_kernel, frames),
            (pair, near, far),
            [((4,) + pair.shape[1:], BF16)],
            flops=SHARE,
        )
        met = swap_bit(mine, "rows", 1)
        return [(mine, False), (sibling(mine), True), (met, False), (sibling(met), True)]
    parts = [pair]
    for axis, count in (("frames", frames), ("rows", rows)):
        assert count & (count - 1) == 0
        bit = 1
        while bit < count:
            held = stack(*parts, flops=SHARE)
            parts = [held, swap_bit(held, axis, bit)]
            bit *= 2
    return [(part, False) for part in parts]


def halves(core, half):
    own = pl.multiple_of(core * half, 16)
    return pl.ds(own, half), pl.ds(pl.multiple_of(half - own, 16), half)


def beside(near_ref, places, core, frames):
    frame = lax.axis_index("frames")
    after = lax.rem(frame, 2) == core
    there = jnp.where(after, frame < frames - 1, frame > 0)
    near = near_ref[:places]
    return jnp.where(there, near, jnp.zeros_like(near)), jnp.where(after, 2, 0)


def middle_kernel(own_ref, other_ref, w_ref, wo_own_ref, wo_other_ref, acc_ref, wo_ref, full):
    core = lax.axis_index("heads")
    half = wo_own_ref.shape[0]
    own, other = own_ref[...], other_ref[...]
    full[:, :half] = jnp.where(core == 0, own, other)
    full[:, half:] = jnp.where(core == 0, other, own)
    whole = full[...]
    acc_ref[...] = whole.astype(F32) + jnp.dot(whole, w_ref[1], preferred_element_type=F32)
    wo_ref[:half] = jnp.where(core == 0, wo_own_ref[:, :half], wo_own_ref[:, half:])
    wo_ref[half:] = jnp.where(core == 0, wo_other_ref[:, :half], wo_other_ref[:, half:])


def first_kernel(frames, acc_ref, near_ref, near_other_ref, w_ref, sum_ref):
    core = lax.axis_index("heads")
    places = acc_ref.shape[0]
    own, other = halves(core, near_ref.shape[1])
    near, tap = beside(near_ref, places, core, frames)
    sums = acc_ref[...] + jnp.dot(near, w_ref[tap, own], preferred_element_type=F32)
    near, tap = beside(near_other_ref, places, 1 - core, frames)
    sum_ref[...] = sums + jnp.dot(near, w_ref[tap, other], preferred_element_type=F32)


def second_kernel(frames, acc_ref, near_ref, w_ref, sum_ref):
    core = lax.axis_index("heads")
    near, tap = beside(near_ref, acc_ref.shape[0], core, frames)
    other = halves(core, near_ref.shape[1])[1]
    sum_ref[...] = acc_ref[...] + jnp.dot(near, w_ref[tap, other], preferred_element_type=F32)


def query_kernel(frames, acc_ref, near_ref, w_ref, wq_own_ref, wq_other_ref, gain_ref, temporal_ref, query_ref):
    core = lax.axis_index("heads")
    half = wq_own_ref.shape[0]
    near, tap = beside(near_ref, acc_ref.shape[0], 1 - core, frames)
    own = halves(core, half)[0]
    temporal = (acc_ref[...] + jnp.dot(near, w_ref[tap, own], preferred_element_type=F32)).astype(BF16)
    temporal_ref[...] = jnp.where(core == 0, temporal[:, :half], temporal[:, half:])
    feats = temporal.astype(F32)
    centre = jnp.mean(feats, axis=-1, keepdims=True)
    centred = feats - centre
    spread = jnp.mean(centred * centred, axis=-1, keepdims=True)
    normed = (centred * lax.rsqrt(spread + EPS) * gain_ref[...]).astype(BF16)
    scale = (C // HEADS) ** -0.5
    query_ref[:half] = (nt_dot(wq_own_ref[...], normed) * scale).astype(BF16)
    query_ref[half:] = (nt_dot(wq_other_ref[...], normed) * scale).astype(BF16)


def attend_kernel(flipped, *refs):
    core = lax.axis_index("heads")
    blocks, refs = refs[: len(flipped)], refs[len(flipped) :]
    query_ref, temporal_ref, wk_own_ref, wk_other_ref, wv_own_ref, wv_other_ref, wo_ref = refs[:7]
    out_ref, tokens, keys, values, attended = refs[7:]
    half = wk_own_ref.shape[0]
    size = C // HEADS
    at = 0
    for ref, flip in zip(blocks, flipped):
        for i in range(0, ref.shape[0], 2):
            first, second = (ref[i + 1], ref[i]) if flip else (ref[i], ref[i + 1])
            rows = slice(at, at + ref.shape[1])
            tokens[rows, :half] = jnp.where(core == 0, first, second)
            tokens[rows, half:] = jnp.where(core == 0, second, first)
            at += ref.shape[1]
    toks = tokens[...]
    for part, (wk_ref, wv_ref) in enumerate(((wk_own_ref, wv_own_ref), (wk_other_ref, wv_other_ref))):
        values[part * half : (part + 1) * half] = nt_dot(wv_ref[...], toks).astype(BF16)
        found = nt_dot(toks, wk_ref[...]).astype(BF16)
        for head in range(half // size):
            keys[part * (half // size) + head, :, :size] = found[:, head * size : (head + 1) * size]
    probs = []
    for head in range(HEADS):
        rows = slice(head * size, (head + 1) * size)
        scores = jnp.dot(keys[head, :, :size], query_ref[rows], preferred_element_type=F32)
        expo = jnp.exp(scores - jnp.max(scores, axis=0, keepdims=True))
        probs.append((expo.astype(BF16), 1.0 / jnp.sum(expo, axis=0, keepdims=True)))
    for head in range(HEADS):
        rows = slice(head * size, (head + 1) * size)
        prob, inverse = probs[head]
        mixed = jnp.dot(values[rows], prob, preferred_element_type=F32)
        attended[rows] = (mixed * inverse).astype(BF16)
    mixed = tn_dot(attended[...], wo_ref[...])
    out_ref[...] = (temporal_ref[...].astype(F32) + mixed).astype(BF16)


def body(clip_latent, norm_gain, w_time, w_query, w_key, w_value, w_out, reference_tokens):
    frames_here, rows_here, cols_here, half = clip_latent.shape
    assert frames_here == 1 and lax.axis_size("heads") == 2
    places = rows_here * cols_here
    width = reference_tokens.shape[0]
    clip = clip_latent.reshape(places, half)
    frames = lax.axis_size("frames")
    clip_other, toks_other = sibling(clip), sibling(reference_tokens)
    near = swap_near(clip)
    message, pair = call(
        pack_kernel,
        (clip_other, reference_tokens, toks_other),
        [((places + 2 * width, half), BF16), ((2, width, half), BF16)],
        flops=PACK,
    )
    late = swap_near(message)
    near_other, late_other = sibling(near), sibling(late)
    toks = gather_tokens(pair, late)
    wq, wk, wv = w_query.T, w_key.T, w_value.T
    wq_other, wk_other, wv_other, wo_other = sibling(wq), sibling(wk), sibling(wv), sibling(w_out)
    acc, wo = call(
        middle_kernel,
        (clip, clip_other, w_time, w_out, wo_other),
        [((places, C), F32), ((C, half), BF16)],
        [pltpu.VMEM((places, C), BF16)],
        flops=MIDDLE,
    )
    (acc,) = call(
        functools.partial(first_kernel, frames),
        (acc, near, near_other, w_time),
        [((places, C), F32)],
        flops=FIRST,
    )
    (acc,) = call(
        functools.partial(second_kernel, frames), (acc, late, w_time), [((places, C), F32)], flops=SECOND
    )
    temporal, query = call(
        functools.partial(query_kernel, frames),
        (acc, late_other, w_time, wq, wq_other, norm_gain),
        [((places, half), BF16), ((C, places), BF16)],
        flops=QUERY,
    )
    count = width * frames * lax.axis_size("rows")
    (out,) = call(
        functools.partial(attend_kernel, [flip for _, flip in toks]),
        (*[part for part, _ in toks], query, temporal, wk, wk_other, wv, wv_other, wo),
        [((places, half), BF16)],
        [
            pltpu.VMEM((count, C), BF16),
            pltpu.VMEM((HEADS, count, 128), BF16),
            pltpu.VMEM((C, count), BF16),
            pltpu.VMEM((C, places), BF16),
        ],
        flops=ATTEND,
    )
    return out.reshape(clip_latent.shape)


def solution(mesh):
    return jax.shard_map(
        body,
        mesh=mesh,
        in_specs=(
            P(("groups", "frames"), "rows", None, "heads"),
            P(),
            P(),
            P(None, "heads"),
            P(None, "heads"),
            P(None, "heads"),
            P("heads", None),
            P(("groups", "frames", "rows"), "heads"),
        ),
        out_specs=P(("groups", "frames"), "rows", None, "heads"),
        check_vma=False,
    )
```

time: 31.7 us -> 24.9 us (0.79)
  the two profiles are of different devices: /device:TPU:11 before, /device:TPU:0 now
where the time goes in v2:
time: 24.9 us; the launch traced here: 24.5 us
  starting transfers between devices  10.4 us (42%)
  waiting for transfers between devices  6.83 us (27%)
  Pallas kernels  5.22 us (21%)
  local copies, waits for them, and re-layouts  1.91 us (8%)
    ppermute x3, starting transfers between devices, swap(): return lax.ppermute(x, ('frames', 'rows', 'heads'), perm)  5.99 us
    pallas_call x8, Pallas kernels, call(): pl.pallas_call(kernel, out_shape=[jax.ShapeDtypeStruct(shape, dtype) for...  5.22 us
    ppermute x3, waiting for transfers between devices, swap(): return lax.ppermute(x, ('frames', 'rows', 'heads'), perm)  3.85 us
    ppermute x10, starting transfers between devices, sibling(): return lax.ppermute(x, 'heads', [(0, 1), (1, 0)])  2.43 us
    ppermute x1, starting transfers between devices, swap_bit(): lax.ppermute(x, axis, [(i, i ^ bit) for i in range(lax.axis_size(axis))])  2 us
    unnamed x16, local copies, waits for them, and re-layouts  1.91 us
    ppermute x1, waiting for transfers between devices, swap_bit(): lax.ppermute(x, axis, [(i, i ^ bit) for i in range(lax.axis_size(axis))])  1.64 us
    ppermute x10, waiting for transfers between devices, sibling(): return lax.ppermute(x, 'heads', [(0, 1), (1, 0)])  1.34 us
  transfers between devices with their start and end apart: 14, of which 3 were waited for; matrix products, arithmetic and copies ran while one was open for 0% of the time, Pallas kernels for 12%

profile of v2, /device:TPU:0, one launch (start us, length us, event | category | flops | bytes accessed | tf_op | source)
XLA Modules:
  0.0 24.5 jit_solution(15020899617731333663)
XLA Ops:
  0.0 0.5 %collective-permute-start = (bf16[288,320]{1,0:T(8,128)(2,1)}, bf16[288,320]{1,0:T(8,128)(2,1)S(1)}, u32[]{:S(2)}, u32[]{:S(2)}) collective-permute-start(bf16[288,320]{1,0:T(8,128)(2,1)} %bitcast.7), channel_id=1, source_target_pairs={{0,1},{1,0},{2,3},{3,2},{4,5},{5,4},{6,7},{7,6},{8,9},{9,8},{10,11... | collective-permute-start | bytes 552968 | tf_op jit(solution)/shard_map/ppermute | solution.py:30
  0.5 0.1 collective-permute-start.1
  0.6 1.3 %collective-permute-done.1.tok_other_ref = bf16[18,320]{1,0:T(8,128)(2,1)S(1)} collective-permute-done((bf16[18,320]{1,0:T(8,128)(2,1)}, bf16[18,320]{1,0:T(8,128)(2,1)S(1)}, u32[]{:S(2)}, u32[]{:S(2)}) %collective-permute-start.1) | collective-permute-done | bytes 11552 | tf_op jit(solution)/shard_map/ppermute | solution.py:30
  1.9 0.0 collective-permute-done.clip_other_ref.other_ref
  2.0 0.7 %copy-done.7 = bf16[18,320]{1,0:T(8,128)(2,1)S(1)} copy-done((bf16[18,320]{1,0:T(8,128)(2,1)S(1)}, bf16[18,320]{1,0:T(8,128)(2,1)}, u32[]{:S(2)}) %copy-start.7) | copy-done | bytes 11544
  2.7 3.0 %collective-permute-start.2 = (bf16[324,320]{1,0:T(8,128)(2,1)S(1)}, bf16[324,320]{1,0:T(8,128)(2,1)S(1)}, u32[]{:S(2)}, u32[]{:S(2)}) collective-permute-start(bf16[324,320]{1,0:T(8,128)(2,1)S(1)} %get-tuple-element.12), channel_id=1, source_target_pairs={{0,4},{1,3},{2,6},{3,1},{4,0},{5,9},{6,2},{7,11},{8,12},{9,5},{10,... | collective-permute-start | bytes 622088 | tf_op jit(solution)/shard_map/ppermute | solution.py:42
  5.7 0.1 collective-permute-start.8
  5.7 3.0 %collective-permute-start.3 = (bf16[2,18,320]{2,1,0:T(8,128)(2,1)S(1)}, bf16[2,18,320]{2,1,0:T(8,128)(2,1)S(1)}, u32[]{:S(2)}, u32[]{:S(2)}) collective-permute-start(bf16[2,18,320]{2,1,0:T(8,128)(2,1)S(1)} %get-tuple-element.11.pair_ref), channel_id=1, source_target_pairs={{0,8},{1,13},{2,10},{3,15},{4,12},{5,9},{6,14},{7,11},{8,0},{9,5},... | collective-permute-start | bytes 69128 | tf_op jit(solution)/shard_map/ppermute | solution.py:42
  8.7 0.4 %collective-permute-start.7 = (bf16[320,640]{1,0:T(8,128)(2,1)S(1)}, bf16[320,640]{1,0:T(8,128)(2,1)S(1)}, u32[]{:S(2)}, u32[]{:S(2)}) collective-permute-start(bf16[320,640]{1,0:T(8,128)(2,1)S(1)} %copy-done.1), channel_id=1, source_target_pairs={{0,1},{1,0},{2,3},{3,2},{4,5},{5,4},{6,7},{7,6},{8,9},{9,8},{10,11... | collective-permute-start | bytes 1228808 | tf_op jit(solution)/shard_map/ppermute | solution.py:30
  9.1 0.1 collective-permute-start.11
  9.2 3.8 %collective-permute-done.8.near_ref = bf16[288,320]{1,0:T(8,128)(2,1)S(1)} collective-permute-done((bf16[288,320]{1,0:T(8,128)(2,1)S(1)}, bf16[288,320]{1,0:T(8,128)(2,1)S(1)}, u32[]{:S(2)}, u32[]{:S(2)}) %collective-permute-start.8) | collective-permute-done | bytes 184352 | tf_op jit(solution)/shard_map/ppermute | solution.py:42
  13.1 0.5 %collective-permute-start.13 = (bf16[320,640]{1,0:T(8,128)(2,1)S(1)}, bf16[320,640]{1,0:T(8,128)(2,1)S(1)}, u32[]{:S(2)}, u32[]{:S(2)}) collective-permute-start(bf16[320,640]{1,0:T(8,128)(2,1)S(1)} %bitcast.12), channel_id=1, source_target_pairs={{0,1},{1,0},{2,3},{3,2},{4,5},{5,4},{6,7},{7,6},{8,9},{9,8},{10,11... | collective-permute-start | bytes 1228808 | tf_op jit(solution)/shard_map/ppermute | solution.py:30
  13.6 0.1 collective-permute-start.9
  13.7 0.5 %collective-permute-start.10 = (bf16[324,320]{1,0:T(8,128)(2,1)S(1)}, bf16[324,320]{1,0:T(8,128)(2,1)S(1)}, u32[]{:S(2)}, u32[]{:S(2)}) collective-permute-start(bf16[324,320]{1,0:T(8,128)(2,1)S(1)} %collective-permute-done.2.near_ref), channel_id=1, source_target_pairs={{0,1},{1,0},{2,3},{3,2},{4,5},{5,4},{6,7},{7,6},{8,9},{9,8},{10,11... | collective-permute-start | bytes 622088 | tf_op jit(solution)/shard_map/ppermute | solution.py:30
  14.2 1.2 %copy-done = bf16[3,640,640]{2,1,0:T(8,128)(2,1)S(1)} copy-done((bf16[3,640,640]{2,1,0:T(8,128)(2,1)S(1)}, bf16[3,640,640]{2,1,0:T(8,128)(2,1)}, u32[]{:S(2)}) %copy-start) | copy-done | bytes 2457624
  15.4 0.6 %shard_map.85 = (f32[288,640]{1,0:T(8,128)S(1)}, bf16[640,320]{1,0:T(8,128)(2,1)S(1)}) custom-call(bf16[288,320]{1,0:T(8,128)(2,1)S(1)} %bitcast.9, bf16[288,320]{1,0:T(8,128)(2,1)S(1)} %collective-permute-done.clip_other_ref.other_ref, bf16[3,640,640]{2,1,0:T(8,128)(2,1)S(1)} %copy-done, bf16[320,640]{1,0:T(8,128)(2,1)S(1)} %copy-done.1, ...), custom_call_target="tpu_custom_call" | custom-call | flops 500000000 | tf_op jit(solution)/shard_map/pallas_call | solution.py:69
  15.9 2.0 %collective-permute-start.5 = (bf16[4,18,320]{2,1,0:T(8,128)(2,1)S(1)}, bf16[4,18,320]{2,1,0:T(8,128)(2,1)S(1)}, u32[]{:S(2)}, u32[]{:S(2)}) collective-permute-start(bf16[4,18,320]{2,1,0:T(8,128)(2,1)S(1)} %shard_map.84.refs_0_), channel_id=1, source_target_pairs={{0,2},{2,0},{1,3},{3,1},{4,6},{6,4},{5,7},{7,5},{8,10},{10,8},{9,1... | collective-permute-start | bytes 138248 | tf_op jit(solution)/shard_map/ppermute | solution.py:62
  17.9 0.6 %shard_map.86.acc_ref = f32[288,640]{1,0:T(8,128)S(1)} custom-call(f32[288,640]{1,0:T(8,128)S(1)} %get-tuple-element.13.acc_ref, bf16[288,320]{1,0:T(8,128)(2,1)S(1)} %collective-permute-done.8.near_ref, bf16[288,320]{1,0:T(8,128)(2,1)S(1)} %collective-permute-done.9.near_other_ref, bf16[3,640,640]{2,1,0:T(8,128)(2,1)S(1)} %copy-done), custom_call_target="tpu_custom_call" | custom-call | flops 500000000 | tf_op jit(solution)/shard_map/pallas_call | solution.py:69
  18.5 0.0 copy-start.4
  18.5 0.4 %shard_map.87.acc_ref = f32[288,640]{1,0:T(8,128)S(1)} custom-call(f32[288,640]{1,0:T(8,128)S(1)} %shard_map.86.acc_ref, bf16[324,320]{1,0:T(8,128)(2,1)S(1)} %collective-permute-done.2.near_ref, bf16[3,640,640]{2,1,0:T(8,128)(2,1)S(1)} %copy-done), custom_call_target="tpu_custom_call" | custom-call | flops 300000000 | tf_op jit(solution)/shard_map/pallas_call | solution.py:69
  18.9 0.2 collective-permute-start.4
  19.2 1.6 %collective-permute-done.5.refs_2_ = bf16[4,18,320]{2,1,0:T(8,128)(2,1)S(1)} collective-permute-done((bf16[4,18,320]{2,1,0:T(8,128)(2,1)S(1)}, bf16[4,18,320]{2,1,0:T(8,128)(2,1)S(1)}, u32[]{:S(2)}, u32[]{:S(2)}) %collective-permute-start.5) | collective-permute-done | bytes 46112 | tf_op jit(solution)/shard_map/ppermute | solution.py:62
  20.8 1.3 %shard_map.88 = (bf16[288,320]{1,0:T(8,128)(2,1)S(1)}, bf16[640,288]{1,0:T(8,128)(2,1)S(1)}) custom-call(f32[288,640]{1,0:T(8,128)S(1)} %shard_map.87.acc_ref, bf16[324,320]{1,0:T(8,128)(2,1)S(1)} %collective-permute-done.10.near_ref, bf16[3,640,640]{2,1,0:T(8,128)(2,1)S(1)} %copy-done, bf16[320,640]{1,0:T(8,128)(2,1)S(1)} %bitcast.6, ...), custom_call_target="tpu_custom_call" | custom-call | flops 1000000000 | tf_op jit(solution)/shard_map/pallas_call | solution.py:69
  22.2 2.3 %shard_map.89 = bf16[288,320]{1,0:T(8,128)(2,1)} custom-call(bf16[4,18,320]{2,1,0:T(8,128)(2,1)S(1)} %shard_map.84.refs_0_, bf16[4,18,320]{2,1,0:T(8,128)(2,1)S(1)} %collective-permute-done.4.refs_1_, bf16[4,18,320]{2,1,0:T(8,128)(2,1)S(1)} %collective-permute-done.5.refs_2_, bf16[4,18,320]{2,1,0:T(8,128)(2,1)S(1)} %collective-permute-done.6.refs_3_, ...), custom_call_target="tpu_custom_call" | custom-call | flops 2000000000 | tf_op jit(solution)/shard_map/pallas_call | solution.py:69
  (28 shorter events, 0.1 us)
Async XLA Ops:
  0.0 5.7 %copy-start.3 = (bf16[1,6,48,320]{3,2,1,0:T(8,128)(2,1)S(1)}, bf16[1,6,48,320]{3,2,1,0:T(8,128)(2,1)}, u32[]{:S(2)}) copy-start(bf16[1,6,48,320]{3,2,1,0:T(8,128)(2,1)} %param.8) | copy-start | bytes 552964
  0.0 8.7 %copy-start.1 = (bf16[320,640]{1,0:T(8,128)(2,1)S(1)}, bf16[320,640]{1,0:T(8,128)(2,1)}, u32[]{:S(2)}) copy-start(bf16[320,640]{1,0:T(8,128)(2,1)} %wo_own_ref.1) | copy-start | bytes 1228804
  0.0 9.1 %copy-start.2 = (bf16[640,320]{0,1:T(8,128)(2,1)S(1)}, bf16[640,320]{0,1:T(8,128)(2,1)}, u32[]{:S(2)}) copy-start(bf16[640,320]{0,1:T(8,128)(2,1)} %param.11) | copy-start | bytes 1228804
  0.0 13.1 %copy-start.5 = (bf16[640,320]{0,1:T(8,128)(2,1)S(1)}, bf16[640,320]{0,1:T(8,128)(2,1)}, u32[]{:S(2)}) copy-start(bf16[640,320]{0,1:T(8,128)(2,1)} %param.12) | copy-start | bytes 1228804
  0.0 13.1 %copy-start.6 = (bf16[640,320]{0,1:T(8,128)(2,1)S(1)}, bf16[640,320]{0,1:T(8,128)(2,1)}, u32[]{:S(2)}) copy-start(bf16[640,320]{0,1:T(8,128)(2,1)} %param.13) | copy-start | bytes 1228804
  0.0 1.9 %collective-permute-start = (bf16[288,320]{1,0:T(8,128)(2,1)}, bf16[288,320]{1,0:T(8,128)(2,1)S(1)}, u32[]{:S(2)}, u32[]{:S(2)}) collective-permute-start(bf16[288,320]{1,0:T(8,128)(2,1)} %bitcast.7), channel_id=1, source_target_pairs={{0,1},{1,0},{2,3},{3,2},{4,5},{5,4},{6,7},{7,6},{8,9},{9,8},{10,11... | collective-permute-start | bytes 552968 | tf_op jit(solution)/shard_map/ppermute | solution.py:30
  0.5 1.4 %collective-permute-start.1 = (bf16[18,320]{1,0:T(8,128)(2,1)}, bf16[18,320]{1,0:T(8,128)(2,1)S(1)}, u32[]{:S(2)}, u32[]{:S(2)}) collective-permute-start(bf16[18,320]{1,0:T(8,128)(2,1)} %tok_ref.1), channel_id=1, source_target_pairs={{0,1},{1,0},{2,3},{3,2},{4,5},{5,4},{6,7},{7,6},{8,9},{9,8},{10,11... | collective-permute-start | bytes 34568 | tf_op jit(solution)/shard_map/ppermute | solution.py:30
  1.9 0.7 %copy-start.7 = (bf16[18,320]{1,0:T(8,128)(2,1)S(1)}, bf16[18,320]{1,0:T(8,128)(2,1)}, u32[]{:S(2)}) copy-start(bf16[18,320]{1,0:T(8,128)(2,1)} %tok_ref.1) | copy-start | bytes 34564
  2.7 10.9 %collective-permute-start.2 = (bf16[324,320]{1,0:T(8,128)(2,1)S(1)}, bf16[324,320]{1,0:T(8,128)(2,1)S(1)}, u32[]{:S(2)}, u32[]{:S(2)}) collective-permute-start(bf16[324,320]{1,0:T(8,128)(2,1)S(1)} %get-tuple-element.12), channel_id=1, source_target_pairs={{0,4},{1,3},{2,6},{3,1},{4,0},{5,9},{6,2},{7,11},{8,12},{9,5},{10,... | collective-permute-start | bytes 622088 | tf_op jit(solution)/shard_map/ppermute | solution.py:42
  5.7 7.4 %collective-permute-start.8 = (bf16[288,320]{1,0:T(8,128)(2,1)S(1)}, bf16[288,320]{1,0:T(8,128)(2,1)S(1)}, u32[]{:S(2)}, u32[]{:S(2)}) collective-permute-start(bf16[288,320]{1,0:T(8,128)(2,1)S(1)} %bitcast.8), channel_id=1, source_target_pairs={{0,4},{1,3},{2,6},{3,1},{4,0},{5,9},{6,2},{7,11},{8,12},{9,5},{10,... | collective-permute-start | bytes 552968 | tf_op jit(solution)/shard_map/ppermute | solution.py:42
  5.7 7.3 %collective-permute-start.3 = (bf16[2,18,320]{2,1,0:T(8,128)(2,1)S(1)}, bf16[2,18,320]{2,1,0:T(8,128)(2,1)S(1)}, u32[]{:S(2)}, u32[]{:S(2)}) collective-permute-start(bf16[2,18,320]{2,1,0:T(8,128)(2,1)S(1)} %get-tuple-element.11.pair_ref), channel_id=1, source_target_pairs={{0,8},{1,13},{2,10},{3,15},{4,12},{5,9},{6,14},{7,11},{8,0},{9,5},... | collective-permute-start | bytes 69128 | tf_op jit(solution)/shard_map/ppermute | solution.py:42
  8.7 5.0 %collective-permute-start.7 = (bf16[320,640]{1,0:T(8,128)(2,1)S(1)}, bf16[320,640]{1,0:T(8,128)(2,1)S(1)}, u32[]{:S(2)}, u32[]{:S(2)}) collective-permute-start(bf16[320,640]{1,0:T(8,128)(2,1)S(1)} %copy-done.1), channel_id=1, source_target_pairs={{0,1},{1,0},{2,3},{3,2},{4,5},{5,4},{6,7},{7,6},{8,9},{9,8},{10,11... | collective-permute-start | bytes 1228808 | tf_op jit(solution)/shard_map/ppermute | solution.py:30
  9.1 9.9 %collective-permute-start.11 = (bf16[320,640]{1,0:T(8,128)(2,1)S(1)}, bf16[320,640]{1,0:T(8,128)(2,1)S(1)}, u32[]{:S(2)}, u32[]{:S(2)}) collective-permute-start(bf16[320,640]{1,0:T(8,128)(2,1)S(1)} %bitcast.5), channel_id=1, source_target_pairs={{0,1},{1,0},{2,3},{3,2},{4,5},{5,4},{6,7},{7,6},{8,9},{9,8},{10,11... | collective-permute-start | bytes 1228808 | tf_op jit(solution)/shard_map/ppermute | solution.py:30
  13.1 9.1 %collective-permute-start.12 = (bf16[320,640]{1,0:T(8,128)(2,1)S(1)}, bf16[320,640]{1,0:T(8,128)(2,1)S(1)}, u32[]{:S(2)}, u32[]{:S(2)}) collective-permute-start(bf16[320,640]{1,0:T(8,128)(2,1)S(1)} %bitcast.10), channel_id=1, source_target_pairs={{0,1},{1,0},{2,3},{3,2},{4,5},{5,4},{6,7},{7,6},{8,9},{9,8},{10,11... | collective-permute-start | bytes 1228808 | tf_op jit(solution)/shard_map/ppermute | solution.py:30
  13.1 9.1 %collective-permute-start.13 = (bf16[320,640]{1,0:T(8,128)(2,1)S(1)}, bf16[320,640]{1,0:T(8,128)(2,1)S(1)}, u32[]{:S(2)}, u32[]{:S(2)}) collective-permute-start(bf16[320,640]{1,0:T(8,128)(2,1)S(1)} %bitcast.12), channel_id=1, source_target_pairs={{0,1},{1,0},{2,3},{3,2},{4,5},{5,4},{6,7},{7,6},{8,9},{9,8},{10,11... | collective-permute-start | bytes 1228808 | tf_op jit(solution)/shard_map/ppermute | solution.py:30
  13.6 2.4 %collective-permute-start.9 = (bf16[288,320]{1,0:T(8,128)(2,1)S(1)}, bf16[288,320]{1,0:T(8,128)(2,1)S(1)}, u32[]{:S(2)}, u32[]{:S(2)}) collective-permute-start(bf16[288,320]{1,0:T(8,128)(2,1)S(1)} %collective-permute-done.8.near_ref), channel_id=1, source_target_pairs={{0,1},{1,0},{2,3},{3,2},{4,5},{5,4},{6,7},{7,6},{8,9},{9,8},{10,11... | collective-permute-start | bytes 552968 | tf_op jit(solution)/shard_map/ppermute | solution.py:30
  13.7 1.7 %copy-start = (bf16[3,640,640]{2,1,0:T(8,128)(2,1)S(1)}, bf16[3,640,640]{2,1,0:T(8,128)(2,1)}, u32[]{:S(2)}) copy-start(bf16[3,640,640]{2,1,0:T(8,128)(2,1)} %w_ref.7) | copy-start | bytes 7372804
  13.7 7.1 %collective-permute-start.10 = (bf16[324,320]{1,0:T(8,128)(2,1)S(1)}, bf16[324,320]{1,0:T(8,128)(2,1)S(1)}, u32[]{:S(2)}, u32[]{:S(2)}) collective-permute-start(bf16[324,320]{1,0:T(8,128)(2,1)S(1)} %collective-permute-done.2.near_ref), channel_id=1, source_target_pairs={{0,1},{1,0},{2,3},{3,2},{4,5},{5,4},{6,7},{7,6},{8,9},{9,8},{10,11... | collective-permute-start | bytes 622088 | tf_op jit(solution)/shard_map/ppermute | solution.py:30
  15.9 4.9 %collective-permute-start.5 = (bf16[4,18,320]{2,1,0:T(8,128)(2,1)S(1)}, bf16[4,18,320]{2,1,0:T(8,128)(2,1)S(1)}, u32[]{:S(2)}, u32[]{:S(2)}) collective-permute-start(bf16[4,18,320]{2,1,0:T(8,128)(2,1)S(1)} %shard_map.84.refs_0_), channel_id=1, source_target_pairs={{0,2},{2,0},{1,3},{3,1},{4,6},{6,4},{5,7},{7,5},{8,10},{10,8},{9,1... | collective-permute-start | bytes 138248 | tf_op jit(solution)/shard_map/ppermute | solution.py:62
  18.5 2.3 %copy-start.4 = (f32[640]{0:T(1024)S(1)}, f32[640]{0:T(1024)}, u32[]{:S(2)}) copy-start(f32[640]{0:T(1024)} %gain_ref.1) | copy-start | bytes 7684
  18.9 3.2 %collective-permute-start.4 = (bf16[4,18,320]{2,1,0:T(8,128)(2,1)S(1)}, bf16[4,18,320]{2,1,0:T(8,128)(2,1)S(1)}, u32[]{:S(2)}, u32[]{:S(2)}) collective-permute-start(bf16[4,18,320]{2,1,0:T(8,128)(2,1)S(1)} %shard_map.84.refs_0_), channel_id=1, source_target_pairs={{0,1},{1,0},{2,3},{3,2},{4,5},{5,4},{6,7},{7,6},{8,9},{9,8},{10,11... | collective-permute-start | bytes 138248 | tf_op jit(solution)/shard_map/ppermute | solution.py:30
  20.8 1.4 %collective-permute-start.6 = (bf16[4,18,320]{2,1,0:T(8,128)(2,1)S(1)}, bf16[4,18,320]{2,1,0:T(8,128)(2,1)S(1)}, u32[]{:S(2)}, u32[]{:S(2)}) collective-permute-start(bf16[4,18,320]{2,1,0:T(8,128)(2,1)S(1)} %collective-permute-done.5.refs_2_), channel_id=1, source_target_pairs={{0,1},{1,0},{2,3},{3,2},{4,5},{5,4},{6,7},{7,6},{8,9},{9,8},{10,11... | collective-permute-start | bytes 138248 | tf_op jit(solution)/shard_map/ppermute | solution.py:30

commit v3 on v2

v3 whole, which is shorter than its diff:
```python
import functools

import jax
import jax.numpy as jnp
from jax import lax
from jax.experimental import pallas as pl
from jax.experimental.pallas import tpu as pltpu
from jax.sharding import PartitionSpec as P

C = 640
HEADS = 8
EPS = 1e-05

LOAD, JOIN = 10**9, 10**9
MIDDLE, FIRST, SELECT, QUERY, ATTEND = 5 * 10**8, 5 * 10**8, 10**8, 10**9, 2 * 10**9
REST = 5 * 10**9
LATE = 1

F32 = jnp.float32
BF16 = jnp.bfloat16


def nt_dot(a, b):
    return lax.dot_general(a, b, (((1,), (1,)), ((), ())), preferred_element_type=F32)


def tn_dot(a, b):
    return lax.dot_general(a, b, (((0,), (0,)), ((), ())), preferred_element_type=F32)


def sibling(x):
    return lax.ppermute(x, "heads", [(0, 1), (1, 0)])


def swap(x, partner):
    frames, rows = lax.axis_size("frames"), lax.axis_size("rows")
    perm = []
    for frame in range(frames):
        for row in range(rows):
            for core in range(2):
                to = partner(frame, row, core)
                if to is not None:
                    perm.append((((frame * rows) + row) * 2 + core, ((to[0] * rows) + to[1]) * 2 + to[2]))
    return lax.ppermute(x, ("frames", "rows", "heads"), perm)


def swap_near(x):
    frames, rows = lax.axis_size("frames"), lax.axis_size("rows")

    def partner(frame, row, core):
        to = frame + 1 if frame % 2 == core else frame - 1
        if 0 <= to < frames:
            return to, row, core
        return (frame, row ^ 1, core) if rows % 2 == 0 else None

    return swap(x, partner)


def swap_bit(x, axis, bit):
    return lax.ppermute(x, axis, [(i, i ^ bit) for i in range(lax.axis_size(axis))])


VMEM = pl.BlockSpec(memory_space=pltpu.VMEM)


def call(kernel, operands, outs, scratch=(), flops=0):
    return pl.pallas_call(
        kernel,
        out_shape=[jax.ShapeDtypeStruct(shape, dtype) for shape, dtype in outs],
        in_specs=[VMEM] * len(operands),
        out_specs=[VMEM] * len(outs),
        scratch_shapes=list(scratch),
        compiler_params=pltpu.CompilerParams(vmem_limit_bytes=40 * 2**20),
        cost_estimate=pl.CostEstimate(flops=flops, bytes_accessed=0, transcendentals=0),
    )(*operands)


def stack_kernel(*refs):
    at = 0
    for ref in refs[:-1]:
        refs[-1][at : at + ref.shape[0]] = ref[...]
        at += ref.shape[0]


def load_kernel(*refs):
    count = len(refs) // 2
    for source, target in zip(refs[:count], refs[count:]):
        target[...] = source[...]


def load(*operands):
    return call(load_kernel, operands, [(x.shape, x.dtype) for x in operands], flops=LOAD)


def join_kernel(clip_ref, clip_other_ref, tok_ref, tok_other_ref, out_ref, own_ref):
    core = lax.axis_index("heads")
    places, half = clip_ref.shape
    for own, other, rows in ((clip_ref, clip_other_ref, slice(0, places)), (tok_ref, tok_other_ref, slice(places, None))):
        own, other = own[...], other[...]
        out_ref[rows, :half] = jnp.where(core == 0, own, other)
        out_ref[rows, half:] = jnp.where(core == 0, other, own)
    own_ref[...] = out_ref[places:]


def gather_tokens(own, near, near_other):
    frames, rows = lax.axis_size("frames"), lax.axis_size("rows")
    if frames == 4 and rows == 2:
        edge = lambda frame: frame in (0, frames - 1)
        far = swap(own, lambda f, r, c: (f ^ 2, r, c) if c == 0 else (f ^ 3, r, c) if edge(f) else (f, r ^ 1, c))
        across = swap(own, lambda f, r, c: (f ^ (2 if c else 1), r ^ 1, c))
        last = swap(own, lambda f, r, c: (f ^ 3, r ^ 1, c) if edge(f) == (c == 0) else (f, r ^ 1, c))
        shape = (3 * own.shape[0], C)
        (rest,) = call(stack_kernel, (far, across, last), [(shape, BF16)], flops=REST)
        return [(own, "all"), (near, "below"), (near_other, "below"), (rest, "inner"), (sibling(rest), "outer")]
    parts = [own]
    for axis, count in (("frames", frames), ("rows", rows)):
        assert count & (count - 1) == 0
        bit = 1
        while bit < count:
            held = parts[0]
            if len(parts) > 1:
                shape = (2 * held.shape[0], C)
                (held,) = call(stack_kernel, parts, [(shape, BF16)], flops=JOIN)
            parts = [held, swap_bit(held, axis, bit)]
            bit *= 2
    return [(part, "all") for part in parts]


def beside(near_ref, places, core, frames):
    frame = lax.axis_index("frames")
    after = lax.rem(frame, 2) == core
    there = jnp.where(after, frame < frames - 1, frame > 0)
    near = near_ref[:places]
    return jnp.where(there, near, jnp.zeros_like(near)), jnp.where(after, 2, 0)


def middle_kernel(full_ref, w_ref, acc_ref):
    full = full_ref[: acc_ref.shape[0]]
    acc_ref[...] = full.astype(F32) + jnp.dot(full, w_ref[1], preferred_element_type=F32)


def select_kernel(own_ref, other_ref, out_ref):
    core = lax.axis_index("heads")
    half = own_ref.shape[0]
    out_ref[:half] = jnp.where(core == 0, own_ref[:, :half], own_ref[:, half:])
    out_ref[half:] = jnp.where(core == 0, other_ref[:, :half], other_ref[:, half:])


def first_kernel(frames, acc_ref, near_ref, w_ref, sum_ref):
    near, tap = beside(near_ref, acc_ref.shape[0], lax.axis_index("heads"), frames)
    sum_ref[...] = acc_ref[...] + jnp.dot(near, w_ref[tap], preferred_element_type=F32)


def query_kernel(frames, acc_ref, near_ref, w_ref, wq_own_ref, wq_other_ref, gain_ref, temporal_ref, query_ref):
    core = lax.axis_index("heads")
    half = wq_own_ref.shape[0]
    near, tap = beside(near_ref, acc_ref.shape[0], 1 - core, frames)
    temporal = (acc_ref[...] + jnp.dot(near, w_ref[tap], preferred_element_type=F32)).astype(BF16)
    temporal_ref[...] = jnp.where(core == 0, temporal[:, :half], temporal[:, half:])
    feats = temporal.astype(F32)
    centre = jnp.mean(feats, axis=-1, keepdims=True)
    centred = feats - centre
    spread = jnp.mean(centred * centred, axis=-1, keepdims=True)
    normed = (centred * lax.rsqrt(spread + EPS) * gain_ref[...]).astype(BF16)
    scale = (C // HEADS) ** -0.5
    query_ref[:half] = (nt_dot(wq_own_ref[...], normed) * scale).astype(BF16)
    query_ref[half:] = (nt_dot(wq_other_ref[...], normed) * scale).astype(BF16)


def attend_kernel(uses, frames, *refs):
    core = lax.axis_index("heads")
    frame = lax.axis_index("frames")
    blocks, refs = refs[: len(uses)], refs[len(uses) :]
    query_ref, temporal_ref, wk_own_ref, wk_other_ref, wv_own_ref, wv_other_ref, wo_ref = refs[:7]
    out_ref, tokens, keys, values, attended = refs[7:]
    half = wk_own_ref.shape[0]
    size = C // HEADS
    inner = ((frame == 0) | (frame == frames - 1)) == (core == 0)
    at = 0
    for i, use in enumerate(uses):
        found = blocks[i][...]
        if use == "below":
            found = blocks[i][temporal_ref.shape[0] :]
        if use == "inner":
            last = found.shape[0] // 3 * 2
            tokens[at : at + found.shape[0] - last] = jnp.where(inner, found[last:], blocks[i + 1][last:])
            at += found.shape[0] - last
        if use in ("inner", "outer"):
            found = found[:last]
        tokens[at : at + found.shape[0]] = found
        at += found.shape[0]
    toks = tokens[...]
    for part, (wk_ref, wv_ref) in enumerate(((wk_own_ref, wv_own_ref), (wk_other_ref, wv_other_ref))):
        values[part * half : (part + 1) * half] = nt_dot(wv_ref[...], toks).astype(BF16)
        found = nt_dot(toks, wk_ref[...]).astype(BF16)
        for head in range(half // size):
            keys[part * (half // size) + head, :, :size] = found[:, head * size : (head + 1) * size]
    probs = []
    for head in range(HEADS):
        rows = slice(head * size, (head + 1) * size)
        scores = jnp.dot(keys[head, :, :size], query_ref[rows], preferred_element_type=F32)
        expo = jnp.exp(scores - jnp.max(scores, axis=0, keepdims=True))
        probs.append((expo.astype(BF16), 1.0 / jnp.sum(expo, axis=0, keepdims=True)))
    for head in range(HEADS):
        rows = slice(head * size, (head + 1) * size)
        prob, inverse = probs[head]
        mixed = jnp.dot(values[rows], prob, preferred_element_type=F32)
        attended[rows] = (mixed * inverse).astype(BF16)
    mixed = tn_dot(attended[...], wo_ref[...])
    out_ref[...] = (temporal_ref[...].astype(F32) + mixed).astype(BF16)


def body(clip_latent, norm_gain, w_time, w_query, w_key, w_value, w_out, reference_tokens):
    frames_here, rows_here, cols_here, half = clip_latent.shape
    assert frames_here == 1 and lax.axis_size("heads") == 2
    places = rows_here * cols_here
    width = reference_tokens.shape[0]
    clip = clip_latent.reshape(places, half)
    frames = lax.axis_size("frames")
    frames = lax.axis_size("frames")
    clip_other, toks_other = sibling(clip), sibling(reference_tokens)
    clip, toks = load(clip, reference_tokens)
    full, own = call(
        join_kernel,
        (clip, clip_other, toks, toks_other),
        [((places + width, C), BF16), ((width, C), BF16)],
        flops=JOIN,
    )
    near = swap_near(full)
    near_other = sibling(near)
    toks = gather_tokens(own, near, near_other)
    *wide, _ = lax.optimization_barrier((w_query.T, w_key.T, w_value.T, w_out, near if LATE else own))
    wq_other, wk_other, wv_other, wo_other = (sibling(x) for x in wide)
    wq, wk, wv = w_query.T, w_key.T, w_value.T
    (wo,) = call(select_kernel, (w_out, wo_other), [((C, half), BF16)], flops=SELECT)
    (acc,) = call(middle_kernel, (full, w_time), [((places, C), F32)], flops=MIDDLE)
    (acc,) = call(
        functools.partial(first_kernel, frames), (acc, near, w_time), [((places, C), F32)], flops=FIRST
    )
    temporal, query = call(
        functools.partial(query_kernel, frames),
        (acc, near_other, w_time, wq, wq_other, norm_gain),
        [((places, half), BF16), ((C, places), BF16)],
        flops=QUERY,
    )
    count = width * frames * lax.axis_size("rows")
    (out,) = call(
        functools.partial(attend_kernel, [use for _, use in toks], frames),
        (*[x for x, _ in toks], query, temporal, wk, wk_other, wv, wv_other, wo),
        [((places, half), BF16)],
        [
            pltpu.VMEM((count, C), BF16),
            pltpu.VMEM((HEADS, count, 128), BF16),
            pltpu.VMEM((C, count), BF16),
            pltpu.VMEM((C, places), BF16),
        ],
        flops=ATTEND,
    )
    return out.reshape(clip_latent.shape)


def solution(mesh):
    return jax.shard_map(
        body,
        mesh=mesh,
        in_specs=(
            P(("groups", "frames"), "rows", None, "heads"),
            P(),
            P(),
            P(None, "heads"),
            P(None, "heads"),
            P(None, "heads"),
            P("heads", None),
            P(("groups", "frames", "rows"), "heads"),
        ),
        out_specs=P(("groups", "frames"), "rows", None, "heads"),
        check_vma=False,
    )
```

time: 24.9 us -> 21.8 us (0.88)
  waiting for transfers between devices: 6.83 us -> 4.31 us
    ppermute x3 -> x4, starting transfers between devices: 5.99 us -> 8.37 us  [swap(): return lax.ppermute(x, ('frames', 'rows', 'heads'), perm)]
    ppermute x1 -> x0, starting transfers between devices: 2 us -> none  [swap_bit(): lax.ppermute(x, axis, [(i, i ^ bit) for i in range(lax.axis_size(axis))])]
    ppermute x1 -> x0, waiting for transfers between devices: 1.64 us -> none  [swap_bit(): lax.ppermute(x, axis, [(i, i ^ bit) for i in range(lax.axis_size(axis))])]
    ppermute x10 -> x8, waiting for transfers between devices: 1.34 us -> 0.35 us  [sibling(): return lax.ppermute(x, 'heads', [(0, 1), (1, 0)])]
    ppermute x10 -> x8, starting transfers between devices: 2.43 us -> 1.86 us  [sibling(): return lax.ppermute(x, 'heads', [(0, 1), (1, 0)])]
    ppermute x3 -> x4, waiting for transfers between devices: 3.85 us -> 3.96 us  [swap(): return lax.ppermute(x, ('frames', 'rows', 'heads'), perm)]
  transfers between devices with their start and end apart: 14 -> 12, of which waited for: 3 -> 4; matrix products, arithmetic and copies ran while one was open for 0% -> 0% of each run, Pallas kernels for 12% -> 13%
where the time goes in v3:
time: 21.8 us; the launch traced here: 21.6 us
  starting transfers between devices  10.2 us (47%)
  Pallas kernels  5.25 us (24%)
  waiting for transfers between devices  4.31 us (20%)
  local copies, waits for them, and re-layouts  1.69 us (8%)
    ppermute x4, starting transfers between devices, swap(): return lax.ppermute(x, ('frames', 'rows', 'heads'), perm)  8.37 us
    pallas_call x8, Pallas kernels, call(): pl.pallas_call(kernel, out_shape=[jax.ShapeDtypeStruct(shape, dtype) for...  5.25 us
    ppermute x4, waiting for transfers between devices, swap(): return lax.ppermute(x, ('frames', 'rows', 'heads'), perm)  3.96 us
    ppermute x8, starting transfers between devices, sibling(): return lax.ppermute(x, 'heads', [(0, 1), (1, 0)])  1.86 us
    unnamed x16, local copies, waits for them, and re-layouts  1.69 us
  transfers between devices with their start and end apart: 12, of which 4 were waited for; matrix products, arithmetic and copies ran while one was open for 0% of the time, Pallas kernels for 13%

profile of v3, /device:TPU:0, one launch (start us, length us, event | category | flops | bytes accessed | tf_op | source)
XLA Modules:
  0.0 21.6 jit_solution(2150171001372932955)
XLA Ops:
  0.0 0.5 %collective-permute-start = (bf16[288,320]{1,0:T(8,128)(2,1)}, bf16[288,320]{1,0:T(8,128)(2,1)S(1)}, u32[]{:S(2)}, u32[]{:S(2)}) collective-permute-start(bf16[288,320]{1,0:T(8,128)(2,1)} %bitcast.11), channel_id=1, source_target_pairs={{0,1},{1,0},{2,3},{3,2},{4,5},{5,4},{6,7},{7,6},{8,9},{9,8},{10,11... | collective-permute-start | bytes 552968 | tf_op jit(solution)/shard_map/ppermute | solution.py:32
  0.5 0.1 collective-permute-start.1
  0.5 0.9 %copy-done.6 = bf16[1,6,48,320]{3,2,1,0:T(8,128)(2,1)S(1)} copy-done((bf16[1,6,48,320]{3,2,1,0:T(8,128)(2,1)S(1)}, bf16[1,6,48,320]{3,2,1,0:T(8,128)(2,1)}, u32[]{:S(2)}) %copy-start.6) | copy-done | bytes 184344
  1.4 0.7 %copy-done.7 = bf16[18,320]{1,0:T(8,128)(2,1)S(1)} copy-done((bf16[18,320]{1,0:T(8,128)(2,1)S(1)}, bf16[18,320]{1,0:T(8,128)(2,1)}, u32[]{:S(2)}) %copy-start.7) | copy-done | bytes 11544
  2.2 0.0 copy-start
  2.2 0.2 shard_map.83
  2.4 0.0 copy-start.1
  2.5 3.1 %collective-permute-start.2 = (bf16[306,640]{1,0:T(8,128)(2,1)S(1)}, bf16[306,640]{1,0:T(8,128)(2,1)S(1)}, u32[]{:S(2)}, u32[]{:S(2)}) collective-permute-start(bf16[306,640]{1,0:T(8,128)(2,1)S(1)} %get-tuple-element.18.full_ref), channel_id=1, source_target_pairs={{0,4},{1,3},{2,6},{3,1},{4,0},{5,9},{6,2},{7,11},{8,12},{9,5},{10,... | collective-permute-start | bytes 1175048 | tf_op jit(solution)/shard_map/ppermute | solution.py:44
  5.6 2.6 %collective-permute-start.4 = (bf16[18,640]{1,0:T(8,128)(2,1)S(1)}, bf16[18,640]{1,0:T(8,128)(2,1)S(1)}, u32[]{:S(2)}, u32[]{:S(2)}) collective-permute-start(bf16[18,640]{1,0:T(8,128)(2,1)S(1)} %get-tuple-element.17.refs_0_), channel_id=1, source_target_pairs={{0,8},{1,13},{2,10},{3,15},{4,12},{5,7},{6,14},{7,5},{8,0},{9,11},... | collective-permute-start | bytes 69128 | tf_op jit(solution)/shard_map/ppermute | solution.py:44
  8.1 1.4 %collective-permute-start.5 = (bf16[18,640]{1,0:T(8,128)(2,1)S(1)}, bf16[18,640]{1,0:T(8,128)(2,1)S(1)}, u32[]{:S(2)}, u32[]{:S(2)}) collective-permute-start(bf16[18,640]{1,0:T(8,128)(2,1)S(1)} %get-tuple-element.17.refs_0_), channel_id=1, source_target_pairs={{0,6},{1,11},{2,4},{3,9},{4,2},{5,15},{6,0},{7,13},{8,14},{9,3},{1... | collective-permute-start | bytes 69128 | tf_op jit(solution)/shard_map/ppermute | solution.py:44
  9.5 1.3 %collective-permute-start.6 = (bf16[18,640]{1,0:T(8,128)(2,1)S(1)}, bf16[18,640]{1,0:T(8,128)(2,1)S(1)}, u32[]{:S(2)}, u32[]{:S(2)}) collective-permute-start(bf16[18,640]{1,0:T(8,128)(2,1)S(1)} %get-tuple-element.17.refs_0_), channel_id=1, source_target_pairs={{0,14},{1,3},{2,12},{3,1},{4,6},{5,11},{6,4},{7,9},{8,10},{9,7},{1... | collective-permute-start | bytes 69128 | tf_op jit(solution)/shard_map/ppermute | solution.py:44
  10.8 0.5 %shard_map.85.acc_ref = f32[288,640]{1,0:T(8,128)S(1)} custom-call(bf16[306,640]{1,0:T(8,128)(2,1)S(1)} %get-tuple-element.18.full_ref, bf16[3,640,640]{2,1,0:T(8,128)(2,1)S(1)} %copy-done), custom_call_target="tpu_custom_call" | custom-call | flops 500000000 | tf_op jit(solution)/shard_map/pallas_call | solution.py:67
  11.3 0.7 %collective-permute-done.2.near_ref.refs_1_ = bf16[306,640]{1,0:T(8,128)(2,1)S(1)} collective-permute-done((bf16[306,640]{1,0:T(8,128)(2,1)S(1)}, bf16[306,640]{1,0:T(8,128)(2,1)S(1)}, u32[]{:S(2)}, u32[]{:S(2)}) %collective-permute-start.2) | collective-permute-done | bytes 391712 | tf_op jit(solution)/shard_map/ppermute | solution.py:44
  12.0 0.5 %collective-permute-start.11 = (bf16[320,640]{1,0:T(8,128)(2,1)S(1)}, bf16[320,640]{1,0:T(8,128)(2,1)S(1)}, u32[]{:S(2)}, u32[]{:S(2)}) collective-permute-start(bf16[320,640]{1,0:T(8,128)(2,1)S(1)} %copy-done.1), channel_id=1, source_target_pairs={{0,1},{1,0},{2,3},{3,2},{4,5},{5,4},{6,7},{7,6},{8,9},{9,8},{10,11... | collective-permute-start | bytes 1228808 | tf_op jit(solution)/shard_map/ppermute | solution.py:32
  12.6 0.1 collective-permute-start.10
  12.6 1.1 %collective-permute-done.5.refs_1_ = bf16[18,640]{1,0:T(8,128)(2,1)S(1)} collective-permute-done((bf16[18,640]{1,0:T(8,128)(2,1)S(1)}, bf16[18,640]{1,0:T(8,128)(2,1)S(1)}, u32[]{:S(2)}, u32[]{:S(2)}) %collective-permute-start.5) | collective-permute-done | bytes 23072 | tf_op jit(solution)/shard_map/ppermute | solution.py:44
  13.7 0.2 collective-permute-start.9
  13.9 2.2 %collective-permute-done.6.refs_2_ = bf16[18,640]{1,0:T(8,128)(2,1)S(1)} collective-permute-done((bf16[18,640]{1,0:T(8,128)(2,1)S(1)}, bf16[18,640]{1,0:T(8,128)(2,1)S(1)}, u32[]{:S(2)}, u32[]{:S(2)}) %collective-permute-start.6) | collective-permute-done | bytes 23072 | tf_op jit(solution)/shard_map/ppermute | solution.py:44
  16.1 0.5 %shard_map.86.acc_ref = f32[288,640]{1,0:T(8,128)S(1)} custom-call(f32[288,640]{1,0:T(8,128)S(1)} %shard_map.85.acc_ref, bf16[306,640]{1,0:T(8,128)(2,1)S(1)} %collective-permute-done.2.near_ref.refs_1_, bf16[3,640,640]{2,1,0:T(8,128)(2,1)S(1)} %copy-done), custom_call_target="tpu_custom_call" | custom-call | flops 500000000 | tf_op jit(solution)/shard_map/pallas_call | solution.py:67
  16.7 0.6 %collective-permute-start.7 = (bf16[54,640]{1,0:T(8,128)(2,1)S(1)}, bf16[54,640]{1,0:T(8,128)(2,1)S(1)}, u32[]{:S(2)}, u32[]{:S(2)}) collective-permute-start(bf16[54,640]{1,0:T(8,128)(2,1)S(1)} %shard_map.84.refs_3_), channel_id=1, source_target_pairs={{0,1},{1,0},{2,3},{3,2},{4,5},{5,4},{6,7},{7,6},{8,9},{9,8},{10,11... | collective-permute-start | bytes 207368 | tf_op jit(solution)/shard_map/ppermute | solution.py:32
  17.3 0.2 %shard_map.88.refs_11_ = bf16[640,320]{1,0:T(8,128)(2,1)S(1)} custom-call(bf16[320,640]{1,0:T(8,128)(2,1)S(1)} %copy-done.1, bf16[320,640]{1,0:T(8,128)(2,1)S(1)} %collective-permute-done.11.other_ref), custom_call_target="tpu_custom_call" | custom-call | flops 100000000 | tf_op jit(solution)/shard_map/pallas_call | solution.py:67
  17.5 0.3 %collective-permute-done.3.near_ref.refs_2_ = bf16[306,640]{1,0:T(8,128)(2,1)S(1)} collective-permute-done((bf16[306,640]{1,0:T(8,128)(2,1)S(1)}, bf16[306,640]{1,0:T(8,128)(2,1)S(1)}, u32[]{:S(2)}, u32[]{:S(2)}) %collective-permute-start.3) | collective-permute-done | bytes 391712 | tf_op jit(solution)/shard_map/ppermute | solution.py:32
  17.8 1.4 %shard_map.87 = (bf16[288,320]{1,0:T(8,128)(2,1)S(1)}, bf16[640,288]{1,0:T(8,128)(2,1)S(1)}) custom-call(f32[288,640]{1,0:T(8,128)S(1)} %shard_map.86.acc_ref, bf16[306,640]{1,0:T(8,128)(2,1)S(1)} %collective-permute-done.3.near_ref.refs_2_, bf16[3,640,640]{2,1,0:T(8,128)(2,1)S(1)} %copy-done, bf16[320,640]{1,0:T(8,128)(2,1)S(1)} %bitcast.6, ...), custom_call_target="tpu_custom_call" | custom-call | flops 1000000000 | tf_op jit(solution)/shard_map/pallas_call | solution.py:67
  19.3 2.3 %shard_map.89 = bf16[288,320]{1,0:T(8,128)(2,1)} custom-call(bf16[18,640]{1,0:T(8,128)(2,1)S(1)} %get-tuple-element.17.refs_0_, bf16[306,640]{1,0:T(8,128)(2,1)S(1)} %collective-permute-done.2.near_ref.refs_1_, bf16[306,640]{1,0:T(8,128)(2,1)S(1)} %collective-permute-done.3.near_ref.refs_2_, bf16[54,640]{1,0:T(8,128)(2,1)S(1)} %shard_map.84.refs_3_, ...), custom_call_target="tpu_custom_call" | custom-call | flops 2000000000 | tf_op jit(solution)/shard_map/pallas_call | solution.py:67
  (24 shorter events, 0.1 us)
Async XLA Ops:
  0.0 2.2 %collective-permute-start = (bf16[288,320]{1,0:T(8,128)(2,1)}, bf16[288,320]{1,0:T(8,128)(2,1)S(1)}, u32[]{:S(2)}, u32[]{:S(2)}) collective-permute-start(bf16[288,320]{1,0:T(8,128)(2,1)} %bitcast.11), channel_id=1, source_target_pairs={{0,1},{1,0},{2,3},{3,2},{4,5},{5,4},{6,7},{7,6},{8,9},{9,8},{10,11... | collective-permute-start | bytes 552968 | tf_op jit(solution)/shard_map/ppermute | solution.py:32
  0.5 1.8 %collective-permute-start.1 = (bf16[18,320]{1,0:T(8,128)(2,1)}, bf16[18,320]{1,0:T(8,128)(2,1)S(1)}, u32[]{:S(2)}, u32[]{:S(2)}) collective-permute-start(bf16[18,320]{1,0:T(8,128)(2,1)} %refs_1_.1), channel_id=1, source_target_pairs={{0,1},{1,0},{2,3},{3,2},{4,5},{5,4},{6,7},{7,6},{8,9},{9,8},{10,11... | collective-permute-start | bytes 34568 | tf_op jit(solution)/shard_map/ppermute | solution.py:32
  0.5 0.9 %copy-start.6 = (bf16[1,6,48,320]{3,2,1,0:T(8,128)(2,1)S(1)}, bf16[1,6,48,320]{3,2,1,0:T(8,128)(2,1)}, u32[]{:S(2)}) copy-start(bf16[1,6,48,320]{3,2,1,0:T(8,128)(2,1)} %param.8) | copy-start | bytes 552964
  1.4 0.7 %copy-start.7 = (bf16[18,320]{1,0:T(8,128)(2,1)S(1)}, bf16[18,320]{1,0:T(8,128)(2,1)}, u32[]{:S(2)}) copy-start(bf16[18,320]{1,0:T(8,128)(2,1)} %refs_1_.1) | copy-start | bytes 34564
  2.2 8.6 %copy-start = (bf16[3,640,640]{2,1,0:T(8,128)(2,1)S(1)}, bf16[3,640,640]{2,1,0:T(8,128)(2,1)}, u32[]{:S(2)}) copy-start(bf16[3,640,640]{2,1,0:T(8,128)(2,1)} %w_ref.5) | copy-start | bytes 7372804
  2.4 9.6 %copy-start.2 = (bf16[640,320]{0,1:T(8,128)(2,1)S(1)}, bf16[640,320]{0,1:T(8,128)(2,1)}, u32[]{:S(2)}) copy-start(bf16[640,320]{0,1:T(8,128)(2,1)} %param.11) | copy-start | bytes 1228804
  2.4 9.6 %copy-start.1 = (bf16[320,640]{1,0:T(8,128)(2,1)S(1)}, bf16[320,640]{1,0:T(8,128)(2,1)}, u32[]{:S(2)}) copy-start(bf16[320,640]{1,0:T(8,128)(2,1)} %own_ref.1) | copy-start | bytes 1228804
  2.4 10.1 %copy-start.5 = (bf16[640,320]{0,1:T(8,128)(2,1)S(1)}, bf16[640,320]{0,1:T(8,128)(2,1)}, u32[]{:S(2)}) copy-start(bf16[640,320]{0,1:T(8,128)(2,1)} %param.13) | copy-start | bytes 1228804
  2.5 11.3 %copy-start.4 = (bf16[640,320]{0,1:T(8,128)(2,1)S(1)}, bf16[640,320]{0,1:T(8,128)(2,1)}, u32[]{:S(2)}) copy-start(bf16[640,320]{0,1:T(8,128)(2,1)} %param.12) | copy-start | bytes 1228804
  2.5 9.6 %collective-permute-start.2 = (bf16[306,640]{1,0:T(8,128)(2,1)S(1)}, bf16[306,640]{1,0:T(8,128)(2,1)S(1)}, u32[]{:S(2)}, u32[]{:S(2)}) collective-permute-start(bf16[306,640]{1,0:T(8,128)(2,1)S(1)} %get-tuple-element.18.full_ref), channel_id=1, source_target_pairs={{0,4},{1,3},{2,6},{3,1},{4,0},{5,9},{6,2},{7,11},{8,12},{9,5},{10,... | collective-permute-start | bytes 1175048 | tf_op jit(solution)/shard_map/ppermute | solution.py:44
  5.6 7.0 %collective-permute-start.4 = (bf16[18,640]{1,0:T(8,128)(2,1)S(1)}, bf16[18,640]{1,0:T(8,128)(2,1)S(1)}, u32[]{:S(2)}, u32[]{:S(2)}) collective-permute-start(bf16[18,640]{1,0:T(8,128)(2,1)S(1)} %get-tuple-element.17.refs_0_), channel_id=1, source_target_pairs={{0,8},{1,13},{2,10},{3,15},{4,12},{5,7},{6,14},{7,5},{8,0},{9,11},... | collective-permute-start | bytes 69128 | tf_op jit(solution)/shard_map/ppermute | solution.py:44
  8.1 5.6 %collective-permute-start.5 = (bf16[18,640]{1,0:T(8,128)(2,1)S(1)}, bf16[18,640]{1,0:T(8,128)(2,1)S(1)}, u32[]{:S(2)}, u32[]{:S(2)}) collective-permute-start(bf16[18,640]{1,0:T(8,128)(2,1)S(1)} %get-tuple-element.17.refs_0_), channel_id=1, source_target_pairs={{0,6},{1,11},{2,4},{3,9},{4,2},{5,15},{6,0},{7,13},{8,14},{9,3},{1... | collective-permute-start | bytes 69128 | tf_op jit(solution)/shard_map/ppermute | solution.py:44
  9.5 6.6 %collective-permute-start.6 = (bf16[18,640]{1,0:T(8,128)(2,1)S(1)}, bf16[18,640]{1,0:T(8,128)(2,1)S(1)}, u32[]{:S(2)}, u32[]{:S(2)}) collective-permute-start(bf16[18,640]{1,0:T(8,128)(2,1)S(1)} %get-tuple-element.17.refs_0_), channel_id=1, source_target_pairs={{0,14},{1,3},{2,12},{3,1},{4,6},{5,11},{6,4},{7,9},{8,10},{9,7},{1... | collective-permute-start | bytes 69128 | tf_op jit(solution)/shard_map/ppermute | solution.py:44
  12.0 5.8 %collective-permute-start.8 = (bf16[320,640]{1,0:T(8,128)(2,1)S(1)}, bf16[320,640]{1,0:T(8,128)(2,1)S(1)}, u32[]{:S(2)}, u32[]{:S(2)}) collective-permute-start(bf16[320,640]{1,0:T(8,128)(2,1)S(1)} %bitcast.5), channel_id=1, source_target_pairs={{0,1},{1,0},{2,3},{3,2},{4,5},{5,4},{6,7},{7,6},{8,9},{9,8},{10,11... | collective-permute-start | bytes 1228808 | tf_op jit(solution)/shard_map/ppermute | solution.py:32
  12.0 4.7 %collective-permute-start.11 = (bf16[320,640]{1,0:T(8,128)(2,1)S(1)}, bf16[320,640]{1,0:T(8,128)(2,1)S(1)}, u32[]{:S(2)}, u32[]{:S(2)}) collective-permute-start(bf16[320,640]{1,0:T(8,128)(2,1)S(1)} %copy-done.1), channel_id=1, source_target_pairs={{0,1},{1,0},{2,3},{3,2},{4,5},{5,4},{6,7},{7,6},{8,9},{9,8},{10,11... | collective-permute-start | bytes 1228808 | tf_op jit(solution)/shard_map/ppermute | solution.py:32
  12.6 6.7 %collective-permute-start.10 = (bf16[320,640]{1,0:T(8,128)(2,1)S(1)}, bf16[320,640]{1,0:T(8,128)(2,1)S(1)}, u32[]{:S(2)}, u32[]{:S(2)}) collective-permute-start(bf16[320,640]{1,0:T(8,128)(2,1)S(1)} %bitcast.9), channel_id=1, source_target_pairs={{0,1},{1,0},{2,3},{3,2},{4,5},{5,4},{6,7},{7,6},{8,9},{9,8},{10,11... | collective-permute-start | bytes 1228808 | tf_op jit(solution)/shard_map/ppermute | solution.py:32
  13.7 5.6 %collective-permute-start.9 = (bf16[320,640]{1,0:T(8,128)(2,1)S(1)}, bf16[320,640]{1,0:T(8,128)(2,1)S(1)}, u32[]{:S(2)}, u32[]{:S(2)}) collective-permute-start(bf16[320,640]{1,0:T(8,128)(2,1)S(1)} %bitcast.7), channel_id=1, source_target_pairs={{0,1},{1,0},{2,3},{3,2},{4,5},{5,4},{6,7},{7,6},{8,9},{9,8},{10,11... | collective-permute-start | bytes 1228808 | tf_op jit(solution)/shard_map/ppermute | solution.py:32
  16.1 1.7 %collective-permute-start.3 = (bf16[306,640]{1,0:T(8,128)(2,1)S(1)}, bf16[306,640]{1,0:T(8,128)(2,1)S(1)}, u32[]{:S(2)}, u32[]{:S(2)}) collective-permute-start(bf16[306,640]{1,0:T(8,128)(2,1)S(1)} %collective-permute-done.2.near_ref.refs_1_), channel_id=1, source_target_pairs={{0,1},{1,0},{2,3},{3,2},{4,5},{5,4},{6,7},{7,6},{8,9},{9,8},{10,11... | collective-permute-start | bytes 1175048 | tf_op jit(solution)/shard_map/ppermute | solution.py:32
  16.1 1.7 %copy-start.3 = (f32[640]{0:T(1024)S(1)}, f32[640]{0:T(1024)}, u32[]{:S(2)}) copy-start(f32[640]{0:T(1024)} %gain_ref.1) | copy-start | bytes 7684
  16.7 2.6 %collective-permute-start.7 = (bf16[54,640]{1,0:T(8,128)(2,1)S(1)}, bf16[54,640]{1,0:T(8,128)(2,1)S(1)}, u32[]{:S(2)}, u32[]{:S(2)}) collective-permute-start(bf16[54,640]{1,0:T(8,128)(2,1)S(1)} %shard_map.84.refs_3_), channel_id=1, source_target_pairs={{0,1},{1,0},{2,3},{3,2},{4,5},{5,4},{6,7},{7,6},{8,9},{9,8},{10,11... | collective-permute-start | bytes 207368 | tf_op jit(solution)/shard_map/ppermute | solution.py:32

commit v4 on v3

v4 whole, which is shorter than its diff:
```python
import functools

import jax
import jax.numpy as jnp
from jax import lax
from jax.experimental import pallas as pl
from jax.experimental.pallas import tpu as pltpu
from jax.sharding import PartitionSpec as P

C = 640
HEADS = 8
EPS = 1e-05

JOIN = 10 * 10**9
MIDDLE = 5 * 10**8
FIRST = 5 * 10**8
QUERY = 10**9
ATTEND = 2 * 10**9
WEIGHTS = 10**8
REST = 30 * 10**9

F32 = jnp.float32
BF16 = jnp.bfloat16


def nt_dot(a, b):
    return lax.dot_general(a, b, (((1,), (1,)), ((), ())), preferred_element_type=F32)


def tn_dot(a, b):
    return lax.dot_general(a, b, (((0,), (0,)), ((), ())), preferred_element_type=F32)


def sibling(x):
    return lax.ppermute(x, "heads", [(0, 1), (1, 0)])


def swap(x, partner):
    frames, rows = lax.axis_size("frames"), lax.axis_size("rows")
    perm = []
    for frame in range(frames):
        for row in range(rows):
            for core in range(2):
                to = partner(frame, row, core)
                if to is not None:
                    perm.append((((frame * rows) + row) * 2 + core, ((to[0] * rows) + to[1]) * 2 + to[2]))
    return lax.ppermute(x, ("frames", "rows", "heads"), perm)


def swap_frames(x, parity):
    frames, rows = lax.axis_size("frames"), lax.axis_size("rows")

    def partner(frame, row, core):
        to = frame + 1 if frame % 2 == parity else frame - 1
        if 0 <= to < frames:
            return to, row, core
        return (frame, row ^ 1, core) if rows % 2 == 0 else None

    return swap(x, partner)


def swap_bit(x, axis, bit):
    return lax.ppermute(x, axis, [(i, i ^ bit) for i in range(lax.axis_size(axis))])


VMEM = pl.BlockSpec(memory_space=pltpu.VMEM)


def call(kernel, operands, outs, scratch=(), flops=0):
    return pl.pallas_call(
        kernel,
        out_shape=[jax.ShapeDtypeStruct(shape, dtype) for shape, dtype in outs],
        in_specs=[VMEM] * len(operands),
        out_specs=[VMEM] * len(outs),
        scratch_shapes=list(scratch),
        compiler_params=pltpu.CompilerParams(vmem_limit_bytes=40 * 2**20),
        cost_estimate=pl.CostEstimate(flops=flops, bytes_accessed=0, transcendentals=0),
    )(*operands)


def stack_kernel(*refs):
    at = 0
    for ref in refs[:-1]:
        refs[-1][at : at + ref.shape[0]] = ref[...]
        at += ref.shape[0]


def join_kernel(own_ref, other_ref, out_ref):
    core = lax.axis_index("heads")
    half = own_ref.shape[1]
    own, other = own_ref[...], other_ref[...]
    out_ref[:, :half] = jnp.where(core == 0, own, other)
    out_ref[:, half:] = jnp.where(core == 0, other, own)


def gather_tokens(own):
    frames, rows = lax.axis_size("frames"), lax.axis_size("rows")
    if frames == 4 and rows == 2:
        far = [swap(own, lambda f, r, c, d=d: (f ^ d, r ^ c, c)) for d in (3, 2, 1)]
        (rest,) = call(stack_kernel, far, [((3 * own.shape[0], C), BF16)], flops=REST)
        return [own, swap_bit(own, "rows", 1)], [rest]
    parts = [own]
    for axis, count in (("frames", frames), ("rows", rows)):
        assert count & (count - 1) == 0
        bit = 1
        while bit < count:
            held = parts[0]
            if len(parts) > 1:
                shape = (2 * held.shape[0], C)
                (held,) = call(stack_kernel, parts, [(shape, BF16)], flops=JOIN)
            parts = [held, swap_bit(held, axis, bit)]
            bit *= 2
    return parts, []


def halves(core, half):
    own = pl.multiple_of(core * half, 16)
    return pl.ds(own, half), pl.ds(pl.multiple_of(half - own, 16), half)


def beside(refs, w_ref, channels, frames):
    frame = lax.axis_index("frames")
    terms = None
    for parity, ref in enumerate(refs):
        after = lax.rem(frame, 2) == parity
        there = jnp.where(after, frame < frames - 1, frame > 0)
        near = ref[...]
        near = jnp.where(there, near, jnp.zeros_like(near))
        term = jnp.dot(near, w_ref[jnp.where(after, 2, 0), channels], preferred_element_type=F32)
        terms = term if terms is None else terms + term
    return terms


def middle_kernel(own_ref, other_ref, w_ref, acc_ref, full):
    join_kernel(own_ref, other_ref, full)
    whole = full[...]
    acc_ref[...] = whole.astype(F32) + jnp.dot(whole, w_ref[1], preferred_element_type=F32)


def weights_kernel(*refs):
    for i, ref in enumerate(refs[:-1]):
        refs[-1][i] = ref[...]


def first_kernel(frames, acc_ref, even_ref, odd_ref, w_ref, sum_ref):
    own = halves(lax.axis_index("heads"), even_ref.shape[1])[0]
    sum_ref[...] = acc_ref[...] + beside((even_ref, odd_ref), w_ref, own, frames)


def query_kernel(frames, acc_ref, even_ref, odd_ref, w_ref, held_ref, met_ref, gain_ref, temporal_ref, query_ref):
    core = lax.axis_index("heads")
    half = held_ref.shape[1]
    other = halves(core, half)[1]
    temporal = (acc_ref[...] + beside((even_ref, odd_ref), w_ref, other, frames)).astype(BF16)
    temporal_ref[...] = jnp.where(core == 0, temporal[:, :half], temporal[:, half:])
    feats = temporal.astype(F32)
    centre = jnp.mean(feats, axis=-1, keepdims=True)
    centred = feats - centre
    spread = jnp.mean(centred * centred, axis=-1, keepdims=True)
    normed = (centred * lax.rsqrt(spread + EPS) * gain_ref[...]).astype(BF16)
    scale = (C // HEADS) ** -0.5
    query_ref[:half] = (nt_dot(held_ref[0], normed) * scale).astype(BF16)
    query_ref[half:] = (nt_dot(met_ref[0], normed) * scale).astype(BF16)


def attend_kernel(parts, *refs):
    core = lax.axis_index("heads")
    blocks, refs = refs[:parts], refs[parts:]
    query_ref, temporal_ref, held_ref, met_ref, out_ref, tokens, keys, values, attended, out_weights = refs
    half = held_ref.shape[1]
    size = C // HEADS
    at = 0
    for ref in blocks:
        tokens[at : at + ref.shape[0]] = ref[...]
        at += ref.shape[0]
    toks = tokens[...]
    for part, w_ref in enumerate((held_ref, met_ref)):
        out_weights[part * half : (part + 1) * half] = jnp.where(core == 0, w_ref[3, :, :half], w_ref[3, :, half:])
        values[part * half : (part + 1) * half] = nt_dot(w_ref[2], toks).astype(BF16)
        found = nt_dot(toks, w_ref[1]).astype(BF16)
        for head in range(half // size):
            keys[part * (half // size) + head, :, :size] = found[:, head * size : (head + 1) * size]
    probs = []
    for head in range(HEADS):
        rows = slice(head * size, (head + 1) * size)
        scores = jnp.dot(keys[head, :, :size], query_ref[rows], preferred_element_type=F32)
        expo = jnp.exp(scores - jnp.max(scores, axis=0, keepdims=True))
        probs.append((expo.astype(BF16), 1.0 / jnp.sum(expo, axis=0, keepdims=True)))
    for head in range(HEADS):
        rows = slice(head * size, (head + 1) * size)
        prob, inverse = probs[head]
        mixed = jnp.dot(values[rows], prob, preferred_element_type=F32)
        attended[rows] = (mixed * inverse).astype(BF16)
    mixed = tn_dot(attended[...], out_weights[...])
    out_ref[...] = (temporal_ref[...].astype(F32) + mixed).astype(BF16)


def body(clip_latent, norm_gain, w_time, w_query, w_key, w_value, w_out, reference_tokens):
    frames_here, rows_here, cols_here, half = clip_latent.shape
    assert frames_here == 1 and lax.axis_size("heads") == 2
    places = rows_here * cols_here
    width = reference_tokens.shape[0]
    clip = clip_latent.reshape(places, half)
    frames = lax.axis_size("frames")
    frames = lax.axis_size("frames")
    clip_other, toks_other = sibling(clip), sibling(reference_tokens)
    clip_other, toks_other = lax.optimization_barrier((clip_other, toks_other))
    even, odd = swap_frames(clip, 0), swap_frames(clip, 1)
    even_other, odd_other = sibling(even), sibling(odd)
    (own,) = call(join_kernel, (reference_tokens, toks_other), [((width, C), BF16)], flops=JOIN)
    toks, rest = gather_tokens(own)
    (acc,) = call(
        middle_kernel,
        (clip, clip_other, w_time),
        [((places, C), F32)],
        [pltpu.VMEM((places, C), BF16)],
        flops=MIDDLE,
    )
    *wide, _ = lax.optimization_barrier((w_query.T, w_key.T, w_value.T, w_out, acc))
    (held,) = call(weights_kernel, wide, [((4,) + w_out.shape, BF16)], flops=WEIGHTS)
    met = sibling(held)
    (acc,) = call(
        functools.partial(first_kernel, frames), (acc, even, odd, w_time), [((places, C), F32)], flops=FIRST
    )
    temporal, query = call(
        functools.partial(query_kernel, frames),
        (acc, even_other, odd_other, w_time, held, met, norm_gain),
        [((places, half), BF16), ((C, places), BF16)],
        flops=QUERY,
    )
    for part in rest:
        toks += [part, sibling(part)]
    count = width * frames * lax.axis_size("rows")
    (out,) = call(
        functools.partial(attend_kernel, len(toks)),
        (*toks, query, temporal, held, met),
        [((places, half), BF16)],
        [
            pltpu.VMEM((count, C), BF16),
            pltpu.VMEM((HEADS, count, 128), BF16),
            pltpu.VMEM((C, count), BF16),
            pltpu.VMEM((C, places), BF16),
            pltpu.VMEM((C, half), BF16),
        ],
        flops=ATTEND,
    )
    return out.reshape(clip_latent.shape)


def solution(mesh):
    return jax.shard_map(
        body,
        mesh=mesh,
        in_specs=(
            P(("groups", "frames"), "rows", None, "heads"),
            P(),
            P(),
            P(None, "heads"),
            P(None, "heads"),
            P(None, "heads"),
            P("heads", None),
            P(("groups", "frames", "rows"), "heads"),
        ),
        out_specs=P(("groups", "frames"), "rows", None, "heads"),
        check_vma=False,
    )
```

time: 21.8 us -> 19.9 us (0.913)
  waiting for transfers between devices: 4.31 us -> 2.62 us
  local copies, waits for them, and re-layouts: 1.69 us -> 0.75 us
  starting transfers between devices: 10.2 us -> 11 us
    ppermute x4 -> x5, waiting for transfers between devices: 3.96 us -> 1.73 us  [swap(): return lax.ppermute(x, ('frames', 'rows', 'heads'), perm)]
    unnamed x16, local copies, waits for them, and re-layouts: 1.69 us -> 0.75 us
    ppermute x0 -> x1, starting transfers between devices: none -> 0.6 us  [swap_bit(): lax.ppermute(x, axis, [(i, i ^ bit) for i in range(lax.axis_size(axis))])]
    ppermute x4 -> x5, starting transfers between devices: 8.37 us -> 8.96 us  [swap(): return lax.ppermute(x, ('frames', 'rows', 'heads'), perm)]
    ppermute x8 -> x6, waiting for transfers between devices: 0.35 us -> 0.89 us  [sibling(): return lax.ppermute(x, 'heads', [(0, 1), (1, 0)])]
    ppermute x8 -> x6, starting transfers between devices: 1.86 us -> 1.46 us  [sibling(): return lax.ppermute(x, 'heads', [(0, 1), (1, 0)])]
    pallas_call x8 -> x7, Pallas kernels: 5.25 us -> 5.23 us  [call(): pl.pallas_call(kernel, out_shape=[jax.ShapeDtypeStruct(shape, dtype) for...]
  transfers between devices with their start and end apart: 12 -> 12, of which waited for: 4 -> 4; matrix products, arithmetic and copies ran while one was open for 0% -> 0% of each run, Pallas kernels for 13% -> 14%
where the time goes in v4:
time: 19.9 us; the launch traced here: 19.8 us
  starting transfers between devices  11 us (55%)
  Pallas kernels  5.23 us (26%)
  waiting for transfers between devices  2.62 us (13%)
  local copies, waits for them, and re-layouts  0.75 us (4%)
    ppermute x5, starting transfers between devices, swap(): return lax.ppermute(x, ('frames', 'rows', 'heads'), perm)  8.96 us
    pallas_call x7, Pallas kernels, call(): pl.pallas_call(kernel, out_shape=[jax.ShapeDtypeStruct(shape, dtype) for...  5.23 us
    ppermute x5, waiting for transfers between devices, swap(): return lax.ppermute(x, ('frames', 'rows', 'heads'), perm)  1.73 us
    ppermute x6, starting transfers between devices, sibling(): return lax.ppermute(x, 'heads', [(0, 1), (1, 0)])  1.46 us
    ppermute x6, waiting for transfers between devices, sibling(): return lax.ppermute(x, 'heads', [(0, 1), (1, 0)])  0.89 us
    unnamed x16, local copies, waits for them, and re-layouts  0.75 us
    ppermute x1, starting transfers between devices, swap_bit(): lax.ppermute(x, axis, [(i, i ^ bit) for i in range(lax.axis_size(axis))])  0.6 us
  transfers between devices with their start and end apart: 12, of which 4 were waited for; matrix products, arithmetic and copies ran while one was open for 0% of the time, Pallas kernels for 14%

profile of v4, /device:TPU:0, one launch (start us, length us, event | category | flops | bytes accessed | tf_op | source)
XLA Modules:
  0.0 19.8 jit_solution(16291436792191575777)
XLA Ops:
  0.0 0.5 %collective-permute-start = (bf16[288,320]{1,0:T(8,128)(2,1)}, bf16[288,320]{1,0:T(8,128)(2,1)S(1)}, u32[]{:S(2)}, u32[]{:S(2)}) collective-permute-start(bf16[288,320]{1,0:T(8,128)(2,1)} %bitcast.8), channel_id=1, source_target_pairs={{0,1},{1,0},{2,3},{3,2},{4,5},{5,4},{6,7},{7,6},{8,9},{9,8},{10,11... | collective-permute-start | bytes 552968 | tf_op jit(solution)/shard_map/ppermute | solution.py:35
  0.5 0.1 collective-permute-start.1
  0.5 3.0 %collective-permute-start.7 = (bf16[288,320]{1,0:T(8,128)(2,1)}, bf16[288,320]{1,0:T(8,128)(2,1)S(1)}, u32[]{:S(2)}, u32[]{:S(2)}) collective-permute-start(bf16[288,320]{1,0:T(8,128)(2,1)} %bitcast.9), channel_id=1, source_target_pairs={{0,4},{1,5},{2,6},{3,7},{4,0},{5,1},{6,2},{7,3},{8,12},{9,13},{10,... | collective-permute-start | bytes 552968 | tf_op jit(solution)/shard_map/ppermute | solution.py:47
  3.5 1.5 %collective-permute-start.8 = (bf16[288,320]{1,0:T(8,128)(2,1)}, bf16[288,320]{1,0:T(8,128)(2,1)S(1)}, u32[]{:S(2)}, u32[]{:S(2)}) collective-permute-start(bf16[288,320]{1,0:T(8,128)(2,1)} %bitcast.10), channel_id=1, source_target_pairs={{0,2},{1,3},{2,0},{3,1},{4,8},{5,9},{6,10},{7,11},{8,4},{9,5},{10,... | collective-permute-start | bytes 552968 | tf_op jit(solution)/shard_map/ppermute | solution.py:47
  5.0 0.7 %copy-done.7 = bf16[18,320]{1,0:T(8,128)(2,1)S(1)} copy-done((bf16[18,320]{1,0:T(8,128)(2,1)S(1)}, bf16[18,320]{1,0:T(8,128)(2,1)}, u32[]{:S(2)}) %copy-start.7) | copy-done | bytes 11544
  5.8 0.1 shard_map.82.refs_0_
  5.9 0.0 copy-start.4
  5.9 2.5 %collective-permute-start.3 = (bf16[18,640]{1,0:T(8,128)(2,1)S(1)}, bf16[18,640]{1,0:T(8,128)(2,1)S(1)}, u32[]{:S(2)}, u32[]{:S(2)}) collective-permute-start(bf16[18,640]{1,0:T(8,128)(2,1)S(1)} %shard_map.82.refs_0_), channel_id=1, source_target_pairs={{0,12},{1,15},{2,14},{3,13},{4,8},{5,11},{6,10},{7,9},{8,4},{9,7},... | collective-permute-start | bytes 69128 | tf_op jit(solution)/shard_map/ppermute | solution.py:47
  8.4 0.6 %collective-permute-start.4 = (bf16[18,640]{1,0:T(8,128)(2,1)S(1)}, bf16[18,640]{1,0:T(8,128)(2,1)S(1)}, u32[]{:S(2)}, u32[]{:S(2)}) collective-permute-start(bf16[18,640]{1,0:T(8,128)(2,1)S(1)} %shard_map.82.refs_0_), channel_id=1, source_target_pairs={{0,8},{1,11},{2,10},{3,9},{4,12},{5,15},{6,14},{7,13},{8,0},{9,3},... | collective-permute-start | bytes 69128 | tf_op jit(solution)/shard_map/ppermute | solution.py:47
  9.1 1.3 %collective-permute-start.5 = (bf16[18,640]{1,0:T(8,128)(2,1)S(1)}, bf16[18,640]{1,0:T(8,128)(2,1)S(1)}, u32[]{:S(2)}, u32[]{:S(2)}) collective-permute-start(bf16[18,640]{1,0:T(8,128)(2,1)S(1)} %shard_map.82.refs_0_), channel_id=1, source_target_pairs={{0,4},{1,7},{2,6},{3,5},{4,0},{5,3},{6,2},{7,1},{8,12},{9,15},{10,... | collective-permute-start | bytes 69128 | tf_op jit(solution)/shard_map/ppermute | solution.py:47
  10.3 0.6 %shard_map.84.acc_ref = f32[288,640]{1,0:T(8,128)S(1)} custom-call(bf16[288,320]{1,0:T(8,128)(2,1)S(1)} %bitcast.11, bf16[288,320]{1,0:T(8,128)(2,1)S(1)} %collective-permute-done.other_ref, bf16[3,640,640]{2,1,0:T(8,128)(2,1)S(1)} %copy-done), custom_call_target="tpu_custom_call" | custom-call | flops 500000000 | tf_op jit(solution)/shard_map/pallas_call | solution.py:70
  10.9 0.1 shard_map.86.held_ref.refs_6_
  11.1 0.6 %collective-permute-start.2 = (bf16[18,640]{1,0:T(8,128)(2,1)S(1)}, bf16[18,640]{1,0:T(8,128)(2,1)S(1)}, u32[]{:S(2)}, u32[]{:S(2)}) collective-permute-start(bf16[18,640]{1,0:T(8,128)(2,1)S(1)} %shard_map.82.refs_0_), channel_id=1, source_target_pairs={{0,2},{2,0},{1,3},{3,1},{4,6},{6,4},{5,7},{7,5},{8,10},{10,8},{9,1... | collective-permute-start | bytes 69128 | tf_op jit(solution)/shard_map/ppermute | solution.py:63
  11.7 0.2 %collective-permute-start.11 = (bf16[4,320,640]{2,1,0:T(8,128)(2,1)S(1)}, bf16[4,320,640]{2,1,0:T(8,128)(2,1)S(1)}, u32[]{:S(2)}, u32[]{:S(2)}) collective-permute-start(bf16[4,320,640]{2,1,0:T(8,128)(2,1)S(1)} %shard_map.86.held_ref.refs_6_), channel_id=1, source_target_pairs={{0,1},{1,0},{2,3},{3,2},{4,5},{5,4},{6,7},{7,6},{8,9},{9,8},{10,11... | collective-permute-start | bytes 4915208 | tf_op jit(solution)/shard_map/ppermute | solution.py:35
  11.9 0.6 %shard_map.85.acc_ref = f32[288,640]{1,0:T(8,128)S(1)} custom-call(f32[288,640]{1,0:T(8,128)S(1)} %shard_map.84.acc_ref, bf16[288,320]{1,0:T(8,128)(2,1)S(1)} %collective-permute-done.7.even_ref, bf16[288,320]{1,0:T(8,128)(2,1)S(1)} %collective-permute-done.8.odd_ref, bf16[3,640,640]{2,1,0:T(8,128)(2,1)S(1)} %copy-done), custom_call_target="tpu_custom_call" | custom-call | flops 500000000 | tf_op jit(solution)/shard_map/pallas_call | solution.py:70
  12.5 0.0 copy-start.6
  12.5 0.2 %collective-permute-done.3.refs_0_ = bf16[18,640]{1,0:T(8,128)(2,1)S(1)} collective-permute-done((bf16[18,640]{1,0:T(8,128)(2,1)S(1)}, bf16[18,640]{1,0:T(8,128)(2,1)S(1)}, u32[]{:S(2)}, u32[]{:S(2)}) %collective-permute-start.3) | collective-permute-done | bytes 23072 | tf_op jit(solution)/shard_map/ppermute | solution.py:47
  12.7 0.2 collective-permute-start.10
  12.9 1.5 %collective-permute-done.4.refs_1_ = bf16[18,640]{1,0:T(8,128)(2,1)S(1)} collective-permute-done((bf16[18,640]{1,0:T(8,128)(2,1)S(1)}, bf16[18,640]{1,0:T(8,128)(2,1)S(1)}, u32[]{:S(2)}, u32[]{:S(2)}) %collective-permute-start.4) | collective-permute-done | bytes 23072 | tf_op jit(solution)/shard_map/ppermute | solution.py:47
  14.4 0.6 %collective-permute-start.6 = (bf16[54,640]{1,0:T(8,128)(2,1)S(1)}, bf16[54,640]{1,0:T(8,128)(2,1)S(1)}, u32[]{:S(2)}, u32[]{:S(2)}) collective-permute-start(bf16[54,640]{1,0:T(8,128)(2,1)S(1)} %shard_map.83.refs_2_), channel_id=1, source_target_pairs={{0,1},{1,0},{2,3},{3,2},{4,5},{5,4},{6,7},{7,6},{8,9},{9,8},{10,11... | collective-permute-start | bytes 207368 | tf_op jit(solution)/shard_map/ppermute | solution.py:35
  15.0 0.5 %collective-permute-done.10.odd_ref = bf16[288,320]{1,0:T(8,128)(2,1)S(1)} collective-permute-done((bf16[288,320]{1,0:T(8,128)(2,1)S(1)}, bf16[288,320]{1,0:T(8,128)(2,1)S(1)}, u32[]{:S(2)}, u32[]{:S(2)}) %collective-permute-start.10) | collective-permute-done | bytes 184352 | tf_op jit(solution)/shard_map/ppermute | solution.py:35
  15.5 0.3 %collective-permute-done.9.even_ref = bf16[288,320]{1,0:T(8,128)(2,1)S(1)} collective-permute-done((bf16[288,320]{1,0:T(8,128)(2,1)S(1)}, bf16[288,320]{1,0:T(8,128)(2,1)S(1)}, u32[]{:S(2)}, u32[]{:S(2)}) %collective-permute-start.9) | collective-permute-done | bytes 184352 | tf_op jit(solution)/shard_map/ppermute | solution.py:35
  15.9 1.4 %shard_map.87 = (bf16[288,320]{1,0:T(8,128)(2,1)S(1)}, bf16[640,288]{1,0:T(8,128)(2,1)S(1)}) custom-call(f32[288,640]{1,0:T(8,128)S(1)} %shard_map.85.acc_ref, bf16[288,320]{1,0:T(8,128)(2,1)S(1)} %collective-permute-done.9.even_ref, bf16[288,320]{1,0:T(8,128)(2,1)S(1)} %collective-permute-done.10.odd_ref, bf16[3,640,640]{2,1,0:T(8,128)(2,1)S(1)} %copy-done, ...), custom_call_target="tpu_custom_call" | custom-call | flops 1000000000 | tf_op jit(solution)/shard_map/pallas_call | solution.py:70
  17.3 2.4 %shard_map.88 = bf16[288,320]{1,0:T(8,128)(2,1)} custom-call(bf16[18,640]{1,0:T(8,128)(2,1)S(1)} %shard_map.82.refs_0_, bf16[18,640]{1,0:T(8,128)(2,1)S(1)} %collective-permute-done.2.refs_1_, bf16[54,640]{1,0:T(8,128)(2,1)S(1)} %shard_map.83.refs_2_, bf16[54,640]{1,0:T(8,128)(2,1)S(1)} %collective-permute-done.6.refs_3_, ...), custom_call_target="tpu_custom_call" | custom-call | flops 2000000000 | tf_op jit(solution)/shard_map/pallas_call | solution.py:70
  (23 shorter events, 0.1 us)
Async XLA Ops:
  0.0 10.3 %copy-start.5 = (bf16[1,6,48,320]{3,2,1,0:T(8,128)(2,1)S(1)}, bf16[1,6,48,320]{3,2,1,0:T(8,128)(2,1)}, u32[]{:S(2)}) copy-start(bf16[1,6,48,320]{3,2,1,0:T(8,128)(2,1)} %param.8) | copy-start | bytes 552964
  0.0 5.0 %collective-permute-start = (bf16[288,320]{1,0:T(8,128)(2,1)}, bf16[288,320]{1,0:T(8,128)(2,1)S(1)}, u32[]{:S(2)}, u32[]{:S(2)}) collective-permute-start(bf16[288,320]{1,0:T(8,128)(2,1)} %bitcast.8), channel_id=1, source_target_pairs={{0,1},{1,0},{2,3},{3,2},{4,5},{5,4},{6,7},{7,6},{8,9},{9,8},{10,11... | collective-permute-start | bytes 552968 | tf_op jit(solution)/shard_map/ppermute | solution.py:35
  0.5 4.6 %collective-permute-start.1 = (bf16[18,320]{1,0:T(8,128)(2,1)}, bf16[18,320]{1,0:T(8,128)(2,1)S(1)}, u32[]{:S(2)}, u32[]{:S(2)}) collective-permute-start(bf16[18,320]{1,0:T(8,128)(2,1)} %own_ref.1), channel_id=1, source_target_pairs={{0,1},{1,0},{2,3},{3,2},{4,5},{5,4},{6,7},{7,6},{8,9},{9,8},{10,11... | collective-permute-start | bytes 34568 | tf_op jit(solution)/shard_map/ppermute | solution.py:35
  0.5 10.6 %collective-permute-start.7 = (bf16[288,320]{1,0:T(8,128)(2,1)}, bf16[288,320]{1,0:T(8,128)(2,1)S(1)}, u32[]{:S(2)}, u32[]{:S(2)}) collective-permute-start(bf16[288,320]{1,0:T(8,128)(2,1)} %bitcast.9), channel_id=1, source_target_pairs={{0,4},{1,5},{2,6},{3,7},{4,0},{5,1},{6,2},{7,3},{8,12},{9,13},{10,... | collective-permute-start | bytes 552968 | tf_op jit(solution)/shard_map/ppermute | solution.py:47
  3.5 8.1 %collective-permute-start.8 = (bf16[288,320]{1,0:T(8,128)(2,1)}, bf16[288,320]{1,0:T(8,128)(2,1)S(1)}, u32[]{:S(2)}, u32[]{:S(2)}) collective-permute-start(bf16[288,320]{1,0:T(8,128)(2,1)} %bitcast.10), channel_id=1, source_target_pairs={{0,2},{1,3},{2,0},{3,1},{4,8},{5,9},{6,10},{7,11},{8,4},{9,5},{10,... | collective-permute-start | bytes 552968 | tf_op jit(solution)/shard_map/ppermute | solution.py:47
  5.0 0.7 %copy-start.7 = (bf16[18,320]{1,0:T(8,128)(2,1)S(1)}, bf16[18,320]{1,0:T(8,128)(2,1)}, u32[]{:S(2)}) copy-start(bf16[18,320]{1,0:T(8,128)(2,1)} %own_ref.1) | copy-start | bytes 34564
  5.8 4.6 %copy-start = (bf16[3,640,640]{2,1,0:T(8,128)(2,1)S(1)}, bf16[3,640,640]{2,1,0:T(8,128)(2,1)}, u32[]{:S(2)}) copy-start(bf16[3,640,640]{2,1,0:T(8,128)(2,1)} %w_ref.5) | copy-start | bytes 7372804
  5.8 5.1 %copy-start.1 = (bf16[640,320]{0,1:T(8,128)(2,1)S(1)}, bf16[640,320]{0,1:T(8,128)(2,1)}, u32[]{:S(2)}) copy-start(bf16[640,320]{0,1:T(8,128)(2,1)} %param.11) | copy-start | bytes 1228804
  5.8 5.1 %copy-start.2 = (bf16[640,320]{0,1:T(8,128)(2,1)S(1)}, bf16[640,320]{0,1:T(8,128)(2,1)}, u32[]{:S(2)}) copy-start(bf16[640,320]{0,1:T(8,128)(2,1)} %param.12) | copy-start | bytes 1228804
  5.8 5.1 %copy-start.3 = (bf16[640,320]{0,1:T(8,128)(2,1)S(1)}, bf16[640,320]{0,1:T(8,128)(2,1)}, u32[]{:S(2)}) copy-start(bf16[640,320]{0,1:T(8,128)(2,1)} %param.13) | copy-start | bytes 1228804
  5.9 5.1 %copy-start.4 = (bf16[320,640]{1,0:T(8,128)(2,1)S(1)}, bf16[320,640]{1,0:T(8,128)(2,1)}, u32[]{:S(2)}) copy-start(bf16[320,640]{1,0:T(8,128)(2,1)} %refs_3_) | copy-start | bytes 1228804
  5.9 6.8 %collective-permute-start.3 = (bf16[18,640]{1,0:T(8,128)(2,1)S(1)}, bf16[18,640]{1,0:T(8,128)(2,1)S(1)}, u32[]{:S(2)}, u32[]{:S(2)}) collective-permute-start(bf16[18,640]{1,0:T(8,128)(2,1)S(1)} %shard_map.82.refs_0_), channel_id=1, source_target_pairs={{0,12},{1,15},{2,14},{3,13},{4,8},{5,11},{6,10},{7,9},{8,4},{9,7},... | collective-permute-start | bytes 69128 | tf_op jit(solution)/shard_map/ppermute | solution.py:47
  8.4 6.0 %collective-permute-start.4 = (bf16[18,640]{1,0:T(8,128)(2,1)S(1)}, bf16[18,640]{1,0:T(8,128)(2,1)S(1)}, u32[]{:S(2)}, u32[]{:S(2)}) collective-permute-start(bf16[18,640]{1,0:T(8,128)(2,1)S(1)} %shard_map.82.refs_0_), channel_id=1, source_target_pairs={{0,8},{1,11},{2,10},{3,9},{4,12},{5,15},{6,14},{7,13},{8,0},{9,3},... | collective-permute-start | bytes 69128 | tf_op jit(solution)/shard_map/ppermute | solution.py:47
  9.1 5.3 %collective-permute-start.5 = (bf16[18,640]{1,0:T(8,128)(2,1)S(1)}, bf16[18,640]{1,0:T(8,128)(2,1)S(1)}, u32[]{:S(2)}, u32[]{:S(2)}) collective-permute-start(bf16[18,640]{1,0:T(8,128)(2,1)S(1)} %shard_map.82.refs_0_), channel_id=1, source_target_pairs={{0,4},{1,7},{2,6},{3,5},{4,0},{5,3},{6,2},{7,1},{8,12},{9,15},{10,... | collective-permute-start | bytes 69128 | tf_op jit(solution)/shard_map/ppermute | solution.py:47
  11.1 6.2 %collective-permute-start.2 = (bf16[18,640]{1,0:T(8,128)(2,1)S(1)}, bf16[18,640]{1,0:T(8,128)(2,1)S(1)}, u32[]{:S(2)}, u32[]{:S(2)}) collective-permute-start(bf16[18,640]{1,0:T(8,128)(2,1)S(1)} %shard_map.82.refs_0_), channel_id=1, source_target_pairs={{0,2},{2,0},{1,3},{3,1},{4,6},{6,4},{5,7},{7,5},{8,10},{10,8},{9,1... | collective-permute-start | bytes 69128 | tf_op jit(solution)/shard_map/ppermute | solution.py:63
  11.7 4.2 %collective-permute-start.11 = (bf16[4,320,640]{2,1,0:T(8,128)(2,1)S(1)}, bf16[4,320,640]{2,1,0:T(8,128)(2,1)S(1)}, u32[]{:S(2)}, u32[]{:S(2)}) collective-permute-start(bf16[4,320,640]{2,1,0:T(8,128)(2,1)S(1)} %shard_map.86.held_ref.refs_6_), channel_id=1, source_target_pairs={{0,1},{1,0},{2,3},{3,2},{4,5},{5,4},{6,7},{7,6},{8,9},{9,8},{10,11... | collective-permute-start | bytes 4915208 | tf_op jit(solution)/shard_map/ppermute | solution.py:35
  12.5 3.4 %copy-start.6 = (f32[640]{0:T(1024)S(1)}, f32[640]{0:T(1024)}, u32[]{:S(2)}) copy-start(f32[640]{0:T(1024)} %gain_ref.1) | copy-start | bytes 7684
  12.7 2.8 %collective-permute-start.10 = (bf16[288,320]{1,0:T(8,128)(2,1)S(1)}, bf16[288,320]{1,0:T(8,128)(2,1)S(1)}, u32[]{:S(2)}, u32[]{:S(2)}) collective-permute-start(bf16[288,320]{1,0:T(8,128)(2,1)S(1)} %collective-permute-done.8.odd_ref), channel_id=1, source_target_pairs={{0,1},{1,0},{2,3},{3,2},{4,5},{5,4},{6,7},{7,6},{8,9},{9,8},{10,11... | collective-permute-start | bytes 552968 | tf_op jit(solution)/shard_map/ppermute | solution.py:35
  14.4 1.5 %collective-permute-start.9 = (bf16[288,320]{1,0:T(8,128)(2,1)S(1)}, bf16[288,320]{1,0:T(8,128)(2,1)S(1)}, u32[]{:S(2)}, u32[]{:S(2)}) collective-permute-start(bf16[288,320]{1,0:T(8,128)(2,1)S(1)} %collective-permute-done.7.even_ref), channel_id=1, source_target_pairs={{0,1},{1,0},{2,3},{3,2},{4,5},{5,4},{6,7},{7,6},{8,9},{9,8},{10,11... | collective-permute-start | bytes 552968 | tf_op jit(solution)/shard_map/ppermute | solution.py:35
  14.4 2.9 %collective-permute-start.6 = (bf16[54,640]{1,0:T(8,128)(2,1)S(1)}, bf16[54,640]{1,0:T(8,128)(2,1)S(1)}, u32[]{:S(2)}, u32[]{:S(2)}) collective-permute-start(bf16[54,640]{1,0:T(8,128)(2,1)S(1)} %shard_map.83.refs_2_), channel_id=1, source_target_pairs={{0,1},{1,0},{2,3},{3,2},{4,5},{5,4},{6,7},{7,6},{8,9},{9,8},{10,11... | collective-permute-start | bytes 207368 | tf_op jit(solution)/shard_map/ppermute | solution.py:35

commit v5 on v4

--- a/solution.py
+++ b/solution.py
@@ -10,8 +10,10 @@
 C = 640
 HEADS = 8
 EPS = 1e-05
+LANES = 128
 
 JOIN = 10 * 10**9
+AHEAD = 20 * 10**9
 MIDDLE = 5 * 10**8
 FIRST = 5 * 10**8
 QUERY = 10**9
@@ -93,11 +95,30 @@
     out_ref[:, half:] = jnp.where(core == 0, other, own)
 
 
-def gather_tokens(own):
+def blank_kernel(_, out_ref):
+    out_ref[...] = jnp.zeros_like(out_ref)
+
+
+def first_join_kernel(own_ref, other_ref, _, out_ref, packed_ref):
+    join_kernel(own_ref, other_ref, out_ref)
+    width = out_ref.shape[0]
+    for i in range(C // LANES):
+        packed_ref[i * width : (i + 1) * width] = out_ref[:, i * LANES : (i + 1) * LANES]
+
+
+def unpack_kernel(*refs):
+    out_ref = refs[-1]
+    width = refs[0].shape[0] * LANES // C
+    for at, ref in enumerate(refs[:-1]):
+        for i in range(C // LANES):
+            out_ref[at * width : (at + 1) * width, i * LANES : (i + 1) * LANES] = ref[i * width : (i + 1) * width]
+
+
+def gather_tokens(own, packed):
     frames, rows = lax.axis_size("frames"), lax.axis_size("rows")
     if frames == 4 and rows == 2:
-        far = [swap(own, lambda f, r, c, d=d: (f ^ d, r ^ c, c)) for d in (3, 2, 1)]
-        (rest,) = call(stack_kernel, far, [((3 * own.shape[0], C), BF16)], flops=REST)
+        far = [swap(packed, lambda f, r, c, d=d: (f ^ d, r ^ c, c)) for d in (3, 2, 1)]
+        (rest,) = call(unpack_kernel, far, [((3 * own.shape[0], C), BF16)], flops=REST)
         return [own, swap_bit(own, "rows", 1)], [rest]
     parts = [own]
     for axis, count in (("frames", frames), ("rows", rows)):
@@ -137,9 +158,16 @@
     acc_ref[...] = whole.astype(F32) + jnp.dot(whole, w_ref[1], preferred_element_type=F32)
 
 
-def weights_kernel(*refs):
-    for i, ref in enumerate(refs[:-1]):
-        refs[-1][i] = ref[...]
+def weights_kernel(wq_ref, wk_ref, wv_ref, wo_ref, held_ref, out_ref):
+    core = lax.axis_index("heads")
+    half = wo_ref.shape[0]
+    for i, ref in enumerate((wq_ref, wk_ref, wv_ref)):
+        held_ref[i * half : (i + 1) * half] = ref[...]
+    left, right = wo_ref[:, :half], wo_ref[:, half:]
+    out_ref[...] = jnp.where(core == 0, left, right)
+    sent = jnp.where(core == 0, right, left)
+    held_ref[3 * half :, :half] = sent[: half // 2]
+    held_ref[3 * half :, half:] = sent[half // 2 :]
 
 
 def first_kernel(frames, acc_ref, even_ref, odd_ref, w_ref, sum_ref):
@@ -149,7 +177,7 @@
 
 def query_kernel(frames, acc_ref, even_ref, odd_ref, w_ref, held_ref, met_ref, gain_ref, temporal_ref, query_ref):
     core = lax.axis_index("heads")
-    half = held_ref.shape[1]
+    half = held_ref.shape[1] // 2
     other = halves(core, half)[1]
     temporal = (acc_ref[...] + beside((even_ref, odd_ref), w_ref, other, frames)).astype(BF16)
     temporal_ref[...] = jnp.where(core == 0, temporal[:, :half], temporal[:, half:])
@@ -159,27 +187,27 @@
     spread = jnp.mean(centred * centred, axis=-1, keepdims=True)
     normed = (centred * lax.rsqrt(spread + EPS) * gain_ref[...]).astype(BF16)
     scale = (C // HEADS) ** -0.5
-    query_ref[:half] = (nt_dot(held_ref[0], normed) * scale).astype(BF16)
-    query_ref[half:] = (nt_dot(met_ref[0], normed) * scale).astype(BF16)
+    query_ref[:half] = (nt_dot(held_ref[:half], normed) * scale).astype(BF16)
+    query_ref[half:] = (nt_dot(met_ref[:half], normed) * scale).astype(BF16)
 
 
 def attend_kernel(parts, *refs):
-    core = lax.axis_index("heads")
     blocks, refs = refs[:parts], refs[parts:]
-    query_ref, temporal_ref, held_ref, met_ref, out_ref, tokens, keys, values, attended, out_weights = refs
-    half = held_ref.shape[1]
+    query_ref, temporal_ref, held_ref, met_ref, wo_ref, out_ref, tokens, keys, values, attended, out_weights = refs
+    half = held_ref.shape[1] // 2
     size = C // HEADS
     at = 0
     for ref in blocks:
         tokens[at : at + ref.shape[0]] = ref[...]
         at += ref.shape[0]
     toks = tokens[...]
-    for part, w_ref in enumerate((held_ref, met_ref)):
-        out_weights[part * half : (part + 1) * half] = jnp.where(core == 0, w_ref[3, :, :half], w_ref[3, :, half:])
-        values[part * half : (part + 1) * half] = nt_dot(w_ref[2], toks).astype(BF16)
-        found = nt_dot(toks, w_ref[1]).astype(BF16)
-        for head in range(half // size):
-            keys[part * (half // size) + head, :, :size] = found[:, head * size : (head + 1) * size]
+    wk, wv = (
+        jnp.concatenate([ref[i * half : (i + 1) * half] for ref in (held_ref, met_ref)], axis=0) for i in (1, 2)
+    )
+    values[...] = nt_dot(wv, toks).astype(BF16)
+    found = nt_dot(toks, wk).astype(BF16)
+    for head in range(HEADS):
+        keys[head, :, :size] = found[:, head * size : (head + 1) * size]
     probs = []
     for head in range(HEADS):
         rows = slice(head * size, (head + 1) * size)
@@ -191,6 +219,9 @@
         prob, inverse = probs[head]
         mixed = jnp.dot(values[rows], prob, preferred_element_type=F32)
         attended[rows] = (mixed * inverse).astype(BF16)
+    out_weights[:half] = wo_ref[...]
+    out_weights[half : half + half // 2] = met_ref[3 * half :, :half]
+    out_weights[half + half // 2 :] = met_ref[3 * half :, half:]
     mixed = tn_dot(attended[...], out_weights[...])
     out_ref[...] = (temporal_ref[...].astype(F32) + mixed).astype(BF16)
 
@@ -207,8 +238,14 @@
     clip_other, toks_other = lax.optimization_barrier((clip_other, toks_other))
     even, odd = swap_frames(clip, 0), swap_frames(clip, 1)
     even_other, odd_other = sibling(even), sibling(odd)
-    (own,) = call(join_kernel, (reference_tokens, toks_other), [((width, C), BF16)], flops=JOIN)
-    toks, rest = gather_tokens(own)
+    (blank,) = call(blank_kernel, (toks_other,), [((8, 128), F32)], flops=AHEAD)
+    own, packed = call(
+        first_join_kernel,
+        (reference_tokens, toks_other, blank),
+        [((width, C), BF16), ((width * C // LANES, LANES), BF16)],
+        flops=JOIN,
+    )
+    toks, rest = gather_tokens(own, packed)
     (acc,) = call(
         middle_kernel,
         (clip, clip_other, w_time),
@@ -217,7 +254,7 @@
         flops=MIDDLE,
     )
     *wide, _ = lax.optimization_barrier((w_query.T, w_key.T, w_value.T, w_out, acc))
-    (held,) = call(weights_kernel, wide, [((4,) + w_out.shape, BF16)], flops=WEIGHTS)
+    held, wo = call(weights_kernel, wide, [((7 * half // 2, C), BF16), ((half, half), BF16)], flops=WEIGHTS)
     met = sibling(held)
     (acc,) = call(
         functools.partial(first_kernel, frames), (acc, even, odd, w_time), [((places, C), F32)], flops=FIRST
@@ -233,7 +270,7 @@
     count = width * frames * lax.axis_size("rows")
     (out,) = call(
         functools.partial(attend_kernel, len(toks)),
-        (*toks, query, temporal, held, met),
+        (*toks, query, temporal, held, met, wo),
         [((places, half), BF16)],
         [
             pltpu.VMEM((count, C), BF16),

time: 19.9 us -> 19.3 us (0.970)
  waiting for transfers between devices: 2.62 us -> 1.66 us
  starting transfers between devices: 11 us -> 11.9 us
  local copies, waits for them, and re-layouts: 0.75 us -> 0.05 us
    ppermute x1, starting transfers between devices: 0.6 us -> 1.68 us  [swap_bit(): lax.ppermute(x, axis, [(i, i ^ bit) for i in range(lax.axis_size(axis))])]
    ppermute x5, waiting for transfers between devices: 1.73 us -> 0.78 us  [swap(): return lax.ppermute(x, ('frames', 'rows', 'heads'), perm)]
    unnamed x16, local copies, waits for them, and re-layouts: 0.75 us -> 0.05 us
    ppermute x6, starting transfers between devices: 1.46 us -> 1.23 us  [sibling(): return lax.ppermute(x, 'heads', [(0, 1), (1, 0)])]
    pallas_call x7 -> x8, Pallas kernels: 5.23 us -> 5.35 us  [call(): pl.pallas_call(kernel, out_shape=[jax.ShapeDtypeStruct(shape, dtype) for...]
  transfers between devices with their start and end apart: 12 -> 12, of which waited for: 4 -> 4; matrix products, arithmetic and copies ran while one was open for 0% -> 0% of each run, Pallas kernels for 14% -> 16%
where the time goes in v5:
time: 19.3 us; the launch traced here: 19.1 us
  starting transfers between devices  11.9 us (62%)
  Pallas kernels  5.35 us (28%)
  waiting for transfers between devices  1.66 us (9%)
  between operations  0.2 us (1%)
    ppermute x5, starting transfers between devices, swap(): return lax.ppermute(x, ('frames', 'rows', 'heads'), perm)  8.96 us
    pallas_call x8, Pallas kernels, call(): pl.pallas_call(kernel, out_shape=[jax.ShapeDtypeStruct(shape, dtype) for...  5.35 us
    ppermute x1, starting transfers between devices, swap_bit(): lax.ppermute(x, axis, [(i, i ^ bit) for i in range(lax.axis_size(axis))])  1.68 us
    ppermute x6, starting transfers between devices, sibling(): return lax.ppermute(x, 'heads', [(0, 1), (1, 0)])  1.23 us
    ppermute x6, waiting for transfers between devices, sibling(): return lax.ppermute(x, 'heads', [(0, 1), (1, 0)])  0.88 us
    ppermute x5, waiting for transfers between devices, swap(): return lax.ppermute(x, ('frames', 'rows', 'heads'), perm)  0.78 us
  transfers between devices with their start and end apart: 12, of which 4 were waited for; matrix products, arithmetic and copies ran while one was open for 0% of the time, Pallas kernels for 16%

profile of v5, /device:TPU:0, one launch (start us, length us, event | category | flops | bytes accessed | tf_op | source)
XLA Modules:
  0.0 19.1 jit_solution(510333479636117011)
XLA Ops:
  0.0 0.5 %collective-permute-start = (bf16[288,320]{1,0:T(8,128)(2,1)}, bf16[288,320]{1,0:T(8,128)(2,1)S(1)}, u32[]{:S(2)}, u32[]{:S(2)}) collective-permute-start(bf16[288,320]{1,0:T(8,128)(2,1)} %bitcast.8), channel_id=1, source_target_pairs={{0,1},{1,0},{2,3},{3,2},{4,5},{5,4},{6,7},{7,6},{8,9},{9,8},{10,11... | collective-permute-start | bytes 552968 | tf_op jit(solution)/shard_map/ppermute | solution.py:37
  0.5 0.1 collective-permute-start.1
  0.5 3.0 %collective-permute-start.7 = (bf16[288,320]{1,0:T(8,128)(2,1)}, bf16[288,320]{1,0:T(8,128)(2,1)S(1)}, u32[]{:S(2)}, u32[]{:S(2)}) collective-permute-start(bf16[288,320]{1,0:T(8,128)(2,1)} %bitcast.9), channel_id=1, source_target_pairs={{0,4},{1,5},{2,6},{3,7},{4,0},{5,1},{6,2},{7,3},{8,12},{9,13},{10,... | collective-permute-start | bytes 552968 | tf_op jit(solution)/shard_map/ppermute | solution.py:49
  3.5 1.5 %collective-permute-start.8 = (bf16[288,320]{1,0:T(8,128)(2,1)}, bf16[288,320]{1,0:T(8,128)(2,1)S(1)}, u32[]{:S(2)}, u32[]{:S(2)}) collective-permute-start(bf16[288,320]{1,0:T(8,128)(2,1)} %bitcast.10), channel_id=1, source_target_pairs={{0,2},{1,3},{2,0},{3,1},{4,8},{5,9},{6,10},{7,11},{8,4},{9,5},{10,... | collective-permute-start | bytes 552968 | tf_op jit(solution)/shard_map/ppermute | solution.py:49
  5.1 0.0 copy-start
  5.1 0.1 shard_map.83
  5.2 0.0 copy-start.1
  5.2 0.0 copy-start.2
  5.2 2.5 %collective-permute-start.3 = (bf16[90,128]{1,0:T(8,128)(2,1)S(1)}, bf16[90,128]{1,0:T(8,128)(2,1)S(1)}, u32[]{:S(2)}, u32[]{:S(2)}) collective-permute-start(bf16[90,128]{1,0:T(8,128)(2,1)S(1)} %get-tuple-element.19), channel_id=1, source_target_pairs={{0,12},{1,15},{2,14},{3,13},{4,8},{5,11},{6,10},{7,9},{8,4},{9,7},... | collective-permute-start | bytes 69128 | tf_op jit(solution)/shard_map/ppermute | solution.py:49
  7.8 0.6 %collective-permute-start.4 = (bf16[90,128]{1,0:T(8,128)(2,1)S(1)}, bf16[90,128]{1,0:T(8,128)(2,1)S(1)}, u32[]{:S(2)}, u32[]{:S(2)}) collective-permute-start(bf16[90,128]{1,0:T(8,128)(2,1)S(1)} %get-tuple-element.19), channel_id=1, source_target_pairs={{0,8},{1,11},{2,10},{3,9},{4,12},{5,15},{6,14},{7,13},{8,0},{9,3},... | collective-permute-start | bytes 69128 | tf_op jit(solution)/shard_map/ppermute | solution.py:49
  8.4 1.3 %collective-permute-start.5 = (bf16[90,128]{1,0:T(8,128)(2,1)S(1)}, bf16[90,128]{1,0:T(8,128)(2,1)S(1)}, u32[]{:S(2)}, u32[]{:S(2)}) collective-permute-start(bf16[90,128]{1,0:T(8,128)(2,1)S(1)} %get-tuple-element.19), channel_id=1, source_target_pairs={{0,4},{1,7},{2,6},{3,5},{4,0},{5,3},{6,2},{7,1},{8,12},{9,15},{10,... | collective-permute-start | bytes 69128 | tf_op jit(solution)/shard_map/ppermute | solution.py:49
  9.7 0.6 %shard_map.85.acc_ref = f32[288,640]{1,0:T(8,128)S(1)} custom-call(bf16[288,320]{1,0:T(8,128)(2,1)S(1)} %bitcast.11, bf16[288,320]{1,0:T(8,128)(2,1)S(1)} %collective-permute-done.other_ref, bf16[3,640,640]{2,1,0:T(8,128)(2,1)S(1)} %copy-done), custom_call_target="tpu_custom_call" | custom-call | flops 500000000 | tf_op jit(solution)/shard_map/pallas_call | solution.py:72
  10.3 0.3 %shard_map.87 = (bf16[1120,640]{1,0:T(8,128)(2,1)S(1)}, bf16[320,320]{1,0:T(8,128)(2,1)S(1)}) custom-call(bf16[320,640]{1,0:T(8,128)(2,1)S(1)} %bitcast.5, bf16[320,640]{1,0:T(8,128)(2,1)S(1)} %bitcast.6, bf16[320,640]{1,0:T(8,128)(2,1)S(1)} %bitcast.7, bf16[320,640]{1,0:T(8,128)(2,1)S(1)} %copy-done.4), custom_call_target="tpu_custom_call" | custom-call | flops 100000000 | tf_op jit(solution)/shard_map/pallas_call | solution.py:72
  10.6 0.1 collective-permute-start.11
  10.7 0.2 collective-permute-done.8.odd_ref
  10.9 1.7 %collective-permute-start.2 = (bf16[18,640]{1,0:T(8,128)(2,1)S(1)}, bf16[18,640]{1,0:T(8,128)(2,1)S(1)}, u32[]{:S(2)}, u32[]{:S(2)}) collective-permute-start(bf16[18,640]{1,0:T(8,128)(2,1)S(1)} %get-tuple-element.18.refs_0_), channel_id=1, source_target_pairs={{0,2},{2,0},{1,3},{3,1},{4,6},{6,4},{5,7},{7,5},{8,10},{10,8},{9,1... | collective-permute-start | bytes 69128 | tf_op jit(solution)/shard_map/ppermute | solution.py:65
  12.5 0.6 %shard_map.86.acc_ref = f32[288,640]{1,0:T(8,128)S(1)} custom-call(f32[288,640]{1,0:T(8,128)S(1)} %shard_map.85.acc_ref, bf16[288,320]{1,0:T(8,128)(2,1)S(1)} %collective-permute-done.7.even_ref, bf16[288,320]{1,0:T(8,128)(2,1)S(1)} %collective-permute-done.8.odd_ref, bf16[3,640,640]{2,1,0:T(8,128)(2,1)S(1)} %copy-done), custom_call_target="tpu_custom_call" | custom-call | flops 500000000 | tf_op jit(solution)/shard_map/pallas_call | solution.py:72
  13.2 0.1 collective-permute-start.10
  13.2 0.6 %collective-permute-done.4.refs_1_ = bf16[90,128]{1,0:T(8,128)(2,1)S(1)} collective-permute-done((bf16[90,128]{1,0:T(8,128)(2,1)S(1)}, bf16[90,128]{1,0:T(8,128)(2,1)S(1)}, u32[]{:S(2)}, u32[]{:S(2)}) %collective-permute-start.4) | collective-permute-done | bytes 23072 | tf_op jit(solution)/shard_map/ppermute | solution.py:49
  13.9 0.6 %collective-permute-start.6 = (bf16[54,640]{1,0:T(8,128)(2,1)S(1)}, bf16[54,640]{1,0:T(8,128)(2,1)S(1)}, u32[]{:S(2)}, u32[]{:S(2)}) collective-permute-start(bf16[54,640]{1,0:T(8,128)(2,1)S(1)} %shard_map.84.refs_2_), channel_id=1, source_target_pairs={{0,1},{1,0},{2,3},{3,2},{4,5},{5,4},{6,7},{7,6},{8,9},{9,8},{10,11... | collective-permute-start | bytes 207368 | tf_op jit(solution)/shard_map/ppermute | solution.py:37
  14.5 0.2 %collective-permute-done.10.odd_ref = bf16[288,320]{1,0:T(8,128)(2,1)S(1)} collective-permute-done((bf16[288,320]{1,0:T(8,128)(2,1)S(1)}, bf16[288,320]{1,0:T(8,128)(2,1)S(1)}, u32[]{:S(2)}, u32[]{:S(2)}) %collective-permute-start.10) | collective-permute-done | bytes 184352 | tf_op jit(solution)/shard_map/ppermute | solution.py:37
  14.7 0.6 %collective-permute-done.9.even_ref = bf16[288,320]{1,0:T(8,128)(2,1)S(1)} collective-permute-done((bf16[288,320]{1,0:T(8,128)(2,1)S(1)}, bf16[288,320]{1,0:T(8,128)(2,1)S(1)}, u32[]{:S(2)}, u32[]{:S(2)}) %collective-permute-start.9) | collective-permute-done | bytes 184352 | tf_op jit(solution)/shard_map/ppermute | solution.py:37
  15.3 1.4 %shard_map.88 = (bf16[288,320]{1,0:T(8,128)(2,1)S(1)}, bf16[640,288]{1,0:T(8,128)(2,1)S(1)}) custom-call(f32[288,640]{1,0:T(8,128)S(1)} %shard_map.86.acc_ref, bf16[288,320]{1,0:T(8,128)(2,1)S(1)} %collective-permute-done.9.even_ref, bf16[288,320]{1,0:T(8,128)(2,1)S(1)} %collective-permute-done.10.odd_ref, bf16[3,640,640]{2,1,0:T(8,128)(2,1)S(1)} %copy-done, ...), custom_call_target="tpu_custom_call" | custom-call | flops 1000000000 | tf_op jit(solution)/shard_map/pallas_call | solution.py:72
  16.8 2.3 %shard_map.89 = bf16[288,320]{1,0:T(8,128)(2,1)} custom-call(bf16[18,640]{1,0:T(8,128)(2,1)S(1)} %get-tuple-element.18.refs_0_, bf16[18,640]{1,0:T(8,128)(2,1)S(1)} %collective-permute-done.2.refs_1_, bf16[54,640]{1,0:T(8,128)(2,1)S(1)} %shard_map.84.refs_2_, bf16[54,640]{1,0:T(8,128)(2,1)S(1)} %collective-permute-done.6.refs_3_, ...), custom_call_target="tpu_custom_call" | custom-call | flops 2000000000 | tf_op jit(solution)/shard_map/pallas_call | solution.py:72
  (24 shorter events, 0.1 us)
Async XLA Ops:
  0.0 5.0 %copy-start.7 = (bf16[18,320]{1,0:T(8,128)(2,1)S(1)}, bf16[18,320]{1,0:T(8,128)(2,1)}, u32[]{:S(2)}) copy-start(bf16[18,320]{1,0:T(8,128)(2,1)} %own_ref.1) | copy-start | bytes 34564
  0.0 5.0 %collective-permute-start = (bf16[288,320]{1,0:T(8,128)(2,1)}, bf16[288,320]{1,0:T(8,128)(2,1)S(1)}, u32[]{:S(2)}, u32[]{:S(2)}) collective-permute-start(bf16[288,320]{1,0:T(8,128)(2,1)} %bitcast.8), channel_id=1, source_target_pairs={{0,1},{1,0},{2,3},{3,2},{4,5},{5,4},{6,7},{7,6},{8,9},{9,8},{10,11... | collective-permute-start | bytes 552968 | tf_op jit(solution)/shard_map/ppermute | solution.py:37
  0.5 4.6 %collective-permute-start.1 = (bf16[18,320]{1,0:T(8,128)(2,1)}, bf16[18,320]{1,0:T(8,128)(2,1)S(1)}, u32[]{:S(2)}, u32[]{:S(2)}) collective-permute-start(bf16[18,320]{1,0:T(8,128)(2,1)} %own_ref.1), channel_id=1, source_target_pairs={{0,1},{1,0},{2,3},{3,2},{4,5},{5,4},{6,7},{7,6},{8,9},{9,8},{10,11... | collective-permute-start | bytes 34568 | tf_op jit(solution)/shard_map/ppermute | solution.py:37
  0.5 10.1 %collective-permute-start.7 = (bf16[288,320]{1,0:T(8,128)(2,1)}, bf16[288,320]{1,0:T(8,128)(2,1)S(1)}, u32[]{:S(2)}, u32[]{:S(2)}) collective-permute-start(bf16[288,320]{1,0:T(8,128)(2,1)} %bitcast.9), channel_id=1, source_target_pairs={{0,4},{1,5},{2,6},{3,7},{4,0},{5,1},{6,2},{7,3},{8,12},{9,13},{10,... | collective-permute-start | bytes 552968 | tf_op jit(solution)/shard_map/ppermute | solution.py:49
  3.5 7.3 %collective-permute-start.8 = (bf16[288,320]{1,0:T(8,128)(2,1)}, bf16[288,320]{1,0:T(8,128)(2,1)S(1)}, u32[]{:S(2)}, u32[]{:S(2)}) collective-permute-start(bf16[288,320]{1,0:T(8,128)(2,1)} %bitcast.10), channel_id=1, source_target_pairs={{0,2},{1,3},{2,0},{3,1},{4,8},{5,9},{6,10},{7,11},{8,4},{9,5},{10,... | collective-permute-start | bytes 552968 | tf_op jit(solution)/shard_map/ppermute | solution.py:49
  5.1 4.6 %copy-start = (bf16[3,640,640]{2,1,0:T(8,128)(2,1)S(1)}, bf16[3,640,640]{2,1,0:T(8,128)(2,1)}, u32[]{:S(2)}) copy-start(bf16[3,640,640]{2,1,0:T(8,128)(2,1)} %w_ref.5) | copy-start | bytes 7372804
  5.1 4.6 %copy-start.5 = (bf16[1,6,48,320]{3,2,1,0:T(8,128)(2,1)S(1)}, bf16[1,6,48,320]{3,2,1,0:T(8,128)(2,1)}, u32[]{:S(2)}) copy-start(bf16[1,6,48,320]{3,2,1,0:T(8,128)(2,1)} %param.8) | copy-start | bytes 552964
  5.2 5.1 %copy-start.1 = (bf16[640,320]{0,1:T(8,128)(2,1)S(1)}, bf16[640,320]{0,1:T(8,128)(2,1)}, u32[]{:S(2)}) copy-start(bf16[640,320]{0,1:T(8,128)(2,1)} %param.11) | copy-start | bytes 1228804
  5.2 5.1 %copy-start.2 = (bf16[640,320]{0,1:T(8,128)(2,1)S(1)}, bf16[640,320]{0,1:T(8,128)(2,1)}, u32[]{:S(2)}) copy-start(bf16[640,320]{0,1:T(8,128)(2,1)} %param.12) | copy-start | bytes 1228804
  5.2 5.1 %copy-start.3 = (bf16[640,320]{0,1:T(8,128)(2,1)S(1)}, bf16[640,320]{0,1:T(8,128)(2,1)}, u32[]{:S(2)}) copy-start(bf16[640,320]{0,1:T(8,128)(2,1)} %param.13) | copy-start | bytes 1228804
  5.2 5.1 %copy-start.4 = (bf16[320,640]{1,0:T(8,128)(2,1)S(1)}, bf16[320,640]{1,0:T(8,128)(2,1)}, u32[]{:S(2)}) copy-start(bf16[320,640]{1,0:T(8,128)(2,1)} %wo_ref) | copy-start | bytes 1228804
  5.2 7.9 %collective-permute-start.3 = (bf16[90,128]{1,0:T(8,128)(2,1)S(1)}, bf16[90,128]{1,0:T(8,128)(2,1)S(1)}, u32[]{:S(2)}, u32[]{:S(2)}) collective-permute-start(bf16[90,128]{1,0:T(8,128)(2,1)S(1)} %get-tuple-element.19), channel_id=1, source_target_pairs={{0,12},{1,15},{2,14},{3,13},{4,8},{5,11},{6,10},{7,9},{8,4},{9,7},... | collective-permute-start | bytes 69128 | tf_op jit(solution)/shard_map/ppermute | solution.py:49
  7.8 6.1 %collective-permute-start.4 = (bf16[90,128]{1,0:T(8,128)(2,1)S(1)}, bf16[90,128]{1,0:T(8,128)(2,1)S(1)}, u32[]{:S(2)}, u32[]{:S(2)}) collective-permute-start(bf16[90,128]{1,0:T(8,128)(2,1)S(1)} %get-tuple-element.19), channel_id=1, source_target_pairs={{0,8},{1,11},{2,10},{3,9},{4,12},{5,15},{6,14},{7,13},{8,0},{9,3},... | collective-permute-start | bytes 69128 | tf_op jit(solution)/shard_map/ppermute | solution.py:49
  8.4 5.4 %collective-permute-start.5 = (bf16[90,128]{1,0:T(8,128)(2,1)S(1)}, bf16[90,128]{1,0:T(8,128)(2,1)S(1)}, u32[]{:S(2)}, u32[]{:S(2)}) collective-permute-start(bf16[90,128]{1,0:T(8,128)(2,1)S(1)} %get-tuple-element.19), channel_id=1, source_target_pairs={{0,4},{1,7},{2,6},{3,5},{4,0},{5,3},{6,2},{7,1},{8,12},{9,15},{10,... | collective-permute-start | bytes 69128 | tf_op jit(solution)/shard_map/ppermute | solution.py:49
  10.6 4.7 %collective-permute-start.11 = (bf16[1120,640]{1,0:T(8,128)(2,1)S(1)}, bf16[1120,640]{1,0:T(8,128)(2,1)S(1)}, u32[]{:S(2)}, u32[]{:S(2)}) collective-permute-start(bf16[1120,640]{1,0:T(8,128)(2,1)S(1)} %get-tuple-element.25.held_ref.refs_6_), channel_id=1, source_target_pairs={{0,1},{1,0},{2,3},{3,2},{4,5},{5,4},{6,7},{7,6},{8,9},{9,8},{10,11... | collective-permute-start | bytes 4300808 | tf_op jit(solution)/shard_map/ppermute | solution.py:37
  10.9 5.9 %collective-permute-start.2 = (bf16[18,640]{1,0:T(8,128)(2,1)S(1)}, bf16[18,640]{1,0:T(8,128)(2,1)S(1)}, u32[]{:S(2)}, u32[]{:S(2)}) collective-permute-start(bf16[18,640]{1,0:T(8,128)(2,1)S(1)} %get-tuple-element.18.refs_0_), channel_id=1, source_target_pairs={{0,2},{2,0},{1,3},{3,1},{4,6},{6,4},{5,7},{7,5},{8,10},{10,8},{9,1... | collective-permute-start | bytes 69128 | tf_op jit(solution)/shard_map/ppermute | solution.py:65
  13.1 2.2 %copy-start.6 = (f32[640]{0:T(1024)S(1)}, f32[640]{0:T(1024)}, u32[]{:S(2)}) copy-start(f32[640]{0:T(1024)} %gain_ref.1) | copy-start | bytes 7684
  13.2 1.5 %collective-permute-start.10 = (bf16[288,320]{1,0:T(8,128)(2,1)S(1)}, bf16[288,320]{1,0:T(8,128)(2,1)S(1)}, u32[]{:S(2)}, u32[]{:S(2)}) collective-permute-start(bf16[288,320]{1,0:T(8,128)(2,1)S(1)} %collective-permute-done.8.odd_ref), channel_id=1, source_target_pairs={{0,1},{1,0},{2,3},{3,2},{4,5},{5,4},{6,7},{7,6},{8,9},{9,8},{10,11... | collective-permute-start | bytes 552968 | tf_op jit(solution)/shard_map/ppermute | solution.py:37
  13.9 1.5 %collective-permute-start.9 = (bf16[288,320]{1,0:T(8,128)(2,1)S(1)}, bf16[288,320]{1,0:T(8,128)(2,1)S(1)}, u32[]{:S(2)}, u32[]{:S(2)}) collective-permute-start(bf16[288,320]{1,0:T(8,128)(2,1)S(1)} %collective-permute-done.7.even_ref), channel_id=1, source_target_pairs={{0,1},{1,0},{2,3},{3,2},{4,5},{5,4},{6,7},{7,6},{8,9},{9,8},{10,11... | collective-permute-start | bytes 552968 | tf_op jit(solution)/shard_map/ppermute | solution.py:37
  13.9 2.9 %collective-permute-start.6 = (bf16[54,640]{1,0:T(8,128)(2,1)S(1)}, bf16[54,640]{1,0:T(8,128)(2,1)S(1)}, u32[]{:S(2)}, u32[]{:S(2)}) collective-permute-start(bf16[54,640]{1,0:T(8,128)(2,1)S(1)} %shard_map.84.refs_2_), channel_id=1, source_target_pairs={{0,1},{1,0},{2,3},{3,2},{4,5},{5,4},{6,7},{7,6},{8,9},{9,8},{10,11... | collective-permute-start | bytes 207368 | tf_op jit(solution)/shard_map/ppermute | solution.py:37

commit v6 on v5

--- a/solution.py
+++ b/solution.py
@@ -117,7 +117,7 @@
 def gather_tokens(own, packed):
     frames, rows = lax.axis_size("frames"), lax.axis_size("rows")
     if frames == 4 and rows == 2:
-        far = [swap(packed, lambda f, r, c, d=d: (f ^ d, r ^ c, c)) for d in (3, 2, 1)]
+        far = [swap(packed, lambda f, r, c, d=d: (f ^ d, r ^ c, c)) for d in (2, 1, 3)]
         (rest,) = call(unpack_kernel, far, [((3 * own.shape[0], C), BF16)], flops=REST)
         return [own, swap_bit(own, "rows", 1)], [rest]
     parts = [own]

time: 19.3 us -> 19.3 us (level)
  starting transfers between devices: 11.9 us -> 11.7 us
    ppermute x5, waiting for transfers between devices: 0.78 us -> 0.52 us  [swap(): return lax.ppermute(x, ('frames', 'rows', 'heads'), perm)]
    ppermute x6, waiting for transfers between devices: 0.88 us -> 1.09 us  [sibling(): return lax.ppermute(x, 'heads', [(0, 1), (1, 0)])]
where the time goes in v6:
time: 19.3 us; the launch traced here: 18.9 us
  starting transfers between devices  11.7 us (61%)
  Pallas kernels  5.35 us (28%)
  waiting for transfers between devices  1.61 us (8%)
  between operations  0.21 us (1%)
    ppermute x5, starting transfers between devices, swap(): return lax.ppermute(x, ('frames', 'rows', 'heads'), perm)  8.96 us
    pallas_call x8, Pallas kernels, call(): pl.pallas_call(kernel, out_shape=[jax.ShapeDtypeStruct(shape, dtype) for...  5.35 us
    ppermute x1, starting transfers between devices, swap_bit(): lax.ppermute(x, axis, [(i, i ^ bit) for i in range(lax.axis_size(axis))])  1.54 us
    ppermute x6, starting transfers between devices, sibling(): return lax.ppermute(x, 'heads', [(0, 1), (1, 0)])  1.22 us
    ppermute x6, waiting for transfers between devices, sibling(): return lax.ppermute(x, 'heads', [(0, 1), (1, 0)])  1.09 us
    ppermute x5, waiting for transfers between devices, swap(): return lax.ppermute(x, ('frames', 'rows', 'heads'), perm)  0.52 us
  transfers between devices with their start and end apart: 12, of which 4 were waited for; matrix products, arithmetic and copies ran while one was open for 0% of the time, Pallas kernels for 16%

profile of v6, /device:TPU:0, one launch (start us, length us, event | category | flops | bytes accessed | tf_op | source)
XLA Modules:
  0.0 18.9 jit_solution(9961928585307113659)
XLA Ops:
  0.0 0.5 %collective-permute-start = (bf16[288,320]{1,0:T(8,128)(2,1)}, bf16[288,320]{1,0:T(8,128)(2,1)S(1)}, u32[]{:S(2)}, u32[]{:S(2)}) collective-permute-start(bf16[288,320]{1,0:T(8,128)(2,1)} %bitcast.8), channel_id=1, source_target_pairs={{0,1},{1,0},{2,3},{3,2},{4,5},{5,4},{6,7},{7,6},{8,9},{9,8},{10,11... | collective-permute-start | bytes 552968 | tf_op jit(solution)/shard_map/ppermute | solution.py:37
  0.5 0.1 collective-permute-start.1
  0.5 3.0 %collective-permute-start.7 = (bf16[288,320]{1,0:T(8,128)(2,1)}, bf16[288,320]{1,0:T(8,128)(2,1)S(1)}, u32[]{:S(2)}, u32[]{:S(2)}) collective-permute-start(bf16[288,320]{1,0:T(8,128)(2,1)} %bitcast.9), channel_id=1, source_target_pairs={{0,4},{1,5},{2,6},{3,7},{4,0},{5,1},{6,2},{7,3},{8,12},{9,13},{10,... | collective-permute-start | bytes 552968 | tf_op jit(solution)/shard_map/ppermute | solution.py:49
  3.5 1.5 %collective-permute-start.8 = (bf16[288,320]{1,0:T(8,128)(2,1)}, bf16[288,320]{1,0:T(8,128)(2,1)S(1)}, u32[]{:S(2)}, u32[]{:S(2)}) collective-permute-start(bf16[288,320]{1,0:T(8,128)(2,1)} %bitcast.10), channel_id=1, source_target_pairs={{0,2},{1,3},{2,0},{3,1},{4,8},{5,9},{6,10},{7,11},{8,4},{9,5},{10,... | collective-permute-start | bytes 552968 | tf_op jit(solution)/shard_map/ppermute | solution.py:49
  5.1 0.1 shard_map.83
  5.2 0.0 copy-start.1
  5.2 0.0 copy-start.4
  5.2 1.2 %collective-permute-start.3 = (bf16[90,128]{1,0:T(8,128)(2,1)S(1)}, bf16[90,128]{1,0:T(8,128)(2,1)S(1)}, u32[]{:S(2)}, u32[]{:S(2)}) collective-permute-start(bf16[90,128]{1,0:T(8,128)(2,1)S(1)} %get-tuple-element.19), channel_id=1, source_target_pairs={{0,8},{1,11},{2,10},{3,9},{4,12},{5,15},{6,14},{7,13},{8,0},{9,3},... | collective-permute-start | bytes 69128 | tf_op jit(solution)/shard_map/ppermute | solution.py:49
  6.4 1.9 %collective-permute-start.4 = (bf16[90,128]{1,0:T(8,128)(2,1)S(1)}, bf16[90,128]{1,0:T(8,128)(2,1)S(1)}, u32[]{:S(2)}, u32[]{:S(2)}) collective-permute-start(bf16[90,128]{1,0:T(8,128)(2,1)S(1)} %get-tuple-element.19), channel_id=1, source_target_pairs={{0,4},{1,7},{2,6},{3,5},{4,0},{5,3},{6,2},{7,1},{8,12},{9,15},{10,... | collective-permute-start | bytes 69128 | tf_op jit(solution)/shard_map/ppermute | solution.py:49
  8.3 1.3 %collective-permute-start.5 = (bf16[90,128]{1,0:T(8,128)(2,1)S(1)}, bf16[90,128]{1,0:T(8,128)(2,1)S(1)}, u32[]{:S(2)}, u32[]{:S(2)}) collective-permute-start(bf16[90,128]{1,0:T(8,128)(2,1)S(1)} %get-tuple-element.19), channel_id=1, source_target_pairs={{0,12},{1,15},{2,14},{3,13},{4,8},{5,11},{6,10},{7,9},{8,4},{9,7},... | collective-permute-start | bytes 69128 | tf_op jit(solution)/shard_map/ppermute | solution.py:49
  9.7 0.6 %shard_map.85.acc_ref = f32[288,640]{1,0:T(8,128)S(1)} custom-call(bf16[288,320]{1,0:T(8,128)(2,1)S(1)} %bitcast.11, bf16[288,320]{1,0:T(8,128)(2,1)S(1)} %collective-permute-done.other_ref, bf16[3,640,640]{2,1,0:T(8,128)(2,1)S(1)} %copy-done), custom_call_target="tpu_custom_call" | custom-call | flops 500000000 | tf_op jit(solution)/shard_map/pallas_call | solution.py:72
  10.3 0.3 %shard_map.87 = (bf16[1120,640]{1,0:T(8,128)(2,1)S(1)}, bf16[320,320]{1,0:T(8,128)(2,1)S(1)}) custom-call(bf16[320,640]{1,0:T(8,128)(2,1)S(1)} %bitcast.5, bf16[320,640]{1,0:T(8,128)(2,1)S(1)} %bitcast.6, bf16[320,640]{1,0:T(8,128)(2,1)S(1)} %bitcast.7, bf16[320,640]{1,0:T(8,128)(2,1)S(1)} %copy-done.4), custom_call_target="tpu_custom_call" | custom-call | flops 100000000 | tf_op jit(solution)/shard_map/pallas_call | solution.py:72
  10.6 0.1 collective-permute-start.11
  10.7 0.4 %collective-permute-done.8.odd_ref = bf16[288,320]{1,0:T(8,128)(2,1)S(1)} collective-permute-done((bf16[288,320]{1,0:T(8,128)(2,1)}, bf16[288,320]{1,0:T(8,128)(2,1)S(1)}, u32[]{:S(2)}, u32[]{:S(2)}) %collective-permute-start.8) | collective-permute-done | bytes 184352 | tf_op jit(solution)/shard_map/ppermute | solution.py:49
  11.1 1.5 %collective-permute-start.2 = (bf16[18,640]{1,0:T(8,128)(2,1)S(1)}, bf16[18,640]{1,0:T(8,128)(2,1)S(1)}, u32[]{:S(2)}, u32[]{:S(2)}) collective-permute-start(bf16[18,640]{1,0:T(8,128)(2,1)S(1)} %get-tuple-element.18.refs_0_), channel_id=1, source_target_pairs={{0,2},{2,0},{1,3},{3,1},{4,6},{6,4},{5,7},{7,5},{8,10},{10,8},{9,1... | collective-permute-start | bytes 69128 | tf_op jit(solution)/shard_map/ppermute | solution.py:65
  12.7 0.6 %shard_map.86.acc_ref = f32[288,640]{1,0:T(8,128)S(1)} custom-call(f32[288,640]{1,0:T(8,128)S(1)} %shard_map.85.acc_ref, bf16[288,320]{1,0:T(8,128)(2,1)S(1)} %collective-permute-done.7.even_ref, bf16[288,320]{1,0:T(8,128)(2,1)S(1)} %collective-permute-done.8.odd_ref, bf16[3,640,640]{2,1,0:T(8,128)(2,1)S(1)} %copy-done), custom_call_target="tpu_custom_call" | custom-call | flops 500000000 | tf_op jit(solution)/shard_map/pallas_call | solution.py:72
  13.3 0.1 collective-permute-start.10
  13.4 0.5 %collective-permute-start.9 = (bf16[288,320]{1,0:T(8,128)(2,1)S(1)}, bf16[288,320]{1,0:T(8,128)(2,1)S(1)}, u32[]{:S(2)}, u32[]{:S(2)}) collective-permute-start(bf16[288,320]{1,0:T(8,128)(2,1)S(1)} %collective-permute-done.7.even_ref), channel_id=1, source_target_pairs={{0,1},{1,0},{2,3},{3,2},{4,5},{5,4},{6,7},{7,6},{8,9},{9,8},{10,11... | collective-permute-start | bytes 552968 | tf_op jit(solution)/shard_map/ppermute | solution.py:37
  13.9 0.1 collective-permute-done.5.refs_2_
  14.0 0.1 collective-permute-start.6
  14.1 0.8 %collective-permute-done.10.odd_ref = bf16[288,320]{1,0:T(8,128)(2,1)S(1)} collective-permute-done((bf16[288,320]{1,0:T(8,128)(2,1)S(1)}, bf16[288,320]{1,0:T(8,128)(2,1)S(1)}, u32[]{:S(2)}, u32[]{:S(2)}) %collective-permute-start.10) | collective-permute-done | bytes 184352 | tf_op jit(solution)/shard_map/ppermute | solution.py:37
  14.8 0.3 %collective-permute-done.9.even_ref = bf16[288,320]{1,0:T(8,128)(2,1)S(1)} collective-permute-done((bf16[288,320]{1,0:T(8,128)(2,1)S(1)}, bf16[288,320]{1,0:T(8,128)(2,1)S(1)}, u32[]{:S(2)}, u32[]{:S(2)}) %collective-permute-start.9) | collective-permute-done | bytes 184352 | tf_op jit(solution)/shard_map/ppermute | solution.py:37
  15.1 1.4 %shard_map.88 = (bf16[288,320]{1,0:T(8,128)(2,1)S(1)}, bf16[640,288]{1,0:T(8,128)(2,1)S(1)}) custom-call(f32[288,640]{1,0:T(8,128)S(1)} %shard_map.86.acc_ref, bf16[288,320]{1,0:T(8,128)(2,1)S(1)} %collective-permute-done.9.even_ref, bf16[288,320]{1,0:T(8,128)(2,1)S(1)} %collective-permute-done.10.odd_ref, bf16[3,640,640]{2,1,0:T(8,128)(2,1)S(1)} %copy-done, ...), custom_call_target="tpu_custom_call" | custom-call | flops 1000000000 | tf_op jit(solution)/shard_map/pallas_call | solution.py:72
  16.6 2.3 %shard_map.89 = bf16[288,320]{1,0:T(8,128)(2,1)} custom-call(bf16[18,640]{1,0:T(8,128)(2,1)S(1)} %get-tuple-element.18.refs_0_, bf16[18,640]{1,0:T(8,128)(2,1)S(1)} %collective-permute-done.2.refs_1_, bf16[54,640]{1,0:T(8,128)(2,1)S(1)} %shard_map.84.refs_2_, bf16[54,640]{1,0:T(8,128)(2,1)S(1)} %collective-permute-done.6.refs_3_, ...), custom_call_target="tpu_custom_call" | custom-call | flops 2000000000 | tf_op jit(solution)/shard_map/pallas_call | solution.py:72
  (24 shorter events, 0.1 us)
Async XLA Ops:
  0.0 5.0 %copy-start.7 = (bf16[18,320]{1,0:T(8,128)(2,1)S(1)}, bf16[18,320]{1,0:T(8,128)(2,1)}, u32[]{:S(2)}) copy-start(bf16[18,320]{1,0:T(8,128)(2,1)} %own_ref.1) | copy-start | bytes 34564
  0.0 5.0 %collective-permute-start = (bf16[288,320]{1,0:T(8,128)(2,1)}, bf16[288,320]{1,0:T(8,128)(2,1)S(1)}, u32[]{:S(2)}, u32[]{:S(2)}) collective-permute-start(bf16[288,320]{1,0:T(8,128)(2,1)} %bitcast.8), channel_id=1, source_target_pairs={{0,1},{1,0},{2,3},{3,2},{4,5},{5,4},{6,7},{7,6},{8,9},{9,8},{10,11... | collective-permute-start | bytes 552968 | tf_op jit(solution)/shard_map/ppermute | solution.py:37
  0.5 4.6 %collective-permute-start.1 = (bf16[18,320]{1,0:T(8,128)(2,1)}, bf16[18,320]{1,0:T(8,128)(2,1)S(1)}, u32[]{:S(2)}, u32[]{:S(2)}) collective-permute-start(bf16[18,320]{1,0:T(8,128)(2,1)} %own_ref.1), channel_id=1, source_target_pairs={{0,1},{1,0},{2,3},{3,2},{4,5},{5,4},{6,7},{7,6},{8,9},{9,8},{10,11... | collective-permute-start | bytes 34568 | tf_op jit(solution)/shard_map/ppermute | solution.py:37
  0.5 10.1 %collective-permute-start.7 = (bf16[288,320]{1,0:T(8,128)(2,1)}, bf16[288,320]{1,0:T(8,128)(2,1)S(1)}, u32[]{:S(2)}, u32[]{:S(2)}) collective-permute-start(bf16[288,320]{1,0:T(8,128)(2,1)} %bitcast.9), channel_id=1, source_target_pairs={{0,4},{1,5},{2,6},{3,7},{4,0},{5,1},{6,2},{7,3},{8,12},{9,13},{10,... | collective-permute-start | bytes 552968 | tf_op jit(solution)/shard_map/ppermute | solution.py:49
  3.5 7.6 %collective-permute-start.8 = (bf16[288,320]{1,0:T(8,128)(2,1)}, bf16[288,320]{1,0:T(8,128)(2,1)S(1)}, u32[]{:S(2)}, u32[]{:S(2)}) collective-permute-start(bf16[288,320]{1,0:T(8,128)(2,1)} %bitcast.10), channel_id=1, source_target_pairs={{0,2},{1,3},{2,0},{3,1},{4,8},{5,9},{6,10},{7,11},{8,4},{9,5},{10,... | collective-permute-start | bytes 552968 | tf_op jit(solution)/shard_map/ppermute | solution.py:49
  5.1 4.6 %copy-start = (bf16[3,640,640]{2,1,0:T(8,128)(2,1)S(1)}, bf16[3,640,640]{2,1,0:T(8,128)(2,1)}, u32[]{:S(2)}) copy-start(bf16[3,640,640]{2,1,0:T(8,128)(2,1)} %w_ref.5) | copy-start | bytes 7372804
  5.1 4.6 %copy-start.5 = (bf16[1,6,48,320]{3,2,1,0:T(8,128)(2,1)S(1)}, bf16[1,6,48,320]{3,2,1,0:T(8,128)(2,1)}, u32[]{:S(2)}) copy-start(bf16[1,6,48,320]{3,2,1,0:T(8,128)(2,1)} %param.8) | copy-start | bytes 552964
  5.2 5.1 %copy-start.1 = (bf16[640,320]{0,1:T(8,128)(2,1)S(1)}, bf16[640,320]{0,1:T(8,128)(2,1)}, u32[]{:S(2)}) copy-start(bf16[640,320]{0,1:T(8,128)(2,1)} %param.11) | copy-start | bytes 1228804
  5.2 5.1 %copy-start.2 = (bf16[640,320]{0,1:T(8,128)(2,1)S(1)}, bf16[640,320]{0,1:T(8,128)(2,1)}, u32[]{:S(2)}) copy-start(bf16[640,320]{0,1:T(8,128)(2,1)} %param.12) | copy-start | bytes 1228804
  5.2 5.1 %copy-start.3 = (bf16[640,320]{0,1:T(8,128)(2,1)S(1)}, bf16[640,320]{0,1:T(8,128)(2,1)}, u32[]{:S(2)}) copy-start(bf16[640,320]{0,1:T(8,128)(2,1)} %param.13) | copy-start | bytes 1228804
  5.2 5.1 %copy-start.4 = (bf16[320,640]{1,0:T(8,128)(2,1)S(1)}, bf16[320,640]{1,0:T(8,128)(2,1)}, u32[]{:S(2)}) copy-start(bf16[320,640]{1,0:T(8,128)(2,1)} %wo_ref) | copy-start | bytes 1228804
  5.2 8.1 %collective-permute-start.3 = (bf16[90,128]{1,0:T(8,128)(2,1)S(1)}, bf16[90,128]{1,0:T(8,128)(2,1)S(1)}, u32[]{:S(2)}, u32[]{:S(2)}) collective-permute-start(bf16[90,128]{1,0:T(8,128)(2,1)S(1)} %get-tuple-element.19), channel_id=1, source_target_pairs={{0,8},{1,11},{2,10},{3,9},{4,12},{5,15},{6,14},{7,13},{8,0},{9,3},... | collective-permute-start | bytes 69128 | tf_op jit(solution)/shard_map/ppermute | solution.py:49
  6.4 7.0 %collective-permute-start.4 = (bf16[90,128]{1,0:T(8,128)(2,1)S(1)}, bf16[90,128]{1,0:T(8,128)(2,1)S(1)}, u32[]{:S(2)}, u32[]{:S(2)}) collective-permute-start(bf16[90,128]{1,0:T(8,128)(2,1)S(1)} %get-tuple-element.19), channel_id=1, source_target_pairs={{0,4},{1,7},{2,6},{3,5},{4,0},{5,3},{6,2},{7,1},{8,12},{9,15},{10,... | collective-permute-start | bytes 69128 | tf_op jit(solution)/shard_map/ppermute | solution.py:49
  8.3 5.6 %collective-permute-start.5 = (bf16[90,128]{1,0:T(8,128)(2,1)S(1)}, bf16[90,128]{1,0:T(8,128)(2,1)S(1)}, u32[]{:S(2)}, u32[]{:S(2)}) collective-permute-start(bf16[90,128]{1,0:T(8,128)(2,1)S(1)} %get-tuple-element.19), channel_id=1, source_target_pairs={{0,12},{1,15},{2,14},{3,13},{4,8},{5,11},{6,10},{7,9},{8,4},{9,7},... | collective-permute-start | bytes 69128 | tf_op jit(solution)/shard_map/ppermute | solution.py:49
  10.6 4.5 %collective-permute-start.11 = (bf16[1120,640]{1,0:T(8,128)(2,1)S(1)}, bf16[1120,640]{1,0:T(8,128)(2,1)S(1)}, u32[]{:S(2)}, u32[]{:S(2)}) collective-permute-start(bf16[1120,640]{1,0:T(8,128)(2,1)S(1)} %get-tuple-element.25.held_ref.refs_6_), channel_id=1, source_target_pairs={{0,1},{1,0},{2,3},{3,2},{4,5},{5,4},{6,7},{7,6},{8,9},{9,8},{10,11... | collective-permute-start | bytes 4300808 | tf_op jit(solution)/shard_map/ppermute | solution.py:37
  11.1 5.5 %collective-permute-start.2 = (bf16[18,640]{1,0:T(8,128)(2,1)S(1)}, bf16[18,640]{1,0:T(8,128)(2,1)S(1)}, u32[]{:S(2)}, u32[]{:S(2)}) collective-permute-start(bf16[18,640]{1,0:T(8,128)(2,1)S(1)} %get-tuple-element.18.refs_0_), channel_id=1, source_target_pairs={{0,2},{2,0},{1,3},{3,1},{4,6},{6,4},{5,7},{7,5},{8,10},{10,8},{9,1... | collective-permute-start | bytes 69128 | tf_op jit(solution)/shard_map/ppermute | solution.py:65
  13.3 1.9 %copy-start.6 = (f32[640]{0:T(1024)S(1)}, f32[640]{0:T(1024)}, u32[]{:S(2)}) copy-start(f32[640]{0:T(1024)} %gain_ref.1) | copy-start | bytes 7684
  13.3 1.5 %collective-permute-start.10 = (bf16[288,320]{1,0:T(8,128)(2,1)S(1)}, bf16[288,320]{1,0:T(8,128)(2,1)S(1)}, u32[]{:S(2)}, u32[]{:S(2)}) collective-permute-start(bf16[288,320]{1,0:T(8,128)(2,1)S(1)} %collective-permute-done.8.odd_ref), channel_id=1, source_target_pairs={{0,1},{1,0},{2,3},{3,2},{4,5},{5,4},{6,7},{7,6},{8,9},{9,8},{10,11... | collective-permute-start | bytes 552968 | tf_op jit(solution)/shard_map/ppermute | solution.py:37
  13.4 1.8 %collective-permute-start.9 = (bf16[288,320]{1,0:T(8,128)(2,1)S(1)}, bf16[288,320]{1,0:T(8,128)(2,1)S(1)}, u32[]{:S(2)}, u32[]{:S(2)}) collective-permute-start(bf16[288,320]{1,0:T(8,128)(2,1)S(1)} %collective-permute-done.7.even_ref), channel_id=1, source_target_pairs={{0,1},{1,0},{2,3},{3,2},{4,5},{5,4},{6,7},{7,6},{8,9},{9,8},{10,11... | collective-permute-start | bytes 552968 | tf_op jit(solution)/shard_map/ppermute | solution.py:37
  14.0 2.6 %collective-permute-start.6 = (bf16[54,640]{1,0:T(8,128)(2,1)S(1)}, bf16[54,640]{1,0:T(8,128)(2,1)S(1)}, u32[]{:S(2)}, u32[]{:S(2)}) collective-permute-start(bf16[54,640]{1,0:T(8,128)(2,1)S(1)} %shard_map.84.refs_2_), channel_id=1, source_target_pairs={{0,1},{1,0},{2,3},{3,2},{4,5},{5,4},{6,7},{7,6},{8,9},{9,8},{10,11... | collective-permute-start | bytes 207368 | tf_op jit(solution)/shard_map/ppermute | solution.py:37

commit v7 on v5

--- a/solution.py
+++ b/solution.py
@@ -163,11 +163,13 @@
     half = wo_ref.shape[0]
     for i, ref in enumerate((wq_ref, wk_ref, wv_ref)):
         held_ref[i * half : (i + 1) * half] = ref[...]
-    left, right = wo_ref[:, :half], wo_ref[:, half:]
-    out_ref[...] = jnp.where(core == 0, left, right)
-    sent = jnp.where(core == 0, right, left)
-    held_ref[3 * half :, :half] = sent[: half // 2]
-    held_ref[3 * half :, half:] = sent[half // 2 :]
+    for which in range(2):
+
+        @pl.when(core == which)
+        def _(keep=slice(which * half, (which + 1) * half), send=slice((1 - which) * half, (2 - which) * half)):
+            out_ref[...] = wo_ref[:, keep]
+            held_ref[3 * half :, :half] = wo_ref[: half // 2, send]
+            held_ref[3 * half :, half:] = wo_ref[half // 2 :, send]
 
 
 def first_kernel(frames, acc_ref, even_ref, odd_ref, w_ref, sum_ref):

time: 19.3 us -> 19.3 us (level)
  transfers between devices with their start and end apart: 12 -> 12, of which waited for: 4 -> 4; matrix products, arithmetic and copies ran while one was open for 0% -> 0% of each run, Pallas kernels for 16% -> 15%
where the time goes in v7:
time: 19.3 us; the launch traced here: 19.1 us
  starting transfers between devices  11.9 us (62%)
  Pallas kernels  5.24 us (27%)
  waiting for transfers between devices  1.77 us (9%)
    ppermute x5, starting transfers between devices, swap(): return lax.ppermute(x, ('frames', 'rows', 'heads'), perm)  8.96 us
    pallas_call x8, Pallas kernels, call(): pl.pallas_call(kernel, out_shape=[jax.ShapeDtypeStruct(shape, dtype) for...  5.24 us
    ppermute x1, starting transfers between devices, swap_bit(): lax.ppermute(x, axis, [(i, i ^ bit) for i in range(lax.axis_size(axis))])  1.68 us
    ppermute x6, starting transfers between devices, sibling(): return lax.ppermute(x, 'heads', [(0, 1), (1, 0)])  1.23 us
    ppermute x5, waiting for transfers between devices, swap(): return lax.ppermute(x, ('frames', 'rows', 'heads'), perm)  0.89 us
    ppermute x6, waiting for transfers between devices, sibling(): return lax.ppermute(x, 'heads', [(0, 1), (1, 0)])  0.88 us
  transfers between devices with their start and end apart: 12, of which 4 were waited for; matrix products, arithmetic and copies ran while one was open for 0% of the time, Pallas kernels for 15%

profile of v7, /device:TPU:0, one launch (start us, length us, event | category | flops | bytes accessed | tf_op | source)
XLA Modules:
  0.0 19.1 jit_solution(17509953914357950863)
XLA Ops:
  0.0 0.5 %collective-permute-start = (bf16[288,320]{1,0:T(8,128)(2,1)}, bf16[288,320]{1,0:T(8,128)(2,1)S(1)}, u32[]{:S(2)}, u32[]{:S(2)}) collective-permute-start(bf16[288,320]{1,0:T(8,128)(2,1)} %bitcast.8), channel_id=1, source_target_pairs={{0,1},{1,0},{2,3},{3,2},{4,5},{5,4},{6,7},{7,6},{8,9},{9,8},{10,11... | collective-permute-start | bytes 552968 | tf_op jit(solution)/shard_map/ppermute | solution.py:37
  0.5 0.1 collective-permute-start.1
  0.5 3.0 %collective-permute-start.7 = (bf16[288,320]{1,0:T(8,128)(2,1)}, bf16[288,320]{1,0:T(8,128)(2,1)S(1)}, u32[]{:S(2)}, u32[]{:S(2)}) collective-permute-start(bf16[288,320]{1,0:T(8,128)(2,1)} %bitcast.9), channel_id=1, source_target_pairs={{0,4},{1,5},{2,6},{3,7},{4,0},{5,1},{6,2},{7,3},{8,12},{9,13},{10,... | collective-permute-start | bytes 552968 | tf_op jit(solution)/shard_map/ppermute | solution.py:49
  3.5 1.5 %collective-permute-start.8 = (bf16[288,320]{1,0:T(8,128)(2,1)}, bf16[288,320]{1,0:T(8,128)(2,1)S(1)}, u32[]{:S(2)}, u32[]{:S(2)}) collective-permute-start(bf16[288,320]{1,0:T(8,128)(2,1)} %bitcast.10), channel_id=1, source_target_pairs={{0,2},{1,3},{2,0},{3,1},{4,8},{5,9},{6,10},{7,11},{8,4},{9,5},{10,... | collective-permute-start | bytes 552968 | tf_op jit(solution)/shard_map/ppermute | solution.py:49
  5.1 0.0 copy-start
  5.1 0.1 shard_map.83
  5.2 0.0 copy-start.1
  5.2 0.0 copy-start.2
  5.2 2.5 %collective-permute-start.3 = (bf16[90,128]{1,0:T(8,128)(2,1)S(1)}, bf16[90,128]{1,0:T(8,128)(2,1)S(1)}, u32[]{:S(2)}, u32[]{:S(2)}) collective-permute-start(bf16[90,128]{1,0:T(8,128)(2,1)S(1)} %get-tuple-element.19), channel_id=1, source_target_pairs={{0,12},{1,15},{2,14},{3,13},{4,8},{5,11},{6,10},{7,9},{8,4},{9,7},... | collective-permute-start | bytes 69128 | tf_op jit(solution)/shard_map/ppermute | solution.py:49
  7.8 0.6 %collective-permute-start.4 = (bf16[90,128]{1,0:T(8,128)(2,1)S(1)}, bf16[90,128]{1,0:T(8,128)(2,1)S(1)}, u32[]{:S(2)}, u32[]{:S(2)}) collective-permute-start(bf16[90,128]{1,0:T(8,128)(2,1)S(1)} %get-tuple-element.19), channel_id=1, source_target_pairs={{0,8},{1,11},{2,10},{3,9},{4,12},{5,15},{6,14},{7,13},{8,0},{9,3},... | collective-permute-start | bytes 69128 | tf_op jit(solution)/shard_map/ppermute | solution.py:49
  8.4 1.3 %collective-permute-start.5 = (bf16[90,128]{1,0:T(8,128)(2,1)S(1)}, bf16[90,128]{1,0:T(8,128)(2,1)S(1)}, u32[]{:S(2)}, u32[]{:S(2)}) collective-permute-start(bf16[90,128]{1,0:T(8,128)(2,1)S(1)} %get-tuple-element.19), channel_id=1, source_target_pairs={{0,4},{1,7},{2,6},{3,5},{4,0},{5,3},{6,2},{7,1},{8,12},{9,15},{10,... | collective-permute-start | bytes 69128 | tf_op jit(solution)/shard_map/ppermute | solution.py:49
  9.7 0.6 %shard_map.85.acc_ref = f32[288,640]{1,0:T(8,128)S(1)} custom-call(bf16[288,320]{1,0:T(8,128)(2,1)S(1)} %bitcast.11, bf16[288,320]{1,0:T(8,128)(2,1)S(1)} %collective-permute-done.other_ref, bf16[3,640,640]{2,1,0:T(8,128)(2,1)S(1)} %copy-done), custom_call_target="tpu_custom_call" | custom-call | flops 500000000 | tf_op jit(solution)/shard_map/pallas_call | solution.py:72
  10.3 0.2 %shard_map.87 = (bf16[1120,640]{1,0:T(8,128)(2,1)S(1)}, bf16[320,320]{1,0:T(8,128)(2,1)S(1)}) custom-call(bf16[320,640]{1,0:T(8,128)(2,1)S(1)} %bitcast.5, bf16[320,640]{1,0:T(8,128)(2,1)S(1)} %bitcast.6, bf16[320,640]{1,0:T(8,128)(2,1)S(1)} %bitcast.7, bf16[320,640]{1,0:T(8,128)(2,1)S(1)} %copy-done.4), custom_call_target="tpu_custom_call" | custom-call | flops 100000000 | tf_op jit(solution)/shard_map/pallas_call | solution.py:72
  10.5 0.1 collective-permute-start.11
  10.6 0.3 %collective-permute-done.8.odd_ref = bf16[288,320]{1,0:T(8,128)(2,1)S(1)} collective-permute-done((bf16[288,320]{1,0:T(8,128)(2,1)}, bf16[288,320]{1,0:T(8,128)(2,1)S(1)}, u32[]{:S(2)}, u32[]{:S(2)}) %collective-permute-start.8) | collective-permute-done | bytes 184352 | tf_op jit(solution)/shard_map/ppermute | solution.py:49
  10.9 1.7 %collective-permute-start.2 = (bf16[18,640]{1,0:T(8,128)(2,1)S(1)}, bf16[18,640]{1,0:T(8,128)(2,1)S(1)}, u32[]{:S(2)}, u32[]{:S(2)}) collective-permute-start(bf16[18,640]{1,0:T(8,128)(2,1)S(1)} %get-tuple-element.18.refs_0_), channel_id=1, source_target_pairs={{0,2},{2,0},{1,3},{3,1},{4,6},{6,4},{5,7},{7,5},{8,10},{10,8},{9,1... | collective-permute-start | bytes 69128 | tf_op jit(solution)/shard_map/ppermute | solution.py:65
  12.5 0.6 %shard_map.86.acc_ref = f32[288,640]{1,0:T(8,128)S(1)} custom-call(f32[288,640]{1,0:T(8,128)S(1)} %shard_map.85.acc_ref, bf16[288,320]{1,0:T(8,128)(2,1)S(1)} %collective-permute-done.7.even_ref, bf16[288,320]{1,0:T(8,128)(2,1)S(1)} %collective-permute-done.8.odd_ref, bf16[3,640,640]{2,1,0:T(8,128)(2,1)S(1)} %copy-done), custom_call_target="tpu_custom_call" | custom-call | flops 500000000 | tf_op jit(solution)/shard_map/pallas_call | solution.py:72
  13.2 0.1 collective-permute-start.10
  13.2 0.6 %collective-permute-done.4.refs_1_ = bf16[90,128]{1,0:T(8,128)(2,1)S(1)} collective-permute-done((bf16[90,128]{1,0:T(8,128)(2,1)S(1)}, bf16[90,128]{1,0:T(8,128)(2,1)S(1)}, u32[]{:S(2)}, u32[]{:S(2)}) %collective-permute-start.4) | collective-permute-done | bytes 23072 | tf_op jit(solution)/shard_map/ppermute | solution.py:49
  13.9 0.6 %collective-permute-start.6 = (bf16[54,640]{1,0:T(8,128)(2,1)S(1)}, bf16[54,640]{1,0:T(8,128)(2,1)S(1)}, u32[]{:S(2)}, u32[]{:S(2)}) collective-permute-start(bf16[54,640]{1,0:T(8,128)(2,1)S(1)} %shard_map.84.refs_2_), channel_id=1, source_target_pairs={{0,1},{1,0},{2,3},{3,2},{4,5},{5,4},{6,7},{7,6},{8,9},{9,8},{10,11... | collective-permute-start | bytes 207368 | tf_op jit(solution)/shard_map/ppermute | solution.py:37
  14.5 0.2 %collective-permute-done.10.odd_ref = bf16[288,320]{1,0:T(8,128)(2,1)S(1)} collective-permute-done((bf16[288,320]{1,0:T(8,128)(2,1)S(1)}, bf16[288,320]{1,0:T(8,128)(2,1)S(1)}, u32[]{:S(2)}, u32[]{:S(2)}) %collective-permute-start.10) | collective-permute-done | bytes 184352 | tf_op jit(solution)/shard_map/ppermute | solution.py:37
  14.7 0.6 %collective-permute-done.9.even_ref = bf16[288,320]{1,0:T(8,128)(2,1)S(1)} collective-permute-done((bf16[288,320]{1,0:T(8,128)(2,1)S(1)}, bf16[288,320]{1,0:T(8,128)(2,1)S(1)}, u32[]{:S(2)}, u32[]{:S(2)}) %collective-permute-start.9) | collective-permute-done | bytes 184352 | tf_op jit(solution)/shard_map/ppermute | solution.py:37
  15.3 1.4 %shard_map.88 = (bf16[288,320]{1,0:T(8,128)(2,1)S(1)}, bf16[640,288]{1,0:T(8,128)(2,1)S(1)}) custom-call(f32[288,640]{1,0:T(8,128)S(1)} %shard_map.86.acc_ref, bf16[288,320]{1,0:T(8,128)(2,1)S(1)} %collective-permute-done.9.even_ref, bf16[288,320]{1,0:T(8,128)(2,1)S(1)} %collective-permute-done.10.odd_ref, bf16[3,640,640]{2,1,0:T(8,128)(2,1)S(1)} %copy-done, ...), custom_call_target="tpu_custom_call" | custom-call | flops 1000000000 | tf_op jit(solution)/shard_map/pallas_call | solution.py:72
  16.8 2.3 %shard_map.89 = bf16[288,320]{1,0:T(8,128)(2,1)} custom-call(bf16[18,640]{1,0:T(8,128)(2,1)S(1)} %get-tuple-element.18.refs_0_, bf16[18,640]{1,0:T(8,128)(2,1)S(1)} %collective-permute-done.2.refs_1_, bf16[54,640]{1,0:T(8,128)(2,1)S(1)} %shard_map.84.refs_2_, bf16[54,640]{1,0:T(8,128)(2,1)S(1)} %collective-permute-done.6.refs_3_, ...), custom_call_target="tpu_custom_call" | custom-call | flops 2000000000 | tf_op jit(solution)/shard_map/pallas_call | solution.py:72
  (24 shorter events, 0.1 us)
Async XLA Ops:
  0.0 5.0 %copy-start.7 = (bf16[18,320]{1,0:T(8,128)(2,1)S(1)}, bf16[18,320]{1,0:T(8,128)(2,1)}, u32[]{:S(2)}) copy-start(bf16[18,320]{1,0:T(8,128)(2,1)} %own_ref.1) | copy-start | bytes 34564
  0.0 5.0 %collective-permute-start = (bf16[288,320]{1,0:T(8,128)(2,1)}, bf16[288,320]{1,0:T(8,128)(2,1)S(1)}, u32[]{:S(2)}, u32[]{:S(2)}) collective-permute-start(bf16[288,320]{1,0:T(8,128)(2,1)} %bitcast.8), channel_id=1, source_target_pairs={{0,1},{1,0},{2,3},{3,2},{4,5},{5,4},{6,7},{7,6},{8,9},{9,8},{10,11... | collective-permute-start | bytes 552968 | tf_op jit(solution)/shard_map/ppermute | solution.py:37
  0.5 4.6 %collective-permute-start.1 = (bf16[18,320]{1,0:T(8,128)(2,1)}, bf16[18,320]{1,0:T(8,128)(2,1)S(1)}, u32[]{:S(2)}, u32[]{:S(2)}) collective-permute-start(bf16[18,320]{1,0:T(8,128)(2,1)} %own_ref.1), channel_id=1, source_target_pairs={{0,1},{1,0},{2,3},{3,2},{4,5},{5,4},{6,7},{7,6},{8,9},{9,8},{10,11... | collective-permute-start | bytes 34568 | tf_op jit(solution)/shard_map/ppermute | solution.py:37
  0.5 10.0 %collective-permute-start.7 = (bf16[288,320]{1,0:T(8,128)(2,1)}, bf16[288,320]{1,0:T(8,128)(2,1)S(1)}, u32[]{:S(2)}, u32[]{:S(2)}) collective-permute-start(bf16[288,320]{1,0:T(8,128)(2,1)} %bitcast.9), channel_id=1, source_target_pairs={{0,4},{1,5},{2,6},{3,7},{4,0},{5,1},{6,2},{7,3},{8,12},{9,13},{10,... | collective-permute-start | bytes 552968 | tf_op jit(solution)/shard_map/ppermute | solution.py:49
  3.5 7.3 %collective-permute-start.8 = (bf16[288,320]{1,0:T(8,128)(2,1)}, bf16[288,320]{1,0:T(8,128)(2,1)S(1)}, u32[]{:S(2)}, u32[]{:S(2)}) collective-permute-start(bf16[288,320]{1,0:T(8,128)(2,1)} %bitcast.10), channel_id=1, source_target_pairs={{0,2},{1,3},{2,0},{3,1},{4,8},{5,9},{6,10},{7,11},{8,4},{9,5},{10,... | collective-permute-start | bytes 552968 | tf_op jit(solution)/shard_map/ppermute | solution.py:49
  5.1 4.6 %copy-start = (bf16[3,640,640]{2,1,0:T(8,128)(2,1)S(1)}, bf16[3,640,640]{2,1,0:T(8,128)(2,1)}, u32[]{:S(2)}) copy-start(bf16[3,640,640]{2,1,0:T(8,128)(2,1)} %w_ref.5) | copy-start | bytes 7372804
  5.1 4.6 %copy-start.5 = (bf16[1,6,48,320]{3,2,1,0:T(8,128)(2,1)S(1)}, bf16[1,6,48,320]{3,2,1,0:T(8,128)(2,1)}, u32[]{:S(2)}) copy-start(bf16[1,6,48,320]{3,2,1,0:T(8,128)(2,1)} %param.8) | copy-start | bytes 552964
  5.2 5.1 %copy-start.1 = (bf16[640,320]{0,1:T(8,128)(2,1)S(1)}, bf16[640,320]{0,1:T(8,128)(2,1)}, u32[]{:S(2)}) copy-start(bf16[640,320]{0,1:T(8,128)(2,1)} %param.11) | copy-start | bytes 1228804
  5.2 5.1 %copy-start.2 = (bf16[640,320]{0,1:T(8,128)(2,1)S(1)}, bf16[640,320]{0,1:T(8,128)(2,1)}, u32[]{:S(2)}) copy-start(bf16[640,320]{0,1:T(8,128)(2,1)} %param.12) | copy-start | bytes 1228804
  5.2 5.1 %copy-start.3 = (bf16[640,320]{0,1:T(8,128)(2,1)S(1)}, bf16[640,320]{0,1:T(8,128)(2,1)}, u32[]{:S(2)}) copy-start(bf16[640,320]{0,1:T(8,128)(2,1)} %param.13) | copy-start | bytes 1228804
  5.2 5.1 %copy-start.4 = (bf16[320,640]{1,0:T(8,128)(2,1)S(1)}, bf16[320,640]{1,0:T(8,128)(2,1)}, u32[]{:S(2)}) copy-start(bf16[320,640]{1,0:T(8,128)(2,1)} %wo_ref) | copy-start | bytes 1228804
  5.2 7.9 %collective-permute-start.3 = (bf16[90,128]{1,0:T(8,128)(2,1)S(1)}, bf16[90,128]{1,0:T(8,128)(2,1)S(1)}, u32[]{:S(2)}, u32[]{:S(2)}) collective-permute-start(bf16[90,128]{1,0:T(8,128)(2,1)S(1)} %get-tuple-element.19), channel_id=1, source_target_pairs={{0,12},{1,15},{2,14},{3,13},{4,8},{5,11},{6,10},{7,9},{8,4},{9,7},... | collective-permute-start | bytes 69128 | tf_op jit(solution)/shard_map/ppermute | solution.py:49
  7.8 6.1 %collective-permute-start.4 = (bf16[90,128]{1,0:T(8,128)(2,1)S(1)}, bf16[90,128]{1,0:T(8,128)(2,1)S(1)}, u32[]{:S(2)}, u32[]{:S(2)}) collective-permute-start(bf16[90,128]{1,0:T(8,128)(2,1)S(1)} %get-tuple-element.19), channel_id=1, source_target_pairs={{0,8},{1,11},{2,10},{3,9},{4,12},{5,15},{6,14},{7,13},{8,0},{9,3},... | collective-permute-start | bytes 69128 | tf_op jit(solution)/shard_map/ppermute | solution.py:49
  8.4 5.4 %collective-permute-start.5 = (bf16[90,128]{1,0:T(8,128)(2,1)S(1)}, bf16[90,128]{1,0:T(8,128)(2,1)S(1)}, u32[]{:S(2)}, u32[]{:S(2)}) collective-permute-start(bf16[90,128]{1,0:T(8,128)(2,1)S(1)} %get-tuple-element.19), channel_id=1, source_target_pairs={{0,4},{1,7},{2,6},{3,5},{4,0},{5,3},{6,2},{7,1},{8,12},{9,15},{10,... | collective-permute-start | bytes 69128 | tf_op jit(solution)/shard_map/ppermute | solution.py:49
  10.5 4.8 %collective-permute-start.11 = (bf16[1120,640]{1,0:T(8,128)(2,1)S(1)}, bf16[1120,640]{1,0:T(8,128)(2,1)S(1)}, u32[]{:S(2)}, u32[]{:S(2)}) collective-permute-start(bf16[1120,640]{1,0:T(8,128)(2,1)S(1)} %get-tuple-element.25.held_ref.refs_6_), channel_id=1, source_target_pairs={{0,1},{1,0},{2,3},{3,2},{4,5},{5,4},{6,7},{7,6},{8,9},{9,8},{10,11... | collective-permute-start | bytes 4300808 | tf_op jit(solution)/shard_map/ppermute | solution.py:37
  10.9 5.9 %collective-permute-start.2 = (bf16[18,640]{1,0:T(8,128)(2,1)S(1)}, bf16[18,640]{1,0:T(8,128)(2,1)S(1)}, u32[]{:S(2)}, u32[]{:S(2)}) collective-permute-start(bf16[18,640]{1,0:T(8,128)(2,1)S(1)} %get-tuple-element.18.refs_0_), channel_id=1, source_target_pairs={{0,2},{2,0},{1,3},{3,1},{4,6},{6,4},{5,7},{7,5},{8,10},{10,8},{9,1... | collective-permute-start | bytes 69128 | tf_op jit(solution)/shard_map/ppermute | solution.py:65
  13.1 2.2 %copy-start.6 = (f32[640]{0:T(1024)S(1)}, f32[640]{0:T(1024)}, u32[]{:S(2)}) copy-start(f32[640]{0:T(1024)} %gain_ref.1) | copy-start | bytes 7684
  13.2 1.5 %collective-permute-start.10 = (bf16[288,320]{1,0:T(8,128)(2,1)S(1)}, bf16[288,320]{1,0:T(8,128)(2,1)S(1)}, u32[]{:S(2)}, u32[]{:S(2)}) collective-permute-start(bf16[288,320]{1,0:T(8,128)(2,1)S(1)} %collective-permute-done.8.odd_ref), channel_id=1, source_target_pairs={{0,1},{1,0},{2,3},{3,2},{4,5},{5,4},{6,7},{7,6},{8,9},{9,8},{10,11... | collective-permute-start | bytes 552968 | tf_op jit(solution)/shard_map/ppermute | solution.py:37
  13.9 1.5 %collective-permute-start.9 = (bf16[288,320]{1,0:T(8,128)(2,1)S(1)}, bf16[288,320]{1,0:T(8,128)(2,1)S(1)}, u32[]{:S(2)}, u32[]{:S(2)}) collective-permute-start(bf16[288,320]{1,0:T(8,128)(2,1)S(1)} %collective-permute-done.7.even_ref), channel_id=1, source_target_pairs={{0,1},{1,0},{2,3},{3,2},{4,5},{5,4},{6,7},{7,6},{8,9},{9,8},{10,11... | collective-permute-start | bytes 552968 | tf_op jit(solution)/shard_map/ppermute | solution.py:37
  13.9 2.9 %collective-permute-start.6 = (bf16[54,640]{1,0:T(8,128)(2,1)S(1)}, bf16[54,640]{1,0:T(8,128)(2,1)S(1)}, u32[]{:S(2)}, u32[]{:S(2)}) collective-permute-start(bf16[54,640]{1,0:T(8,128)(2,1)S(1)} %shard_map.84.refs_2_), channel_id=1, source_target_pairs={{0,1},{1,0},{2,3},{3,2},{4,5},{5,4},{6,7},{7,6},{8,9},{9,8},{10,11... | collective-permute-start | bytes 207368 | tf_op jit(solution)/shard_map/ppermute | solution.py:37
